TPU v7x, 32 devices: a whole 2x2x4 slice. The times are simulated.
32 devices in a mesh: gx: 8 (over y, x, core), gy: 4 (over z).
Axes of the slice: x: 2, y: 2, z: 4, core: 2. Of those that a mesh axis runs over, the one named last changes fastest.
Arguments:
- fields: float32 [4, 128, 64, 128], P(None, 'gx', 'gy'), may hold values from -6 to 6
- factor_x: float32 [128, 32], P('gx'), may hold values from -0.75 to 0.75
- factor_y: float32 [64, 32], P('gy'), may hold values from -1 to 1
Outputs:
- advanced: float32 [4, 128, 64, 128], P(None, 'gx', 'gy')
- core_tensor: float32 [4, 32, 32, 128], P(None, 'gx', 'gy')
- rebuilt: float32 [4, 128, 64, 128], P(None, 'gx', 'gy')
All inputs are finite; a program needn't handle non-finite values.
Results may differ from a plain program's by a relative error of at most 0.000082.
Values sent between devices are 32-bit elements; how exact they have to be, the bound alone decides.
No kernel may reach another device: no remote copies, remote signals or barrier semaphores. Data moves between devices by JAX's collectives and lax.ppermute only.
A program may use at most 64 MiB of HBM per device.

v0:
```python
import math

import jax
import jax.numpy as jnp
from jax import lax
from jax.sharding import PartitionSpec as P

TIME_STEP = 0.2
REACT_RATE = 0.5
HEAT_RELEASE = 1.0


def extended(block, sides, width):
    for axis, dim in sides:
        count = lax.axis_size(axis)
        forward = [(i, i + 1) for i in range(count - 1)]
        forward.append((count - 1, 0))
        backward = [(target, source) for source, target in forward]
        low = lax.ppermute(
            lax.slice_in_dim(block, block.shape[dim] - width, None, axis=dim), axis, forward
        )
        high = lax.ppermute(lax.slice_in_dim(block, 0, width, axis=dim), axis, backward)
        block = jnp.concatenate([low, block, high], axis=dim)
    return block


def inner_part(array, margin):
    return array[:, margin : array.shape[1] - margin, margin : array.shape[2] - margin]


def tendency(padded):
    n_x = padded.shape[1]
    n_y = padded.shape[2]
    pressure = 0.5 * padded[3]
    flux_x = padded[0][None] * padded
    flux_x = flux_x.at[0].add(pressure)
    flux_y = padded[1][None] * padded
    flux_y = flux_y.at[1].add(pressure)

    def along_x(shift):
        return (
            flux_x[:, 3 + shift : n_x - 3 + shift, 3 : n_y - 3]
            - flux_x[:, 3 - shift : n_x - 3 - shift, 3 : n_y - 3]
        )

    def along_y(shift):
        return (
            flux_y[:, 3 : n_x - 3, 3 + shift : n_y - 3 + shift]
            - flux_y[:, 3 : n_x - 3, 3 - shift : n_y - 3 - shift]
        )

    deriv_x = (45.0 * along_x(1) - 9.0 * along_x(2) + along_x(3)) / 60.0
    deriv_y = (45.0 * along_y(1) - 9.0 * along_y(2) + along_y(3)) / 60.0
    center = inner_part(padded, 3)
    react = REACT_RATE * center[2] * (1.0 + jnp.tanh(center[3]))
    zeros = jnp.zeros_like(react)
    source = jnp.stack([zeros, zeros, -react, HEAT_RELEASE * react])
    return source - deriv_x - deriv_y


def section_tendency(state):
    padded = extended(state, (("gx", 1), ("gy", 2)), 3)
    return tendency(padded)


def per_device(fields, factor_x, factor_y):
    high = lax.Precision.HIGHEST
    section_one = fields + TIME_STEP * section_tendency(fields)
    section_two = 0.75 * fields + 0.25 * (section_one + TIME_STEP * section_tendency(section_one))
    advanced = 1.0 / 3.0 * fields + 2.0 / 3.0 * (
        section_two + TIME_STEP * section_tendency(section_two)
    )
    rank_full = factor_x.shape[1]
    count_x = lax.axis_size("gx")
    count_y = lax.axis_size("gy")
    partial_x = jnp.einsum("fxyz,xa->fayz", advanced, factor_x, precision=high)
    partial_value = lax.psum_scatter(partial_x, "gx", scatter_dimension=1, tiled=True)
    local_core = jnp.einsum("fayz,yb->fabz", partial_value, factor_y, precision=high)
    core_tensor = lax.psum_scatter(local_core, "gy", scatter_dimension=2, tiled=True)
    weights = factor_y
    columns = jnp.einsum(
        "fabz,yb->fayz",
        lax.all_gather(core_tensor, "gy", axis=2, tiled=True),
        weights,
        precision=high,
    )
    weights = factor_x
    expanded = jnp.einsum(
        "fayz,xa->fxyz", lax.all_gather(columns, "gx", axis=1, tiled=True), weights, precision=high
    )
    total_x = factor_x.shape[0] * count_x
    total_y = factor_y.shape[0] * count_y
    rescale = math.sqrt(float(total_x) * float(total_y)) / rank_full
    rebuilt = rescale * expanded
    return (advanced, core_tensor, rebuilt)


def solution(mesh):
    placed = (P(None, "gx", "gy", None), P("gx", None), P("gy", None))
    return jax.shard_map(
        per_device,
        mesh=mesh,
        in_specs=placed,
        out_specs=(P(None, "gx", "gy", None), P(None, "gx", "gy", None), P(None, "gx", "gy", None)),
        check_vma=False,
    )
```

profile of v0, /device:TPU:1, one launch (start us, length us, event | category | flops | bytes accessed | tf_op | source)
XLA Modules:
  0.0 191.4 jit_solution(17280242492883535550)
XLA Ops:
  7.2 1.0 fusion.75
  8.2 2.7 %collective-permute-start = (f32[4,3,16,128]{3,2,1,0:T(8,128)S(1)}, f32[4,3,16,128]{3,2,1,0:T(8,128)S(1)}, u32[]{:S(2)}, u32[]{:S(2)}) collective-permute-start(f32[4,3,16,128]{3,2,1,0:T(8,128)S(1)} %get-tuple-element.104), channel_id=1, source_target_pairs={{0,4},{4,8},{8,12},{12,16},{16,20},{20,24},{24,28},{28,0},{1,5},{5... | collective-permute-start | bytes 294920 | tf_op jit(solution)/shard_map/ppermute | solution.py:19
  10.9 1.6 collective-permute-done
  12.5 1.1 constant_dynamic-update-slice_fusion.1
  13.6 1.5 collective-permute-done.1
  15.2 1.3 collective-permute-start.2
  16.5 2.1 %collective-permute-start.3 = (f32[4,22,3,128]{3,2,1,0:T(4,128)S(1)}, f32[4,22,3,128]{3,2,1,0:T(4,128)S(1)}, u32[]{:S(2)}, u32[]{:S(2)}) collective-permute-start(f32[4,22,3,128]{3,2,1,0:T(4,128)S(1)} %get-tuple-element.98), channel_id=1, source_target_pairs={{1,0},{2,1},{3,2},{0,3},{5,4},{6,5},{7,6},{4,7},{9,8},{10,9},{11,1... | collective-permute-start | bytes 405512 | tf_op jit(solution)/shard_map/ppermute | solution.py:22
  18.7 4.2 %collective-permute-done.2 = f32[4,22,3,128]{3,2,1,0:T(4,128)S(1)} collective-permute-done((f32[4,22,3,128]{3,2,1,0:T(4,128)S(1)}, f32[4,22,3,128]{3,2,1,0:T(4,128)S(1)}, u32[]{:S(2)}, u32[]{:S(2)}) %collective-permute-start.2) | collective-permute-done | bytes 135200 | tf_op jit(solution)/shard_map/ppermute | solution.py:19
  22.9 3.4 %collective-permute-done.3 = f32[4,22,3,128]{3,2,1,0:T(4,128)S(1)} collective-permute-done((f32[4,22,3,128]{3,2,1,0:T(4,128)S(1)}, f32[4,22,3,128]{3,2,1,0:T(4,128)S(1)}, u32[]{:S(2)}, u32[]{:S(2)}) %collective-permute-start.3) | collective-permute-done | bytes 135200 | tf_op jit(solution)/shard_map/ppermute | solution.py:22
  27.7 2.7 %collective-permute-start.4 = (f32[4,3,16,128]{3,2,1,0:T(8,128)S(1)}, f32[4,3,16,128]{3,2,1,0:T(8,128)S(1)}, u32[]{:S(2)}, u32[]{:S(2)}) collective-permute-start(f32[4,3,16,128]{3,2,1,0:T(8,128)S(1)} %get-tuple-element.101), channel_id=1, source_target_pairs={{0,4},{4,8},{8,12},{12,16},{16,20},{20,24},{24,28},{28,0},{1,5},{5... | collective-permute-start | bytes 294920 | tf_op jit(solution)/shard_map/ppermute | solution.py:19
  30.4 1.6 collective-permute-done.4
  32.0 2.4 %collective-permute-done.5 = f32[4,3,16,128]{3,2,1,0:T(8,128)S(1)} collective-permute-done((f32[4,3,16,128]{3,2,1,0:T(8,128)S(1)}, f32[4,3,16,128]{3,2,1,0:T(8,128)S(1)}, u32[]{:S(2)}, u32[]{:S(2)}) %collective-permute-start.5) | collective-permute-done | bytes 98336 | tf_op jit(solution)/shard_map/ppermute | solution.py:22
  35.2 2.6 %collective-permute-start.7 = (f32[4,22,3,128]{3,2,1,0:T(4,128)S(1)}, f32[4,22,3,128]{3,2,1,0:T(4,128)S(1)}, u32[]{:S(2)}, u32[]{:S(2)}) collective-permute-start(f32[4,22,3,128]{3,2,1,0:T(4,128)S(1)} %get-tuple-element.96), channel_id=1, source_target_pairs={{1,0},{2,1},{3,2},{0,3},{5,4},{6,5},{7,6},{4,7},{9,8},{10,9},{11,1... | collective-permute-start | bytes 405512 | tf_op jit(solution)/shard_map/ppermute | solution.py:22
  37.8 4.9 %collective-permute-done.6 = f32[4,22,3,128]{3,2,1,0:T(4,128)S(1)} collective-permute-done((f32[4,22,3,128]{3,2,1,0:T(4,128)S(1)}, f32[4,22,3,128]{3,2,1,0:T(4,128)S(1)}, u32[]{:S(2)}, u32[]{:S(2)}) %collective-permute-start.6) | collective-permute-done | bytes 135200 | tf_op jit(solution)/shard_map/ppermute | solution.py:19
  42.7 2.7 %collective-permute-done.7 = f32[4,22,3,128]{3,2,1,0:T(4,128)S(1)} collective-permute-done((f32[4,22,3,128]{3,2,1,0:T(4,128)S(1)}, f32[4,22,3,128]{3,2,1,0:T(4,128)S(1)}, u32[]{:S(2)}, u32[]{:S(2)}) %collective-permute-start.7) | collective-permute-done | bytes 135200 | tf_op jit(solution)/shard_map/ppermute | solution.py:22
  46.1 0.7 fusion.24
  47.7 1.5 collective-permute-done.8
  49.2 3.5 %collective-permute-done.9 = f32[4,3,16,128]{3,2,1,0:T(8,128)S(1)} collective-permute-done((f32[4,3,16,128]{3,2,1,0:T(8,128)S(1)}, f32[4,3,16,128]{3,2,1,0:T(8,128)S(1)}, u32[]{:S(2)}, u32[]{:S(2)}) %collective-permute-start.9) | collective-permute-done | bytes 98336 | tf_op jit(solution)/shard_map/ppermute | solution.py:22
  52.8 3.3 %collective-permute-start.11 = (f32[4,22,3,128]{3,2,1,0:T(4,128)S(1)}, f32[4,22,3,128]{3,2,1,0:T(4,128)S(1)}, u32[]{:S(2)}, u32[]{:S(2)}) collective-permute-start(f32[4,22,3,128]{3,2,1,0:T(4,128)S(1)} %get-tuple-element.94), channel_id=1, source_target_pairs={{1,0},{2,1},{3,2},{0,3},{5,4},{6,5},{7,6},{4,7},{9,8},{10,9},{11,1... | collective-permute-start | bytes 405512 | tf_op jit(solution)/shard_map/ppermute | solution.py:22
  56.1 4.2 %collective-permute-done.10 = f32[4,22,3,128]{3,2,1,0:T(4,128)S(1)} collective-permute-done((f32[4,22,3,128]{3,2,1,0:T(4,128)S(1)}, f32[4,22,3,128]{3,2,1,0:T(4,128)S(1)}, u32[]{:S(2)}, u32[]{:S(2)}) %collective-permute-start.10) | collective-permute-done | bytes 135200 | tf_op jit(solution)/shard_map/ppermute | solution.py:19
  60.3 1.8 collective-permute-done.11
  62.8 0.7 fusion.8
  63.6 1.1 fusion.48
  64.6 1.6 copy.23
  67.6 54.0 %all-reduce.3.cloned.1.call-done = f32[4,32,16,128]{3,2,1,0:T(8,128)} async-done(((f32[4,32,16,128]{3,2,1,0:T(8,128)}), f32[4,32,16,128]{3,2,1,0:T(8,128)}) %all-reduce.3.cloned.1.call-update) | async-done | bytes 1048592
  121.5 2.0 %convolution_bitcast_fusion = f32[4,4,32,128]{3,2,1,0:T(8,128)} fusion(f32[4,32,16,128]{3,2,1,0:T(8,128)} %all-reduce.3.cloned.1.call-done, u32[]{:T(128)S(6)} %multiply.7, f32[16,32]{1,0:T(8,128)S(1)} %copy-done.3), kind=kOutput, calls=%fused_computation.2 | convolution fusion | flops 12582912 | bytes 395268 | tf_op jit(solution)/shard_map/fayz,yb->fabz/dot_general | solution.py:78
  123.6 18.9 %reduce-scatter.5.cloned.1.call-done = f32[4,4,8,128]{3,2,1,0:T(8,128)} async-done(((f32[4,4,32,128]{3,2,1,0:T(8,128)}), f32[4,4,8,128]{3,2,1,0:T(8,128)}) %reduce-scatter.5.cloned.1.call-update) | async-done | bytes 65552 | tf_op jit(solution)/shard_map/reduce_scatter | solution.py:79
  142.6 11.3 %all_gather.6 = f32[4,4,32,128]{3,2,1,0:T(8,128)S(1)} all-gather(f32[4,4,8,128]{3,2,1,0:T(8,128)} %reduce-scatter.5.cloned.1.call-done), channel_id=1, replica_groups=mesh['gx'=8,'gy'=4] {'gy'}, dimensions={2}, use_global_device_ids=true | all-gather | bytes 327680 | tf_op jit(solution)/shard_map/all_gather | solution.py:83
  153.9 0.9 convolution_bitcast_fusion.1
  154.8 26.6 %all-gather.2.cloned.1.call-done = f32[4,32,16,128]{3,2,0,1:T(8,128)} async-done(((f32[4,4,16,128]{3,2,0,1:T(8,128)}), f32[4,32,16,128]{3,2,0,1:T(8,128)}) %all-gather.2.cloned.1.call-update) | async-done | bytes 1048592 | tf_op jit(solution)/shard_map/all_gather | solution.py:89
  181.5 2.4 %fusion = f32[4,16,16,128]{3,1,2,0:T(8,128)S(1)} fusion(f32[4,32,16,128]{3,2,0,1:T(8,128)} %all-gather.2.cloned.1.call-done, f32[16,32]{1,0:T(8,128)S(1)} %copy-done), kind=kOutput, calls=%fused_computation.1 | convolution fusion | flops 50462720 | bytes 1574912 | tf_op jit(solution)/shard_map/fayz,xa->fxyz/dot_general | solution.py:88
  183.9 1.0 copy.8
  (54 shorter events, 5.5 us)
Async XLA Ops:
  7.2 56.4 %copy-start = (f32[16,32]{1,0:T(8,128)S(1)}, f32[16,32]{1,0:T(8,128)}, u32[]{:S(2)}) copy-start(f32[16,32]{1,0:T(8,128)} %param.16) | copy-start | bytes 6148
  7.2 114.4 %all-reduce.3.cloned.1.call-start = ((), (), s32[]{:S(2)}) async-start(), calls=%async_computation.3 | async-start | bytes 2097152
  8.2 4.3 %collective-permute-start = (f32[4,3,16,128]{3,2,1,0:T(8,128)S(1)}, f32[4,3,16,128]{3,2,1,0:T(8,128)S(1)}, u32[]{:S(2)}, u32[]{:S(2)}) collective-permute-start(f32[4,3,16,128]{3,2,1,0:T(8,128)S(1)} %get-tuple-element.104), channel_id=1, source_target_pairs={{0,4},{4,8},{8,12},{12,16},{16,20},{20,24},{24,28},{28,0},{1,5},{5... | collective-permute-start | bytes 294920 | tf_op jit(solution)/shard_map/ppermute | solution.py:19
  10.8 4.3 %collective-permute-start.1 = (f32[4,3,16,128]{3,2,1,0:T(8,128)S(1)}, f32[4,3,16,128]{3,2,1,0:T(8,128)S(1)}, u32[]{:S(2)}, u32[]{:S(2)}) collective-permute-start(f32[4,3,16,128]{3,2,1,0:T(8,128)S(1)} %get-tuple-element.103), channel_id=1, source_target_pairs={{4,0},{8,4},{12,8},{16,12},{20,16},{24,20},{28,24},{0,28},{5,1},{9... | collective-permute-start | bytes 294920 | tf_op jit(solution)/shard_map/ppermute | solution.py:22
  10.9 7.8 %copy-start.1 = (f32[4,16,16,128]{3,2,1,0:T(8,128)S(1)}, f32[4,16,16,128]{3,2,1,0:T(8,128)}, u32[]{:S(2)}) copy-start(f32[4,16,16,128]{3,2,1,0:T(8,128)} %param.15) | copy-start | bytes 1572868
  15.2 7.7 %collective-permute-start.2 = (f32[4,22,3,128]{3,2,1,0:T(4,128)S(1)}, f32[4,22,3,128]{3,2,1,0:T(4,128)S(1)}, u32[]{:S(2)}, u32[]{:S(2)}) collective-permute-start(f32[4,22,3,128]{3,2,1,0:T(4,128)S(1)} %get-tuple-element.97), channel_id=1, source_target_pairs={{0,1},{1,2},{2,3},{3,0},{4,5},{5,6},{6,7},{7,4},{8,9},{9,10},{10,1... | collective-permute-start | bytes 405512 | tf_op jit(solution)/shard_map/ppermute | solution.py:19
  16.5 9.7 %collective-permute-start.3 = (f32[4,22,3,128]{3,2,1,0:T(4,128)S(1)}, f32[4,22,3,128]{3,2,1,0:T(4,128)S(1)}, u32[]{:S(2)}, u32[]{:S(2)}) collective-permute-start(f32[4,22,3,128]{3,2,1,0:T(4,128)S(1)} %get-tuple-element.98), channel_id=1, source_target_pairs={{1,0},{2,1},{3,2},{0,3},{5,4},{6,5},{7,6},{4,7},{9,8},{10,9},{11,1... | collective-permute-start | bytes 405512 | tf_op jit(solution)/shard_map/ppermute | solution.py:22
  27.7 4.3 %collective-permute-start.4 = (f32[4,3,16,128]{3,2,1,0:T(8,128)S(1)}, f32[4,3,16,128]{3,2,1,0:T(8,128)S(1)}, u32[]{:S(2)}, u32[]{:S(2)}) collective-permute-start(f32[4,3,16,128]{3,2,1,0:T(8,128)S(1)} %get-tuple-element.101), channel_id=1, source_target_pairs={{0,4},{4,8},{8,12},{12,16},{16,20},{20,24},{24,28},{28,0},{1,5},{5... | collective-permute-start | bytes 294920 | tf_op jit(solution)/shard_map/ppermute | solution.py:19
  30.4 4.0 %collective-permute-start.5 = (f32[4,3,16,128]{3,2,1,0:T(8,128)S(1)}, f32[4,3,16,128]{3,2,1,0:T(8,128)S(1)}, u32[]{:S(2)}, u32[]{:S(2)}) collective-permute-start(f32[4,3,16,128]{3,2,1,0:T(8,128)S(1)} %get-tuple-element.102), channel_id=1, source_target_pairs={{4,0},{8,4},{12,8},{16,12},{20,16},{24,20},{28,24},{0,28},{5,1},{9... | collective-permute-start | bytes 294920 | tf_op jit(solution)/shard_map/ppermute | solution.py:22
  34.5 8.2 %collective-permute-start.6 = (f32[4,22,3,128]{3,2,1,0:T(4,128)S(1)}, f32[4,22,3,128]{3,2,1,0:T(4,128)S(1)}, u32[]{:S(2)}, u32[]{:S(2)}) collective-permute-start(f32[4,22,3,128]{3,2,1,0:T(4,128)S(1)} %get-tuple-element.95), channel_id=1, source_target_pairs={{0,1},{1,2},{2,3},{3,0},{4,5},{5,6},{6,7},{7,4},{8,9},{9,10},{10,1... | collective-permute-start | bytes 405512 | tf_op jit(solution)/shard_map/ppermute | solution.py:19
  35.2 10.2 %collective-permute-start.7 = (f32[4,22,3,128]{3,2,1,0:T(4,128)S(1)}, f32[4,22,3,128]{3,2,1,0:T(4,128)S(1)}, u32[]{:S(2)}, u32[]{:S(2)}) collective-permute-start(f32[4,22,3,128]{3,2,1,0:T(4,128)S(1)} %get-tuple-element.96), channel_id=1, source_target_pairs={{1,0},{2,1},{3,2},{0,3},{5,4},{6,5},{7,6},{4,7},{9,8},{10,9},{11,1... | collective-permute-start | bytes 405512 | tf_op jit(solution)/shard_map/ppermute | solution.py:22
  46.9 2.3 %collective-permute-start.8 = (f32[4,3,16,128]{3,2,1,0:T(8,128)S(1)}, f32[4,3,16,128]{3,2,1,0:T(8,128)S(1)}, u32[]{:S(2)}, u32[]{:S(2)}) collective-permute-start(f32[4,3,16,128]{3,2,1,0:T(8,128)S(1)} %get-tuple-element.99), channel_id=1, source_target_pairs={{0,4},{4,8},{8,12},{12,16},{16,20},{20,24},{24,28},{28,0},{1,5},{5... | collective-permute-start | bytes 294920 | tf_op jit(solution)/shard_map/ppermute | solution.py:19
  47.5 5.2 %collective-permute-start.9 = (f32[4,3,16,128]{3,2,1,0:T(8,128)S(1)}, f32[4,3,16,128]{3,2,1,0:T(8,128)S(1)}, u32[]{:S(2)}, u32[]{:S(2)}) collective-permute-start(f32[4,3,16,128]{3,2,1,0:T(8,128)S(1)} %get-tuple-element.100), channel_id=1, source_target_pairs={{4,0},{8,4},{12,8},{16,12},{20,16},{24,20},{28,24},{0,28},{5,1},{9... | collective-permute-start | bytes 294920 | tf_op jit(solution)/shard_map/ppermute | solution.py:22
  52.8 7.5 %collective-permute-start.10 = (f32[4,22,3,128]{3,2,1,0:T(4,128)S(1)}, f32[4,22,3,128]{3,2,1,0:T(4,128)S(1)}, u32[]{:S(2)}, u32[]{:S(2)}) collective-permute-start(f32[4,22,3,128]{3,2,1,0:T(4,128)S(1)} %get-tuple-element.93), channel_id=1, source_target_pairs={{0,1},{1,2},{2,3},{3,0},{4,5},{5,6},{6,7},{7,4},{8,9},{9,10},{10,1... | collective-permute-start | bytes 405512 | tf_op jit(solution)/shard_map/ppermute | solution.py:19
  52.8 9.2 %collective-permute-start.11 = (f32[4,22,3,128]{3,2,1,0:T(4,128)S(1)}, f32[4,22,3,128]{3,2,1,0:T(4,128)S(1)}, u32[]{:S(2)}, u32[]{:S(2)}) collective-permute-start(f32[4,22,3,128]{3,2,1,0:T(4,128)S(1)} %get-tuple-element.94), channel_id=1, source_target_pairs={{1,0},{2,1},{3,2},{0,3},{5,4},{6,5},{7,6},{4,7},{9,8},{10,9},{11,1... | collective-permute-start | bytes 405512 | tf_op jit(solution)/shard_map/ppermute | solution.py:22
  63.6 2.7 %copy-start.2 = (f32[4,16,16,128]{3,2,1,0:T(8,128)}, f32[4,16,16,128]{3,2,1,0:T(8,128)S(1)}, u32[]{:S(2)}) copy-start(f32[4,16,16,128]{3,2,1,0:T(8,128)S(1)} %fusion.8) | copy-start | bytes 1572868
  64.6 1.7 copy-start.4
  64.6 56.9 %copy-start.3 = (f32[16,32]{1,0:T(8,128)S(1)}, f32[16,32]{1,0:T(8,128)}, u32[]{:S(2)}) copy-start(f32[16,32]{1,0:T(8,128)} %param.17) | copy-start | bytes 6148
  66.3 76.3 %reduce-scatter.5.cloned.1.call-start = ((), (), s32[]{:S(2)}) async-start(), calls=%async_computation.1 | async-start | bytes 327680 | tf_op jit(solution)/shard_map/reduce_scatter | solution.py:79
  123.6 57.9 %all-gather.2.cloned.1.call-start = ((), (), s32[]{:S(2)}) async-start(), calls=%async_computation.2 | async-start | bytes 1179648 | tf_op jit(solution)/shard_map/all_gather | solution.py:89
Sparse Core Ops, SparseCore 0:
  66.4 55.1 all-reduce.2
  124.4 18.1 reduce-scatter.4
  155.0 26.4 all-gather.1
where the time goes:
time: 192 us; the launch traced here: 191 us
  waiting for transfers between devices  133 us (69%)
  starting transfers between devices  16.3 us (8%)
  between operations  14.7 us (8%)
  blocking collectives  11.3 us (6%)
  matrix products  6.43 us (3%)
  local copies, waits for them, and re-layouts  5.38 us (3%)
  other arithmetic  4.46 us (2%)
    unnamed x4, waiting for transfers between devices  54 us
    all_gather x1, waiting for transfers between devices, per_device(): lax.all_gather(columns, 'gx', axis=1, tiled=True)  26.6 us
    reduce_scatter x1, waiting for transfers between devices, per_device(): lax.psum_scatter(local_core, 'gy', scatter_dimension=2, tiled=True)  18.9 us
    ppermute x6, waiting for transfers between devices, extended(): lax.ppermute(lax.slice_in_dim(block, block.shape[dim] - width, None, axis...  18 us
    ppermute x6, waiting for transfers between devices, extended(): lax.ppermute(lax.slice_in_dim(block, 0, width, axis=dim), axis, backward)  15.3 us
    all_gather x1, blocking collectives, per_device(): lax.all_gather(core_tensor, 'gy', axis=2, tiled=True)  11.3 us
    ppermute x6, starting transfers between devices, extended(): lax.ppermute(lax.slice_in_dim(block, 0, width, axis=dim), axis, backward)  8.09 us
    ppermute x6, starting transfers between devices, extended(): lax.ppermute(lax.slice_in_dim(block, block.shape[dim] - width, None, axis...  8.07 us
  transfers between devices with their start and end apart: 15, of which 15 were waited for; matrix products, arithmetic and copies ran while one was open for 1% of the time, Pallas kernels for 0%

commit v1 on v0

--- a/solution.py
+++ b/solution.py
@@ -1,13 +1,325 @@
+import functools
 import math
 
 import jax
 import jax.numpy as jnp
 from jax import lax
+from jax.experimental import pallas as pl
+from jax.experimental.pallas import tpu as pltpu
 from jax.sharding import PartitionSpec as P
 
 TIME_STEP = 0.2
 REACT_RATE = 0.5
 HEAT_RELEASE = 1.0
+SUBLANES = 8
+LANES = 128
+
+
+def fits(mesh, fields, factor_x, factor_y):
+    n_f, n_x, n_y, n_z = fields.shape
+    count_x, count_y = mesh.shape["gx"], mesh.shape["gy"]
+    devices = count_x * count_y
+    rank = factor_x.shape[1]
+    if n_x % count_x or n_y % count_y or n_z % devices:
+        return False
+    block_x, block_y, block_z = n_x // count_x, n_y // count_y, n_z // devices
+    return (
+        n_x == LANES
+        and n_z == LANES
+        and block_x * SUBLANES == LANES
+        and block_x == 2 * SUBLANES
+        and block_y == 2 * SUBLANES
+        and 2 * block_z == SUBLANES
+        and count_x == SUBLANES
+        and factor_y.shape[1] == rank
+        and 4 * rank == LANES
+        and rank == count_y * SUBLANES
+        and rank % count_x == 0
+        and 2 * (rank // count_x) * n_f * block_z == LANES
+    )
+
+
+def exchange(blocks, stride):
+    blocks = list(blocks)
+    lane = lax.broadcasted_iota(jnp.int32, (SUBLANES, LANES), 1)
+    step = 1
+    while step < len(blocks):
+        width = stride * step
+        upper = (lane & width) != 0
+        for i in range(len(blocks)):
+            if i & step:
+                continue
+            low, high = blocks[i], blocks[i + step]
+            blocks[i] = jnp.where(upper, pltpu.roll(high, width, 1), low)
+            blocks[i + step] = jnp.where(upper, high, pltpu.roll(low, LANES - width, 1))
+        step *= 2
+    return blocks
+
+
+def pack_kernel(block_x, block_y, fields_ref, factor_x_ref, factor_y_ref, out_ref):
+    n_f = fields_ref.shape[0]
+    tiles = LANES // SUBLANES
+    sub = lax.broadcasted_iota(jnp.int32, (tiles, SUBLANES, LANES), 1)
+    lower = sub < SUBLANES // 2
+    half = SUBLANES // 2
+    for f in range(n_f):
+        turned = []
+        for octet in range(2):
+            rows = [
+                fields_ref[f, pl.ds(octet * SUBLANES + y, block_x, stride=block_y), :]
+                for y in range(SUBLANES)
+            ]
+            matrix = jnp.concatenate(rows, axis=0)
+            turned.append(matrix.T.reshape(tiles, SUBLANES, LANES))
+        first, second = turned
+        at = pl.ds(f * SUBLANES, SUBLANES)
+        out_ref[:, 0, at, :] = jnp.where(lower, first, pltpu.roll(second, half, 1))
+        out_ref[:, 1, at, :] = jnp.where(lower, pltpu.roll(first, half, 1), second)
+    factors = jnp.concatenate(
+        [
+            factor_x_ref[0:SUBLANES, :],
+            factor_x_ref[SUBLANES:, :],
+            factor_y_ref[0:SUBLANES, :],
+            factor_y_ref[SUBLANES:, :],
+        ],
+        axis=1,
+    )
+    out_ref[:, :, n_f * SUBLANES :, :] = jnp.broadcast_to(
+        factors[None, None], (tiles, 2, SUBLANES, LANES)
+    )
+
+
+def split(value):
+    high = value.astype(jnp.bfloat16)
+    low = (value - high.astype(jnp.float32)).astype(jnp.bfloat16)
+    return high, low
+
+
+def mul(a, b):
+    return jnp.dot(a, b, preferred_element_type=jnp.float32)
+
+
+def mul_split(a, b):
+    return mul(a[0], b[0]) + (mul(a[0], b[1]) + mul(a[1], b[0]))
+
+
+def main_kernel(n_f, count_x, count_y, rank, rescale, in_ref, out_ref, ext_a, ext_b, ext_c, adv):
+    half = SUBLANES // 2
+    margin = 3
+    inner = pl.ds(margin, SUBLANES)
+    lower = lax.broadcasted_iota(jnp.int32, (margin, SUBLANES, LANES), 1) < half
+
+    def fill_margins(ext):
+        for f in range(n_f):
+            head = [pltpu.roll(ext[f, s, margin : 2 * margin], half, 1) for s in range(count_y)]
+            tail = [pltpu.roll(ext[f, s, SUBLANES : SUBLANES + margin], half, 1) for s in range(count_y)]
+            for s in range(count_y):
+                ext[f, s, 0:margin] = jnp.where(lower, tail[s - 1], tail[s])
+                ext[f, s, SUBLANES + margin :] = jnp.where(lower, head[s], head[(s + 1) % count_y])
+
+    def section(ext, store):
+        def one(s, carry):
+            padded = [ext[f, s] for f in range(n_f)]
+            center = [p[margin : margin + SUBLANES] for p in padded]
+            react = REACT_RATE * center[2] * (1.0 + jnp.tanh(center[3]))
+            for f in range(n_f):
+                flux_y = padded[1] * padded[f]
+                if f == 1:
+                    flux_y = flux_y + 0.5 * padded[3]
+                flux_x = center[0] * center[f]
+                if f == 0:
+                    flux_x = flux_x + 0.5 * center[3]
+
+                def along_y(k):
+                    ahead = flux_y[margin + k : margin + k + SUBLANES]
+                    return ahead - flux_y[margin - k : margin - k + SUBLANES]
+
+                def along_x(k):
+                    return pltpu.roll(flux_x, LANES - k, 2) - pltpu.roll(flux_x, k, 2)
+
+                change = (
+                    45.0 * (along_x(1) + along_y(1))
+                    - 9.0 * (along_x(2) + along_y(2))
+                    + (along_x(3) + along_y(3))
+                ) * (-1.0 / 60.0)
+                if f == 2:
+                    change = change - react
+                if f == 3:
+                    change = change + HEAT_RELEASE * react
+                store(f, s, center[f], change)
+            return carry
+
+        lax.fori_loop(0, count_y, one, 0)
+
+    for s in range(count_y):
+        for f in range(n_f):
+            got = [in_ref[i, s, f * SUBLANES : (f + 1) * SUBLANES, :] for i in range(count_x)]
+            for y, block in enumerate(exchange(got, LANES // SUBLANES)):
+                ext_a[f, s, margin + y] = block
+    fill_margins(ext_a)
+
+    def first(f, s, center, change):
+        ext_b[f, s, inner] = center + TIME_STEP * change
+
+    def second(f, s, center, change):
+        ext_c[f, s, inner] = 0.75 * ext_a[f, s, inner] + 0.25 * (center + TIME_STEP * change)
+
+    def third(f, s, center, change):
+        adv[f, s] = (1.0 / 3.0) * ext_a[f, s, inner] + (2.0 / 3.0) * (center + TIME_STEP * change)
+
+    section(ext_a, first)
+    fill_margins(ext_b)
+    section(ext_b, second)
+    fill_margins(ext_c)
+    section(ext_c, third)
+
+    at = pl.ds(n_f * SUBLANES, SUBLANES)
+    group = n_f * half
+    wide = rank * group
+    held_x = split(jnp.concatenate([in_ref[i, 0, at, :] for i in range(count_x)], axis=0))
+    row = lax.broadcasted_iota(jnp.int32, (LANES, wide), 0)
+    col = lax.broadcasted_iota(jnp.int32, (LANES, wide), 1)
+
+    def spread(part):
+        pieces = []
+        for octet in range(2):
+            picks = (row - octet * rank == col // group).astype(jnp.bfloat16)
+            pieces.append(mul(part, picks).reshape(count_x, 1, SUBLANES, wide))
+        return jnp.concatenate(pieces, axis=1).reshape(LANES, wide)
+
+    spread_x = [spread(part) for part in held_x]
+    turned_x = [part.T for part in spread_x]
+    plane = count_y * SUBLANES * SUBLANES
+    total = None
+    lane_f = (lax.broadcasted_iota(jnp.int32, (LANES, wide), 1) // half) % n_f
+    for f in range(n_f):
+        weights = [jnp.where(lane_f == f, part, 0.0).astype(jnp.bfloat16) for part in spread_x]
+        term = mul_split(split(adv[f].reshape(plane, LANES)), weights)
+        total = term if total is None else total + term
+    row_z = lax.broadcasted_iota(jnp.int32, (plane, wide), 0) % half
+    col_z = lax.broadcasted_iota(jnp.int32, (plane, wide), 1) % half
+    same_z = row_z == col_z
+    partial = split(jnp.where(same_z, total, 0.0))
+
+    held_y = split(jnp.concatenate([in_ref[0, s, at, :] for s in range(count_y)], axis=0))
+    rows_y = count_y * SUBLANES
+    picks = lax.broadcasted_iota(jnp.int32, (plane, rows_y), 0) // SUBLANES
+    picks = (picks == lax.broadcasted_iota(jnp.int32, (plane, rows_y), 1)).astype(jnp.bfloat16)
+    row_octet = (lax.broadcasted_iota(jnp.int32, (plane, LANES), 0) // half) % 2
+    col_octet = lax.broadcasted_iota(jnp.int32, (plane, LANES), 1) // rank - 2
+    spread_y = [jnp.where(row_octet == col_octet, mul(picks, part), 0.0) for part in held_y]
+    weights_y = [part.astype(jnp.bfloat16) for part in spread_y]
+    turned_y = [part.T.astype(jnp.bfloat16) for part in spread_y]
+    halves = mul_split(turned_y, partial)
+    core = halves[2 * rank : 3 * rank] + halves[3 * rank :]
+
+    for s in range(count_y):
+        for i in range(count_x):
+            place = i * (LANES // 2)
+            block = core[s * SUBLANES : (s + 1) * SUBLANES, place // LANES * LANES : place // LANES * LANES + LANES]
+            if place % LANES:
+                block = pltpu.roll(block, LANES // 2, 1)
+            out_ref[i, s, 2 * n_f * SUBLANES :, :] = block
+
+    doubled = jnp.concatenate([jnp.zeros((2 * rank, wide), jnp.float32), core, core], axis=0)
+    columns = mul_split(weights_y, split(doubled))
+    columns = split(jnp.where(same_z, rescale * columns, 0.0))
+    row_f = (lax.broadcasted_iota(jnp.int32, (wide, LANES), 0) // half) % n_f
+
+    def send(block, f, s, first_row):
+        parts = exchange([block[y] for y in range(SUBLANES)], LANES // SUBLANES)
+        for i in range(count_x):
+            out_ref[i, s, first_row + f * SUBLANES : first_row + (f + 1) * SUBLANES, :] = parts[i]
+
+    for f in range(n_f):
+        weights = [jnp.where(row_f == f, part, 0.0).astype(jnp.bfloat16) for part in turned_x]
+        rebuilt = mul_split(columns, weights).reshape(count_y, SUBLANES, SUBLANES, LANES)
+        for s in range(count_y):
+            send(adv[f, s], f, s, 0)
+            send(rebuilt[s], f, s, n_f * SUBLANES)
+
+
+def unpack_kernel(n_f, block_x, block_y, in_ref, advanced_ref, core_ref, rebuilt_ref):
+    half = SUBLANES // 2
+    tiles = LANES // SUBLANES
+    lower = lax.broadcasted_iota(jnp.int32, (tiles, SUBLANES, LANES), 1) < half
+    for target, first_row in ((advanced_ref, 0), (rebuilt_ref, n_f * SUBLANES)):
+        for f in range(n_f):
+            at = pl.ds(first_row + f * SUBLANES, SUBLANES)
+            even, odd = in_ref[:, 0, at, :], in_ref[:, 1, at, :]
+            first = jnp.where(lower, even, pltpu.roll(odd, half, 1))
+            second = jnp.where(lower, pltpu.roll(even, half, 1), odd)
+            for octet, part in enumerate((first, second)):
+                turned = part.reshape(LANES, LANES).T
+                for y in range(SUBLANES):
+                    rows = pl.ds(octet * SUBLANES + y, block_x, stride=block_y)
+                    target[f, rows, :] = turned[y * block_x : (y + 1) * block_x]
+    at = pl.ds(2 * n_f * SUBLANES, SUBLANES)
+    count = 2 * tiles
+    lane = lax.broadcasted_iota(jnp.int32, (SUBLANES, LANES), 1)
+    upper = lane >= LANES // 2
+    got = [in_ref[d // 2, d % 2, at, :] for d in range(count)]
+    kept = [
+        jnp.where(upper, pltpu.roll(got[d + tiles], LANES // 2, 1), got[d]) for d in range(tiles)
+    ]
+    for place, block in enumerate(exchange(kept, half)):
+        core_ref[place % n_f, place // n_f] = block
+
+
+def z_plan(fields, factor_x, factor_y):
+    n_f, block_x, block_y, n_z = fields.shape
+    rank = factor_x.shape[1]
+    count_x = lax.axis_size("gx")
+    count_y = lax.axis_size("gy")
+    devices = count_x * count_y
+    pairs = devices // 2
+    rows_in = (n_f + 1) * SUBLANES
+    rows_out = (2 * n_f + 1) * SUBLANES
+    rescale = math.sqrt(float(block_x * count_x) * float(block_y * count_y)) / rank
+    params = pltpu.CompilerParams(vmem_limit_bytes=48 * 1024 * 1024)
+    vmem = pl.BlockSpec(memory_space=pltpu.VMEM)
+    f32 = jnp.float32
+
+    packed = pl.pallas_call(
+        functools.partial(pack_kernel, block_x, block_y),
+        out_shape=jax.ShapeDtypeStruct((pairs, 2, rows_in, n_z), f32),
+        in_specs=[vmem] * 3,
+        out_specs=vmem,
+        compiler_params=params,
+        name="pack",
+    )(fields.reshape(n_f, block_x * block_y, n_z), factor_x, factor_y)
+    planes = lax.all_to_all(
+        packed.reshape(devices, rows_in, n_z), ("gx", "gy"), 0, 0, tiled=True
+    )
+    extended = pltpu.VMEM((n_f, count_y, SUBLANES + 6, SUBLANES, LANES), f32)
+    results = pl.pallas_call(
+        functools.partial(main_kernel, n_f, count_x, count_y, rank, rescale),
+        out_shape=jax.ShapeDtypeStruct((count_x, count_y, rows_out, n_z), f32),
+        in_specs=[vmem],
+        out_specs=vmem,
+        scratch_shapes=[
+            extended,
+            extended,
+            extended,
+            pltpu.VMEM((n_f, count_y, SUBLANES, SUBLANES, LANES), f32),
+        ],
+        compiler_params=params,
+        name="sections",
+    )(planes.reshape(count_x, count_y, rows_in, n_z))
+    back = lax.all_to_all(
+        results.reshape(devices, rows_out, n_z), ("gx", "gy"), 0, 0, tiled=True
+    )
+    flat = jax.ShapeDtypeStruct((n_f, block_x * block_y, n_z), f32)
+    core = jax.ShapeDtypeStruct((n_f, rank // count_x, rank // count_y, n_z), f32)
+    advanced, core_tensor, rebuilt = pl.pallas_call(
+        functools.partial(unpack_kernel, n_f, block_x, block_y),
+        out_shape=(flat, core, flat),
+        in_specs=[vmem],
+        out_specs=(vmem, vmem, vmem),
+        compiler_params=params,
+        name="unpack",
+    )(back.reshape(pairs, 2, rows_out, n_z))
+    return advanced.reshape(fields.shape), core_tensor, rebuilt.reshape(fields.shape)
 
 
 def extended(block, sides, width):
@@ -97,10 +409,12 @@
 
 def solution(mesh):
     placed = (P(None, "gx", "gy", None), P("gx", None), P("gy", None))
-    return jax.shard_map(
-        per_device,
-        mesh=mesh,
-        in_specs=placed,
-        out_specs=(P(None, "gx", "gy", None), P(None, "gx", "gy", None), P(None, "gx", "gy", None)),
-        check_vma=False,
-    )
+    out = P(None, "gx", "gy", None)
+
+    def whole(fields, factor_x, factor_y):
+        plan = z_plan if fits(mesh, fields, factor_x, factor_y) else per_device
+        return jax.shard_map(
+            plan, mesh=mesh, in_specs=placed, out_specs=(out, out, out), check_vma=False
+        )(fields, factor_x, factor_y)
+
+    return whole

time: 192 us -> 72.9 us (0.38)
  waiting for transfers between devices: 133 us -> 0 us
  blocking collectives: 11.3 us -> 58.2 us
  starting transfers between devices: 16.3 us -> 0 us
  between operations: 14.7 us -> 0.65 us
  Pallas kernels: 0 us -> 11.3 us
  matrix products: 6.43 us -> 0 us
  other arithmetic: 4.46 us -> 0 us
  local copies, waits for them, and re-layouts: 5.38 us -> 2.43 us
    all_to_all x0 -> x2, blocking collectives: none -> 58.2 us  [the longest x1 33.2 us: z_plan(): lax.all_to_all(results.reshape(devices, rows_out, n_z), ('gx', 'gy'), 0,...]
    unnamed x4 -> x0, waiting for transfers between devices: 54 us -> none
    ppermute x12 -> x0, waiting for transfers between devices: 33.3 us -> none  [the longest x6 18 us: extended(): lax.ppermute(lax.slice_in_dim(block, block.shape[dim] - width, None, axis...]
    all_gather x1 -> x0, waiting for transfers between devices: 26.6 us -> none  [per_device(): lax.all_gather(columns, 'gx', axis=1, tiled=True)]
    reduce_scatter x1 -> x0, waiting for transfers between devices: 18.9 us -> none  [per_device(): lax.psum_scatter(local_core, 'gy', scatter_dimension=2, tiled=True)]
    ppermute x12 -> x0, starting transfers between devices: 16.2 us -> none  [the longest x6 8.09 us: extended(): lax.ppermute(lax.slice_in_dim(block, 0, width, axis=dim), axis, backward)]
    all_gather x1 -> x0, blocking collectives: 11.3 us -> none  [per_device(): lax.all_gather(core_tensor, 'gy', axis=2, tiled=True)]
    pallas_call x0 -> x3, Pallas kernels: none -> 11.3 us  [the longest x1 9.46 us: z_plan(): pl.pallas_call(functools.partial(main_kernel, n_f, count_x, count_y, rank...]
  transfers between devices with their start and end apart: 15 -> 0, of which waited for: 15 -> 0; matrix products, arithmetic and copies ran while one was open for 1% -> 0% of each run, Pallas kernels for 0% -> 0%
where the time goes in v1:
time: 72.9 us; the launch traced here: 72.5 us
  blocking collectives  58.2 us (80%)
  Pallas kernels  11.3 us (16%)
  local copies, waits for them, and re-layouts  2.43 us (3%)
    all_to_all x1, blocking collectives, z_plan(): lax.all_to_all(results.reshape(devices, rows_out, n_z), ('gx', 'gy'), 0,...  33.2 us
    all_to_all x1, blocking collectives, z_plan(): lax.all_to_all(packed.reshape(devices, rows_in, n_z), ('gx', 'gy'), 0, 0,...  25 us
    pallas_call x1, Pallas kernels, z_plan(): pl.pallas_call(functools.partial(main_kernel, n_f, count_x, count_y, rank...  9.46 us
    unnamed x6, local copies, waits for them, and re-layouts  2.43 us
    pallas_call x1, Pallas kernels, z_plan(): pl.pallas_call(functools.partial(unpack_kernel, n_f, block_x, block_y), o...  1.59 us

profile of v1, /device:TPU:1, one launch (start us, length us, event | category | flops | bytes accessed | tf_op | source)
XLA Modules:
  0.0 72.5 jit_solution(15246430467684844238)
XLA Ops:
  0.6 0.0 copy-start
  0.6 1.0 %copy-done = f32[4,16,16,128]{3,2,1,0:T(8,128)S(1)} copy-done((f32[4,16,16,128]{3,2,1,0:T(8,128)S(1)}, f32[4,16,16,128]{3,2,1,0:T(8,128)}, u32[]{:S(2)}) %copy-start) | copy-done | bytes 524312
  1.7 0.0 copy-start.1
  1.7 0.7 copy-done.1
  2.4 0.0 copy-start.2
  2.4 0.7 copy-done.2
  3.1 0.2 pack.1
  3.3 25.0 %all_to_all.10 = f32[32,40,128]{2,1,0:T(8,128)S(1)} all-to-all(f32[32,40,128]{2,1,0:T(8,128)S(1)} %bitcast.10), channel_id=1, replica_groups=mesh['gx'=8,'gy'=4] {'gx','gy'}, dimensions={0} | all-to-all | bytes 1310720 | tf_op jit(solution)/shard_map/all_to_all | solution.py:291
  28.3 9.5 %sections.1 = f32[8,4,72,128]{3,2,1,0:T(8,128)S(1)} custom-call(f32[8,4,40,128]{3,2,1,0:T(8,128)S(1)} %bitcast.9), custom_call_target="tpu_custom_call" | custom-call | tf_op jit(solution)/shard_map/sections/pallas_call | solution.py:295
  37.7 33.2 %all_to_all.11 = f32[32,72,128]{2,1,0:T(8,128)S(1)} all-to-all(f32[32,72,128]{2,1,0:T(8,128)S(1)} %bitcast.8), channel_id=1, replica_groups=mesh['gx'=8,'gy'=4] {'gx','gy'}, dimensions={0} | all-to-all | bytes 2359296 | tf_op jit(solution)/shard_map/all_to_all | solution.py:309
  70.9 1.6 %unpack.1 = (f32[4,256,128]{2,1,0:T(8,128)}, f32[4,4,8,128]{3,2,1,0:T(8,128)}, f32[4,256,128]{2,1,0:T(8,128)}) custom-call(f32[16,2,72,128]{3,2,1,0:T(8,128)S(1)} %bitcast.7), custom_call_target="tpu_custom_call" | custom-call | tf_op jit(solution)/shard_map/unpack/pallas_call | solution.py:314
Async XLA Ops:
  0.6 1.0 %copy-start = (f32[4,16,16,128]{3,2,1,0:T(8,128)S(1)}, f32[4,16,16,128]{3,2,1,0:T(8,128)}, u32[]{:S(2)}) copy-start(f32[4,16,16,128]{3,2,1,0:T(8,128)} %param.3) | copy-start | bytes 1572868
  1.7 0.7 copy-start.1
  2.4 0.7 copy-start.2

commit v2 on v0

--- a/solution.py
+++ b/solution.py
@@ -1,13 +1,348 @@
+import functools
 import math
 
 import jax
 import jax.numpy as jnp
 from jax import lax
+from jax.experimental import pallas as pl
+from jax.experimental.pallas import tpu as pltpu
 from jax.sharding import PartitionSpec as P
 
 TIME_STEP = 0.2
 REACT_RATE = 0.5
 HEAT_RELEASE = 1.0
+SUBLANES = 8
+LANES = 128
+HALF = SUBLANES // 2
+
+
+def fits(mesh, fields, factor_x, factor_y):
+    n_f, n_x, n_y, n_z = fields.shape
+    count_x, count_y = mesh.shape["gx"], mesh.shape["gy"]
+    devices = count_x * count_y
+    rank = factor_x.shape[1]
+    if n_x % count_x or n_y % count_y or n_z % devices:
+        return False
+    block_x, block_y, block_z = n_x // count_x, n_y // count_y, n_z // devices
+    return (
+        n_x == LANES
+        and n_z == LANES
+        and n_f == HALF
+        and block_z == HALF
+        and block_x == 2 * SUBLANES
+        and block_y == 2 * SUBLANES
+        and count_x == SUBLANES
+        and count_y == HALF
+        and rank == count_y * SUBLANES
+        and factor_y.shape[1] == rank
+        and n_f * rank == LANES
+    )
+
+
+def exchange(blocks, stride):
+    blocks = list(blocks)
+    lane = lax.broadcasted_iota(jnp.int32, (SUBLANES, LANES), 1)
+    step = 1
+    while step < len(blocks):
+        width = stride * step
+        upper = (lane & width) != 0
+        for i in range(len(blocks)):
+            if i & step:
+                continue
+            low, high = blocks[i], blocks[i + step]
+            blocks[i] = jnp.where(upper, pltpu.roll(high, width, 1), low)
+            blocks[i + step] = jnp.where(upper, high, pltpu.roll(low, LANES - width, 1))
+        step *= 2
+    return blocks
+
+
+def pack_kernel(fields_hbm, factor_x_hbm, factor_y_hbm, out_ref, fields_ref, x_ref, y_ref, sems):
+    n_f, rows, _ = fields_ref.shape
+    block_x = x_ref.shape[0]
+    block_y = rows // block_x
+    tiles = LANES // SUBLANES
+    copies = [
+        pltpu.make_async_copy(fields_hbm.at[f], fields_ref.at[f], sems.at[f]) for f in range(n_f)
+    ]
+    copies.append(pltpu.make_async_copy(factor_x_hbm, x_ref, sems.at[n_f]))
+    copies.append(pltpu.make_async_copy(factor_y_hbm, y_ref, sems.at[n_f + 1]))
+    for copy in copies:
+        copy.start()
+    for f in range(n_f):
+        copies[f].wait()
+        for octet in range(2):
+            matrix = jnp.concatenate(
+                [
+                    fields_ref[f, pl.ds(octet * SUBLANES + y, block_x, stride=block_y), :]
+                    for y in range(SUBLANES)
+                ],
+                axis=0,
+            )
+            turned = matrix.T.reshape(tiles, SUBLANES, LANES)
+            out_ref[:, 0, 2 * f + octet] = turned[:, :HALF]
+            out_ref[:, 1, 2 * f + octet] = turned[:, HALF:]
+    copies[n_f].wait()
+    copies[n_f + 1].wait()
+    part_x = lax.axis_index("gy")
+    part_y = lax.rem(lax.axis_index("gx"), block_y // HALF)
+    own_x = x_ref[pl.ds(part_x * HALF, HALF), :]
+    own_y = y_ref[pl.ds(part_y * HALF, HALF), :]
+    factors = jnp.concatenate([own_x, own_y, own_y, own_y], axis=1)
+    out_ref[:, :, 2 * n_f] = jnp.broadcast_to(factors[None, None], (tiles, 2, HALF, LANES))
+
+
+def split(value):
+    high = value.astype(jnp.bfloat16)
+    low = (value - high.astype(jnp.float32)).astype(jnp.bfloat16)
+    return high, low
+
+
+def mul(a, b, dims=((1,), (0,))):
+    return lax.dot_general(a, b, (dims, ((), ())), preferred_element_type=jnp.float32)
+
+
+def mul_split(a, b, dims=((1,), (0,))):
+    return mul(a[0], b[0], dims) + (mul(a[0], b[1], dims) + mul(a[1], b[0], dims))
+
+
+def main_kernel(n_f, count_x, count_y, rank, rescale, in_ref, out_ref, ext_a, ext_b, ext_c, adv):
+    margin = 3
+    inner = pl.ds(margin, SUBLANES)
+    lower = lax.broadcasted_iota(jnp.int32, (margin, SUBLANES, LANES), 1) < HALF
+
+    def each(body):
+        def step(s, carry):
+            body(s)
+            return carry
+
+        lax.fori_loop(0, count_y, step, 0)
+
+    def fill_margins(ext):
+        def one(s):
+            before = lax.rem(s + count_y - 1, count_y)
+            after = lax.rem(s + 1, count_y)
+            for f in range(n_f):
+                old = ext[before, f, pl.ds(SUBLANES, margin)]
+                own = ext[s, f, pl.ds(SUBLANES, margin)]
+                ext[s, f, 0:margin] = pltpu.roll(jnp.where(lower, own, old), HALF, 1)
+                own = ext[s, f, pl.ds(margin, margin)]
+                new = ext[after, f, pl.ds(margin, margin)]
+                ext[s, f, pl.ds(SUBLANES + margin, margin)] = pltpu.roll(
+                    jnp.where(lower, new, own), HALF, 1
+                )
+
+        each(one)
+
+    row = lax.broadcasted_iota(jnp.int32, (LANES, LANES), 0)
+    col = lax.broadcasted_iota(jnp.int32, (LANES, LANES), 1)
+    ahead = (row - col) & (LANES - 1)
+    taps = jnp.zeros((LANES, LANES), jnp.float32)
+    for shift, weight in ((1, 45.0), (2, -9.0), (3, 1.0)):
+        taps = jnp.where(ahead == shift, weight, taps)
+        taps = jnp.where(ahead == LANES - shift, -weight, taps)
+    taps = taps.astype(jnp.bfloat16)
+    taps = jnp.concatenate([taps, taps], axis=0)
+
+    def section(ext, step, store):
+        def one(s):
+            padded = [ext[s, f] for f in range(n_f)]
+            center = [p[margin : margin + SUBLANES] for p in padded]
+            flux_x = [center[0] * c for c in center]
+            flux_x[0] = flux_x[0] + 0.5 * center[3]
+            flat = jnp.concatenate(flux_x, axis=0).reshape(n_f * SUBLANES * SUBLANES, LANES)
+            along_x = mul(jnp.concatenate(split(flat), axis=1), taps)
+            along_x = along_x.reshape(n_f, SUBLANES, SUBLANES, LANES)
+            react = (step * REACT_RATE) * center[2] * (1.0 + jnp.tanh(center[3]))
+            for f in range(n_f):
+                flux_y = padded[1] * padded[f]
+                if f == 1:
+                    flux_y = flux_y + 0.5 * padded[3]
+
+                def along_y(k):
+                    after = flux_y[margin + k : margin + k + SUBLANES]
+                    return after - flux_y[margin - k : margin - k + SUBLANES]
+
+                change = (
+                    (-45.0 * step / 60.0) * along_y(1)
+                    + (9.0 * step / 60.0) * along_y(2)
+                    + (-step / 60.0) * (along_y(3) + along_x[f])
+                )
+                if f == 2:
+                    change = change - react
+                if f == 3:
+                    change = change + HEAT_RELEASE * react
+                store(s, f, center[f], change)
+
+        each(one)
+
+    def arrive(s):
+        for f in range(n_f):
+            got = [
+                in_ref[i, s, 2 * f : 2 * f + 2].reshape(SUBLANES, LANES) for i in range(count_x)
+            ]
+            for y, block in enumerate(exchange(got, LANES // SUBLANES)):
+                ext_a[s, f, margin + y] = block
+
+    def send(block, s, f, base):
+        parts = exchange([block[y] for y in range(SUBLANES)], LANES // SUBLANES)
+        for i, part in enumerate(parts):
+            out_ref[i, s, base + 2 * f : base + 2 * f + 2] = part.reshape(2, HALF, LANES)
+
+    def first(s, f, center, change):
+        ext_b[s, f, inner] = center + change
+
+    def second(s, f, center, change):
+        ext_c[s, f, inner] = 0.75 * ext_a[s, f, inner] + (0.25 * center + change)
+
+    def third(s, f, center, change):
+        done = (1.0 / 3.0) * ext_a[s, f, inner] + ((2.0 / 3.0) * center + change)
+        adv[f, s] = done
+        send(done, s, f, 0)
+
+    each(arrive)
+    fill_margins(ext_a)
+    section(ext_a, TIME_STEP, first)
+    fill_margins(ext_b)
+    section(ext_b, 0.25 * TIME_STEP, second)
+    fill_margins(ext_c)
+    section(ext_c, 2.0 / 3.0 * TIME_STEP, third)
+
+    plane = count_y * SUBLANES * SUBLANES
+    held = in_ref[:, :, 2 * n_f].reshape(LANES, LANES)
+    held_x = split(held)
+    held_y = split(jnp.where(col < rank, pltpu.roll(held, LANES - rank, 1), held))
+    picks = (row == col // n_f).astype(jnp.bfloat16)
+    spread_x = [mul(part, picks) for part in held_x]
+    weights_x = [
+        jnp.concatenate(
+            [jnp.where(col % n_f == f, part, 0.0).astype(jnp.bfloat16) for f in range(n_f)], axis=0
+        )
+        for part in spread_x
+    ]
+    r = lax.broadcasted_iota(jnp.int32, (plane, LANES), 0)
+    c = lax.broadcasted_iota(jnp.int32, (plane, LANES), 1)
+    from_s, from_y = r // (SUBLANES * SUBLANES), (r // HALF) % 2 * SUBLANES + (r // SUBLANES) % SUBLANES
+    block_x = LANES // count_x
+    held_at = from_y // HALF * block_x + from_s * HALF + from_y % HALF
+    picks = (held_at == c).astype(jnp.bfloat16)
+    same_z = r % HALF == c // rank
+    weights_y = [jnp.where(same_z, mul(picks, part), 0.0).astype(jnp.bfloat16) for part in held_y]
+
+    def by_x(value):
+        return jnp.concatenate([value[f].reshape(plane, LANES) for f in range(n_f)], axis=1)
+
+    partial = mul_split(split(by_x(adv)), weights_x)
+    core = mul_split(weights_y, split(partial), ((0,), (0,)))
+    columns = split(rescale * mul_split(weights_y, split(core)))
+
+    left = lax.broadcasted_iota(jnp.int32, (SUBLANES, LANES), 1) < LANES // 2
+    for s in range(count_y):
+        tiles = [core[z * rank + s * SUBLANES : z * rank + (s + 1) * SUBLANES] for z in range(HALF)]
+        tiles = exchange(exchange(tiles, 1), LANES // SUBLANES)
+        for i in range(count_x):
+            tile = tiles[i % HALF]
+            turned = pltpu.roll(tile, LANES // 2, 1)
+            if i >= HALF:
+                tile, turned = turned, tile
+            out_ref[i, s, 4 * n_f] = jnp.where(left[:HALF], tile[:HALF], turned[HALF:])
+
+    for f in range(n_f):
+        weights = [part[f * LANES : (f + 1) * LANES] for part in weights_x]
+        adv[f] = mul_split(columns, weights, ((1,), (1,))).reshape(adv.shape[1:])
+
+    def depart(s):
+        for f in range(n_f):
+            send(adv[f, s], s, f, 2 * n_f)
+
+    each(depart)
+
+
+def unpack_kernel(block_x, block_y, in_ref, advanced_ref, core_ref, rebuilt_ref):
+    n_f = advanced_ref.shape[0]
+    tiles = LANES // SUBLANES
+    for target, base in ((advanced_ref, 0), (rebuilt_ref, 2 * n_f)):
+        for f in range(n_f):
+            for octet in range(2):
+                place = base + 2 * f + octet
+                matrix = jnp.concatenate([in_ref[:, 0, place], in_ref[:, 1, place]], axis=1)
+                turned = matrix.reshape(LANES, LANES).T
+                for y in range(SUBLANES):
+                    rows = pl.ds(octet * SUBLANES + y, block_x, stride=block_y)
+                    target[f, rows, :] = turned[y * block_x : (y + 1) * block_x]
+    upper = lax.broadcasted_iota(jnp.int32, (SUBLANES, LANES), 1) >= LANES // 2
+    got = []
+    for d in range(2 * tiles):
+        block = in_ref[d // 2, d % 2, 4 * n_f]
+        got.append(jnp.concatenate([block, pltpu.roll(block, LANES // 2, 1)], axis=0))
+    kept = [
+        jnp.where(upper, pltpu.roll(got[d + tiles], LANES // 2, 1), got[d]) for d in range(tiles)
+    ]
+    a_count = core_ref.shape[1]
+    for place, block in enumerate(exchange(kept, HALF)):
+        core_ref[place // a_count, place % a_count] = block
+
+
+def z_plan(fields, factor_x, factor_y):
+    n_f, block_x, block_y, n_z = fields.shape
+    rank = factor_x.shape[1]
+    count_x = lax.axis_size("gx")
+    count_y = lax.axis_size("gy")
+    devices = count_x * count_y
+    pairs = devices // 2
+    tiles_in = 2 * n_f + 1
+    tiles_out = 4 * n_f + 1
+    rescale = math.sqrt(float(block_x * count_x) * float(block_y * count_y)) / rank
+    params = pltpu.CompilerParams(vmem_limit_bytes=48 * 1024 * 1024)
+    vmem = pl.BlockSpec(memory_space=pltpu.VMEM)
+    hbm = pl.BlockSpec(memory_space=pl.ANY)
+    f32 = jnp.float32
+
+    packed = pl.pallas_call(
+        pack_kernel,
+        out_shape=jax.ShapeDtypeStruct((pairs, 2, tiles_in, HALF, n_z), f32),
+        in_specs=[hbm] * 3,
+        out_specs=vmem,
+        scratch_shapes=[
+            pltpu.VMEM((n_f, block_x * block_y, n_z), f32),
+            pltpu.VMEM(factor_x.shape, f32),
+            pltpu.VMEM(factor_y.shape, f32),
+            pltpu.SemaphoreType.DMA((n_f + 2,)),
+        ],
+        compiler_params=params,
+        name="pack",
+    )(fields.reshape(n_f, block_x * block_y, n_z), factor_x, factor_y)
+    planes = lax.all_to_all(
+        packed.reshape(devices, tiles_in, HALF, n_z), ("gx", "gy"), 0, 0, tiled=True
+    )
+    extended = pltpu.VMEM((count_y, n_f, SUBLANES + 6, SUBLANES, LANES), f32)
+    results = pl.pallas_call(
+        functools.partial(main_kernel, n_f, count_x, count_y, rank, rescale),
+        out_shape=jax.ShapeDtypeStruct((count_x, count_y, tiles_out, HALF, n_z), f32),
+        in_specs=[vmem],
+        out_specs=vmem,
+        scratch_shapes=[
+            extended,
+            extended,
+            extended,
+            pltpu.VMEM((n_f, count_y, SUBLANES, SUBLANES, LANES), f32),
+        ],
+        compiler_params=params,
+        name="sections",
+    )(planes.reshape(count_x, count_y, tiles_in, HALF, n_z))
+    back = lax.all_to_all(
+        results.reshape(devices, tiles_out, HALF, n_z), ("gx", "gy"), 0, 0, tiled=True
+    )
+    flat = jax.ShapeDtypeStruct((n_f, block_x * block_y, n_z), f32)
+    core = jax.ShapeDtypeStruct((n_f, rank // count_x, rank // count_y, n_z), f32)
+    advanced, core_tensor, rebuilt = pl.pallas_call(
+        functools.partial(unpack_kernel, block_x, block_y),
+        out_shape=(flat, core, flat),
+        in_specs=[vmem],
+        out_specs=(vmem, vmem, vmem),
+        compiler_params=params,
+        name="unpack",
+    )(back.reshape(pairs, 2, tiles_out, HALF, n_z))
+    return advanced.reshape(fields.shape), core_tensor, rebuilt.reshape(fields.shape)
 
 
 def extended(block, sides, width):
@@ -97,10 +432,12 @@
 
 def solution(mesh):
     placed = (P(None, "gx", "gy", None), P("gx", None), P("gy", None))
-    return jax.shard_map(
-        per_device,
-        mesh=mesh,
-        in_specs=placed,
-        out_specs=(P(None, "gx", "gy", None), P(None, "gx", "gy", None), P(None, "gx", "gy", None)),
-        check_vma=False,
-    )
+    out = P(None, "gx", "gy", None)
+
+    def whole(fields, factor_x, factor_y):
+        plan = z_plan if fits(mesh, fields, factor_x, factor_y) else per_device
+        return jax.shard_map(
+            plan, mesh=mesh, in_specs=placed, out_specs=(out, out, out), check_vma=False
+        )(fields, factor_x, factor_y)
+
+    return whole

time: 192 us -> 69 us (0.36)
  waiting for transfers between devices: 133 us -> 0 us
  blocking collectives: 11.3 us -> 55.6 us
  starting transfers between devices: 16.3 us -> 0 us
  between operations: 14.7 us -> 0.66 us
  Pallas kernels: 0 us -> 9.72 us
  matrix products: 6.43 us -> 0 us
  other arithmetic: 4.46 us -> 0 us
  local copies, waits for them, and re-layouts: 5.38 us -> 2.43 us
    all_to_all x0 -> x2, blocking collectives: none -> 55.6 us  [the longest x1 32 us: z_plan(): lax.all_to_all(results.reshape(devices, tiles_out, HALF, n_z), ('gx', 'gy...]
    unnamed x4 -> x0, waiting for transfers between devices: 54 us -> none
    ppermute x12 -> x0, waiting for transfers between devices: 33.3 us -> none  [the longest x6 18 us: extended(): lax.ppermute(lax.slice_in_dim(block, block.shape[dim] - width, None, axis...]
    all_gather x1 -> x0, waiting for transfers between devices: 26.6 us -> none  [per_device(): lax.all_gather(columns, 'gx', axis=1, tiled=True)]
    reduce_scatter x1 -> x0, waiting for transfers between devices: 18.9 us -> none  [per_device(): lax.psum_scatter(local_core, 'gy', scatter_dimension=2, tiled=True)]
    ppermute x12 -> x0, starting transfers between devices: 16.2 us -> none  [the longest x6 8.09 us: extended(): lax.ppermute(lax.slice_in_dim(block, 0, width, axis=dim), axis, backward)]
    all_gather x1 -> x0, blocking collectives: 11.3 us -> none  [per_device(): lax.all_gather(core_tensor, 'gy', axis=2, tiled=True)]
    pallas_call x0 -> x3, Pallas kernels: none -> 9.72 us  [the longest x1 6.78 us: z_plan(): pl.pallas_call(functools.partial(main_kernel, n_f, count_x, count_y, rank...]
  transfers between devices with their start and end apart: 15 -> 0, of which waited for: 15 -> 0; matrix products, arithmetic and copies ran while one was open for 1% -> 0% of each run, Pallas kernels for 0% -> 0%
where the time goes in v2:
time: 69 us; the launch traced here: 68.4 us
  blocking collectives  55.6 us (81%)
  Pallas kernels  9.72 us (14%)
  local copies, waits for them, and re-layouts  2.43 us (4%)
    all_to_all x1, blocking collectives, z_plan(): lax.all_to_all(results.reshape(devices, tiles_out, HALF, n_z), ('gx', 'gy...  32 us
    all_to_all x1, blocking collectives, z_plan(): lax.all_to_all(packed.reshape(devices, tiles_in, HALF, n_z), ('gx', 'gy')...  23.6 us
    pallas_call x1, Pallas kernels, z_plan(): pl.pallas_call(functools.partial(main_kernel, n_f, count_x, count_y, rank...  6.78 us
    unnamed x6, local copies, waits for them, and re-layouts  2.43 us
    pallas_call x1, Pallas kernels, z_plan(): pl.pallas_call(functools.partial(unpack_kernel, block_x, block_y), out_sh...  1.72 us

profile of v2, /device:TPU:1, one launch (start us, length us, event | category | flops | bytes accessed | tf_op | source)
XLA Modules:
  0.0 68.4 jit_solution(16851294502963449621)
XLA Ops:
  0.6 0.0 copy-start
  0.6 1.0 %copy-done = f32[4,16,16,128]{3,2,1,0:T(8,128)S(1)} copy-done((f32[4,16,16,128]{3,2,1,0:T(8,128)S(1)}, f32[4,16,16,128]{3,2,1,0:T(8,128)}, u32[]{:S(2)}) %copy-start) | copy-done | bytes 524312
  1.7 0.0 copy-start.1
  1.7 0.7 %copy-done.1 = f32[16,32]{1,0:T(8,128)S(1)} copy-done((f32[16,32]{1,0:T(8,128)S(1)}, f32[16,32]{1,0:T(8,128)}, u32[]{:S(2)}) %copy-start.1) | copy-done | bytes 2072
  2.4 0.0 copy-start.2
  2.4 0.7 %copy-done.2 = f32[16,32]{1,0:T(8,128)S(1)} copy-done((f32[16,32]{1,0:T(8,128)S(1)}, f32[16,32]{1,0:T(8,128)}, u32[]{:S(2)}) %copy-start.2) | copy-done | bytes 2072
  3.1 1.2 %pack.1 = f32[16,2,9,4,128]{4,3,2,1,0:T(4,128)S(1)} custom-call(f32[4,256,128]{2,1,0:T(8,128)S(1)} %bitcast.11, f32[16,32]{1,0:T(8,128)S(1)} %copy-done.1, f32[16,32]{1,0:T(8,128)S(1)} %copy-done.2), custom_call_target="tpu_custom_call" | custom-call | tf_op jit(solution)/shard_map/pack/pallas_call | solution.py:300
  4.3 23.6 %all_to_all.10 = f32[32,9,4,128]{3,2,1,0:T(4,128)S(1)} all-to-all(f32[32,9,4,128]{3,2,1,0:T(4,128)S(1)} %bitcast.10), channel_id=1, replica_groups=mesh['gx'=8,'gy'=4] {'gx','gy'}, dimensions={0} | all-to-all | bytes 1179648 | tf_op jit(solution)/shard_map/all_to_all | solution.py:314
  27.9 6.8 %sections.1 = f32[8,4,17,4,128]{4,3,2,1,0:T(4,128)S(1)} custom-call(f32[8,4,9,4,128]{4,3,2,1,0:T(4,128)S(1)} %bitcast.9), custom_call_target="tpu_custom_call" | custom-call | tf_op jit(solution)/shard_map/sections/pallas_call | solution.py:318
  34.7 32.0 %all_to_all.11 = f32[32,17,4,128]{3,2,1,0:T(4,128)S(1)} all-to-all(f32[32,17,4,128]{3,2,1,0:T(4,128)S(1)} %bitcast.8), channel_id=1, replica_groups=mesh['gx'=8,'gy'=4] {'gx','gy'}, dimensions={0} | all-to-all | bytes 2228224 | tf_op jit(solution)/shard_map/all_to_all | solution.py:332
  66.7 1.7 %unpack.1 = (f32[4,256,128]{2,1,0:T(8,128)}, f32[4,4,8,128]{3,2,1,0:T(8,128)}, f32[4,256,128]{2,1,0:T(8,128)}) custom-call(f32[16,2,17,4,128]{4,3,2,1,0:T(4,128)S(1)} %bitcast.7), custom_call_target="tpu_custom_call" | custom-call | tf_op jit(solution)/shard_map/unpack/pallas_call | solution.py:337
Async XLA Ops:
  0.6 1.0 %copy-start = (f32[4,16,16,128]{3,2,1,0:T(8,128)S(1)}, f32[4,16,16,128]{3,2,1,0:T(8,128)}, u32[]{:S(2)}) copy-start(f32[4,16,16,128]{3,2,1,0:T(8,128)} %param.3) | copy-start | bytes 1572868
  1.7 0.7 %copy-start.1 = (f32[16,32]{1,0:T(8,128)S(1)}, f32[16,32]{1,0:T(8,128)}, u32[]{:S(2)}) copy-start(f32[16,32]{1,0:T(8,128)} %factor_x_hbm.1) | copy-start | bytes 6148
  2.4 0.7 %copy-start.2 = (f32[16,32]{1,0:T(8,128)S(1)}, f32[16,32]{1,0:T(8,128)}, u32[]{:S(2)}) copy-start(f32[16,32]{1,0:T(8,128)} %factor_y_hbm.1) | copy-start | bytes 6148

commit v3 on v2

--- a/solution.py
+++ b/solution.py
@@ -40,18 +40,30 @@
 
 
 def exchange(blocks, stride):
+    count = len(blocks)
+    period = stride * count
+    group = lax.broadcasted_iota(jnp.int32, (SUBLANES, LANES), 1) // stride % count
+    if period == LANES:
+        blocks = [pltpu.roll(b, i * stride, 1) if i else b for i, b in enumerate(blocks)]
+        step = 1
+        while step < count:
+            taken = (group & step) != 0
+            blocks = [
+                jnp.where(taken, blocks[(i + step) % count], blocks[i]) for i in range(count)
+            ]
+            step *= 2
+        blocks = [blocks[-j % count] for j in range(count)]
+        return [pltpu.roll(b, LANES - j * stride, 1) if j else b for j, b in enumerate(blocks)]
     blocks = list(blocks)
-    lane = lax.broadcasted_iota(jnp.int32, (SUBLANES, LANES), 1)
     step = 1
-    while step < len(blocks):
-        width = stride * step
-        upper = (lane & width) != 0
-        for i in range(len(blocks)):
+    while step < count:
+        upper = (group & step) != 0
+        for i in range(count):
             if i & step:
                 continue
             low, high = blocks[i], blocks[i + step]
-            blocks[i] = jnp.where(upper, pltpu.roll(high, width, 1), low)
-            blocks[i + step] = jnp.where(upper, high, pltpu.roll(low, LANES - width, 1))
+            blocks[i] = jnp.where(upper, pltpu.roll(high, stride * step, 1), low)
+            blocks[i + step] = jnp.where(upper, high, pltpu.roll(low, LANES - stride * step, 1))
         step *= 2
     return blocks
 
@@ -115,7 +127,7 @@
             body(s)
             return carry
 
-        lax.fori_loop(0, count_y, step, 0)
+        lax.fori_loop(0, count_y, step, 0, unroll=True)
 
     def fill_margins(ext):
         def one(s):
@@ -294,7 +306,7 @@
     rescale = math.sqrt(float(block_x * count_x) * float(block_y * count_y)) / rank
     params = pltpu.CompilerParams(vmem_limit_bytes=48 * 1024 * 1024)
     vmem = pl.BlockSpec(memory_space=pltpu.VMEM)
-    hbm = pl.BlockSpec(memory_space=pl.ANY)
+    hbm = pl.BlockSpec(memory_space=pltpu.HBM)
     f32 = jnp.float32
 
     packed = pl.pallas_call(

time: 69 us -> 65.9 us (0.955)
  Pallas kernels: 9.72 us -> 6.59 us
    pallas_call x1, Pallas kernels: 6.78 us -> 3.64 us  [z_plan(): pl.pallas_call(functools.partial(main_kernel, n_f, count_x, count_y, rank...]
where the time goes in v3:
time: 65.9 us; the launch traced here: 65.3 us
  blocking collectives  55.6 us (84%)
  Pallas kernels  6.59 us (10%)
  local copies, waits for them, and re-layouts  2.43 us (4%)
  between operations  0.66 us (1%)
    all_to_all x1, blocking collectives, z_plan(): lax.all_to_all(results.reshape(devices, tiles_out, HALF, n_z), ('gx', 'gy...  32 us
    all_to_all x1, blocking collectives, z_plan(): lax.all_to_all(packed.reshape(devices, tiles_in, HALF, n_z), ('gx', 'gy')...  23.6 us
    pallas_call x1, Pallas kernels, z_plan(): pl.pallas_call(functools.partial(main_kernel, n_f, count_x, count_y, rank...  3.64 us
    unnamed x6, local copies, waits for them, and re-layouts  2.43 us
    pallas_call x1, Pallas kernels, z_plan(): pl.pallas_call(functools.partial(unpack_kernel, block_x, block_y), out_sh...  1.72 us

profile of v3, /device:TPU:1, one launch (start us, length us, event | category | flops | bytes accessed | tf_op | source)
XLA Modules:
  0.0 65.3 jit_solution(8285380841813437444)
XLA Ops:
  0.6 0.0 copy-start
  0.6 1.0 %copy-done = f32[4,16,16,128]{3,2,1,0:T(8,128)S(1)} copy-done((f32[4,16,16,128]{3,2,1,0:T(8,128)S(1)}, f32[4,16,16,128]{3,2,1,0:T(8,128)}, u32[]{:S(2)}) %copy-start) | copy-done | bytes 524312
  1.7 0.0 copy-start.1
  1.7 0.7 %copy-done.1 = f32[16,32]{1,0:T(8,128)S(1)} copy-done((f32[16,32]{1,0:T(8,128)S(1)}, f32[16,32]{1,0:T(8,128)}, u32[]{:S(2)}) %copy-start.1) | copy-done | bytes 2072
  2.4 0.0 copy-start.2
  2.4 0.7 %copy-done.2 = f32[16,32]{1,0:T(8,128)S(1)} copy-done((f32[16,32]{1,0:T(8,128)S(1)}, f32[16,32]{1,0:T(8,128)}, u32[]{:S(2)}) %copy-start.2) | copy-done | bytes 2072
  3.1 1.2 %pack.1 = f32[16,2,9,4,128]{4,3,2,1,0:T(4,128)S(1)} custom-call(f32[4,256,128]{2,1,0:T(8,128)S(1)} %bitcast.11, f32[16,32]{1,0:T(8,128)S(1)} %copy-done.1, f32[16,32]{1,0:T(8,128)S(1)} %copy-done.2), custom_call_target="tpu_custom_call" | custom-call | tf_op jit(solution)/shard_map/pack/pallas_call | solution.py:312
  4.3 23.6 %all_to_all.10 = f32[32,9,4,128]{3,2,1,0:T(4,128)S(1)} all-to-all(f32[32,9,4,128]{3,2,1,0:T(4,128)S(1)} %bitcast.10), channel_id=1, replica_groups=mesh['gx'=8,'gy'=4] {'gx','gy'}, dimensions={0} | all-to-all | bytes 1179648 | tf_op jit(solution)/shard_map/all_to_all | solution.py:326
  27.9 3.6 %sections.1 = f32[8,4,17,4,128]{4,3,2,1,0:T(4,128)S(1)} custom-call(f32[8,4,9,4,128]{4,3,2,1,0:T(4,128)S(1)} %bitcast.9), custom_call_target="tpu_custom_call" | custom-call | tf_op jit(solution)/shard_map/sections/pallas_call | solution.py:330
  31.5 32.0 %all_to_all.11 = f32[32,17,4,128]{3,2,1,0:T(4,128)S(1)} all-to-all(f32[32,17,4,128]{3,2,1,0:T(4,128)S(1)} %bitcast.8), channel_id=1, replica_groups=mesh['gx'=8,'gy'=4] {'gx','gy'}, dimensions={0} | all-to-all | bytes 2228224 | tf_op jit(solution)/shard_map/all_to_all | solution.py:344
  63.5 1.7 %unpack.1 = (f32[4,256,128]{2,1,0:T(8,128)}, f32[4,4,8,128]{3,2,1,0:T(8,128)}, f32[4,256,128]{2,1,0:T(8,128)}) custom-call(f32[16,2,17,4,128]{4,3,2,1,0:T(4,128)S(1)} %bitcast.7), custom_call_target="tpu_custom_call" | custom-call | tf_op jit(solution)/shard_map/unpack/pallas_call | solution.py:349
Async XLA Ops:
  0.6 1.0 %copy-start = (f32[4,16,16,128]{3,2,1,0:T(8,128)S(1)}, f32[4,16,16,128]{3,2,1,0:T(8,128)}, u32[]{:S(2)}) copy-start(f32[4,16,16,128]{3,2,1,0:T(8,128)} %param.3) | copy-start | bytes 1572868
  1.7 0.7 %copy-start.1 = (f32[16,32]{1,0:T(8,128)S(1)}, f32[16,32]{1,0:T(8,128)}, u32[]{:S(2)}) copy-start(f32[16,32]{1,0:T(8,128)} %factor_x_hbm.1) | copy-start | bytes 6148
  2.4 0.7 %copy-start.2 = (f32[16,32]{1,0:T(8,128)S(1)}, f32[16,32]{1,0:T(8,128)}, u32[]{:S(2)}) copy-start(f32[16,32]{1,0:T(8,128)} %factor_y_hbm.1) | copy-start | bytes 6148

commit v4 on v3

--- a/solution.py
+++ b/solution.py
@@ -117,7 +117,10 @@
     return mul(a[0], b[0], dims) + (mul(a[0], b[1], dims) + mul(a[1], b[0], dims))
 
 
-def main_kernel(n_f, count_x, count_y, rank, rescale, in_ref, out_ref, ext_a, ext_b, ext_c, adv):
+def main_kernel(
+    n_f, count_x, count_y, rank, rescale, in_ref, adv, spread_ref, *refs
+):
+    column_refs, (ext_a, ext_b, ext_c, staged) = refs[:count_y], refs[count_y:]
     margin = 3
     inner = pl.ds(margin, SUBLANES)
     lower = lax.broadcasted_iota(jnp.int32, (margin, SUBLANES, LANES), 1) < HALF
@@ -195,11 +198,6 @@
             for y, block in enumerate(exchange(got, LANES // SUBLANES)):
                 ext_a[s, f, margin + y] = block
 
-    def send(block, s, f, base):
-        parts = exchange([block[y] for y in range(SUBLANES)], LANES // SUBLANES)
-        for i, part in enumerate(parts):
-            out_ref[i, s, base + 2 * f : base + 2 * f + 2] = part.reshape(2, HALF, LANES)
-
     def first(s, f, center, change):
         ext_b[s, f, inner] = center + change
 
@@ -207,9 +205,7 @@
         ext_c[s, f, inner] = 0.75 * ext_a[s, f, inner] + (0.25 * center + change)
 
     def third(s, f, center, change):
-        done = (1.0 / 3.0) * ext_a[s, f, inner] + ((2.0 / 3.0) * center + change)
-        adv[f, s] = done
-        send(done, s, f, 0)
+        adv[f, s] = (1.0 / 3.0) * ext_a[s, f, inner] + ((2.0 / 3.0) * center + change)
 
     each(arrive)
     fill_margins(ext_a)
@@ -245,53 +241,109 @@
 
     partial = mul_split(split(by_x(adv)), weights_x)
     core = mul_split(weights_y, split(partial), ((0,), (0,)))
-    columns = split(rescale * mul_split(weights_y, split(core)))
-
+    columns = rescale * mul_split(weights_y, split(core))
+    for part in range(2):
+        spread_ref[part] = weights_x[part]
+
+    block = plane // count_y
+    for s in range(count_y):
+        staged[s, 0:block] = columns[s * block : (s + 1) * block]
+        for z in range(HALF):
+            at = z * rank + s * SUBLANES
+            staged[s, block + z * SUBLANES : block + (z + 1) * SUBLANES] = core[at : at + SUBLANES]
+    own = lax.axis_index("gy")
+    for k, ref in enumerate(column_refs):
+        ref[...] = staged[lax.rem(own + k, count_y)]
+
+
+def send_kernel(count_x, adv, out_ref):
+    n_f, count_y = adv.shape[:2]
+    for s in range(count_y):
+        for f in range(n_f):
+            parts = exchange([adv[f, s, y] for y in range(SUBLANES)], LANES // SUBLANES)
+            for i, part in enumerate(parts):
+                out_ref[i, s, 2 * f : 2 * f + 2] = part.reshape(2, HALF, LANES)
+
+
+def expand_kernel(n_f, count_x, count_y, spread_ref, *refs):
+    in_refs, out_refs = refs[:count_y], refs[count_y : count_y + count_x]
+    held, staged = refs[count_y + count_x :]
+    own = lax.axis_index("gy")
+    for k, ref in enumerate(in_refs):
+        held[lax.rem(own + count_y - k, count_y)] = ref[...]
+    block = SUBLANES * SUBLANES
+    plane = count_y * block
+    columns = split(jnp.concatenate([held[s, 0:block] for s in range(count_y)], axis=0))
+    for f in range(n_f):
+        weights = [spread_ref[part, f * LANES : (f + 1) * LANES] for part in range(2)]
+        rebuilt = mul_split(columns, weights, ((1,), (1,)))
+        rebuilt = rebuilt.reshape(count_y, SUBLANES, SUBLANES, LANES)
+        for s in range(count_y):
+            parts = exchange([rebuilt[s, y] for y in range(SUBLANES)], LANES // SUBLANES)
+            for i, part in enumerate(parts):
+                at = (f * count_y + s) * SUBLANES
+                staged[i, at : at + SUBLANES] = part
+    by_f = [
+        exchange([held[s, block + z * SUBLANES : block + (z + 1) * SUBLANES] for z in range(HALF)], 1)
+        for s in range(count_y)
+    ]
     left = lax.broadcasted_iota(jnp.int32, (SUBLANES, LANES), 1) < LANES // 2
-    for s in range(count_y):
-        tiles = [core[z * rank + s * SUBLANES : z * rank + (s + 1) * SUBLANES] for z in range(HALF)]
-        tiles = exchange(exchange(tiles, 1), LANES // SUBLANES)
-        for i in range(count_x):
-            tile = tiles[i % HALF]
-            turned = pltpu.roll(tile, LANES // 2, 1)
-            if i >= HALF:
-                tile, turned = turned, tile
-            out_ref[i, s, 4 * n_f] = jnp.where(left[:HALF], tile[:HALF], turned[HALF:])
-
+    by_i = []
     for f in range(n_f):
-        weights = [part[f * LANES : (f + 1) * LANES] for part in weights_x]
-        adv[f] = mul_split(columns, weights, ((1,), (1,))).reshape(adv.shape[1:])
-
-    def depart(s):
-        for f in range(n_f):
-            send(adv[f, s], s, f, 2 * n_f)
-
-    each(depart)
-
-
-def unpack_kernel(block_x, block_y, in_ref, advanced_ref, core_ref, rebuilt_ref):
-    n_f = advanced_ref.shape[0]
-    tiles = LANES // SUBLANES
-    for target, base in ((advanced_ref, 0), (rebuilt_ref, 2 * n_f)):
-        for f in range(n_f):
-            for octet in range(2):
-                place = base + 2 * f + octet
-                matrix = jnp.concatenate([in_ref[:, 0, place], in_ref[:, 1, place]], axis=1)
-                turned = matrix.reshape(LANES, LANES).T
-                for y in range(SUBLANES):
-                    rows = pl.ds(octet * SUBLANES + y, block_x, stride=block_y)
-                    target[f, rows, :] = turned[y * block_x : (y + 1) * block_x]
-    upper = lax.broadcasted_iota(jnp.int32, (SUBLANES, LANES), 1) >= LANES // 2
-    got = []
-    for d in range(2 * tiles):
-        block = in_ref[d // 2, d % 2, 4 * n_f]
-        got.append(jnp.concatenate([block, pltpu.roll(block, LANES // 2, 1)], axis=0))
-    kept = [
-        jnp.where(upper, pltpu.roll(got[d + tiles], LANES // 2, 1), got[d]) for d in range(tiles)
-    ]
+        tiles = exchange([by_f[s][f] for s in range(count_y)], HALF)
+        by_i.append(exchange(tiles, LANES // SUBLANES))
+    for i in range(count_x):
+        for pair in range(n_f // 2):
+            low, high = by_i[2 * pair][i % HALF], by_i[2 * pair + 1][i % HALF]
+            if i < HALF:
+                tile = jnp.where(left, low, pltpu.roll(high, LANES // 2, 1))
+            else:
+                tile = jnp.where(left, pltpu.roll(low, LANES // 2, 1), high)
+            at = (n_f * count_y + pair) * SUBLANES
+            staged[i, at : at + SUBLANES] = tile
+    own = lax.axis_index("gx")
+    for k, ref in enumerate(out_refs):
+        ref[...] = staged[lax.rem(own + k, count_x)]
+
+
+def scatter_rows(turned, octet, block_x, block_y, target, f):
+    for y in range(SUBLANES):
+        rows = pl.ds(octet * SUBLANES + y, block_x, stride=block_y)
+        target[f, rows, :] = turned[y * block_x : (y + 1) * block_x]
+
+
+def advanced_kernel(block_x, block_y, in_ref, advanced_ref):
+    for f in range(advanced_ref.shape[0]):
+        for octet in range(2):
+            place = 2 * f + octet
+            matrix = jnp.concatenate([in_ref[:, 0, place], in_ref[:, 1, place]], axis=1)
+            turned = matrix.reshape(LANES, LANES).T
+            scatter_rows(turned, octet, block_x, block_y, advanced_ref, f)
+
+
+def rebuilt_kernel(block_x, block_y, count_x, count_y, *refs):
+    in_refs, (rebuilt_ref, core_ref, held) = refs[:count_x], refs[count_x:]
+    n_f = rebuilt_ref.shape[0]
+    own = lax.axis_index("gx")
+    for k, ref in enumerate(in_refs):
+        held[lax.rem(own + count_x - k, count_x)] = ref[...]
+    pairs = count_y // 2
+    lower = lax.broadcasted_iota(jnp.int32, (count_x, pairs, SUBLANES, LANES), 2) < HALF
+    for f in range(n_f):
+        at = pl.ds(f * count_y * SUBLANES, count_y * SUBLANES)
+        tiles = held[:, at, :].reshape(count_x, pairs, 2, SUBLANES, LANES)
+        even, odd = tiles[:, :, 0], tiles[:, :, 1]
+        first = jnp.where(lower, even, pltpu.roll(odd, HALF, 2))
+        second = jnp.where(lower, pltpu.roll(even, HALF, 2), odd)
+        for octet, part in enumerate((first, second)):
+            turned = part.reshape(LANES, LANES).T
+            scatter_rows(turned, octet, block_x, block_y, rebuilt_ref, f)
     a_count = core_ref.shape[1]
-    for place, block in enumerate(exchange(kept, HALF)):
-        core_ref[place // a_count, place % a_count] = block
+    for pair in range(n_f // 2):
+        at = (n_f * count_y + pair) * SUBLANES
+        tiles = exchange([held[i, at : at + SUBLANES] for i in range(count_x)], LANES // SUBLANES)
+        for place, tile in enumerate(tiles):
+            core_ref[2 * pair + place // a_count, place % a_count] = tile
 
 
 def z_plan(fields, factor_x, factor_y):
@@ -301,60 +353,101 @@
     count_y = lax.axis_size("gy")
     devices = count_x * count_y
     pairs = devices // 2
-    tiles_in = 2 * n_f + 1
-    tiles_out = 4 * n_f + 1
     rescale = math.sqrt(float(block_x * count_x) * float(block_y * count_y)) / rank
-    params = pltpu.CompilerParams(vmem_limit_bytes=48 * 1024 * 1024)
     vmem = pl.BlockSpec(memory_space=pltpu.VMEM)
     hbm = pl.BlockSpec(memory_space=pltpu.HBM)
     f32 = jnp.float32
 
-    packed = pl.pallas_call(
+    def array(shape, dtype=f32):
+        return jax.ShapeDtypeStruct(shape, dtype)
+
+    def call(kernel, name, outs, scratch, operands, space=vmem, limit=48 * 1024 * 1024):
+        return pl.pallas_call(
+            kernel,
+            out_shape=tuple(outs),
+            in_specs=[space] * len(operands),
+            out_specs=(vmem,) * len(outs),
+            scratch_shapes=scratch,
+            compiler_params=pltpu.CompilerParams(vmem_limit_bytes=limit),
+            cost_estimate=pl.CostEstimate(flops=10**9, bytes_accessed=0, transcendentals=0),
+            name=name,
+        )(*operands)
+
+    def swap(blocks, tiles):
+        blocks = blocks.reshape(devices, tiles, HALF, n_z)
+        return lax.all_to_all(blocks, ("gx", "gy"), 0, 0, tiled=True)
+
+    def pass_on(blocks, axis):
+        count = len(blocks)
+        moved = [
+            lax.ppermute(block, axis, [(i, (i + k) % count) for i in range(count)])
+            for k, block in enumerate(blocks)
+            if k
+        ]
+        return [blocks[0]] + moved
+
+    flat = (n_f, block_x * block_y, n_z)
+    (packed,) = call(
         pack_kernel,
-        out_shape=jax.ShapeDtypeStruct((pairs, 2, tiles_in, HALF, n_z), f32),
-        in_specs=[hbm] * 3,
-        out_specs=vmem,
-        scratch_shapes=[
-            pltpu.VMEM((n_f, block_x * block_y, n_z), f32),
+        "pack",
+        [array((pairs, 2, 2 * n_f + 1, HALF, n_z))],
+        [
+            pltpu.VMEM(flat, f32),
             pltpu.VMEM(factor_x.shape, f32),
             pltpu.VMEM(factor_y.shape, f32),
             pltpu.SemaphoreType.DMA((n_f + 2,)),
         ],
-        compiler_params=params,
-        name="pack",
-    )(fields.reshape(n_f, block_x * block_y, n_z), factor_x, factor_y)
-    planes = lax.all_to_all(
-        packed.reshape(devices, tiles_in, HALF, n_z), ("gx", "gy"), 0, 0, tiled=True
-    )
+        (fields.reshape(flat), factor_x, factor_y),
+        hbm,
+        None,
+    )
+    planes = swap(packed, 2 * n_f + 1).reshape(count_x, count_y, 2 * n_f + 1, HALF, n_z)
     extended = pltpu.VMEM((count_y, n_f, SUBLANES + 6, SUBLANES, LANES), f32)
-    results = pl.pallas_call(
+    rows = SUBLANES * SUBLANES + HALF * SUBLANES
+    held, spread, *columns = call(
         functools.partial(main_kernel, n_f, count_x, count_y, rank, rescale),
-        out_shape=jax.ShapeDtypeStruct((count_x, count_y, tiles_out, HALF, n_z), f32),
-        in_specs=[vmem],
-        out_specs=vmem,
-        scratch_shapes=[
-            extended,
-            extended,
-            extended,
-            pltpu.VMEM((n_f, count_y, SUBLANES, SUBLANES, LANES), f32),
+        "sections",
+        [
+            array((n_f, count_y, SUBLANES, SUBLANES, LANES)),
+            array((2, n_f * LANES, LANES), jnp.bfloat16),
+        ]
+        + [array((rows, LANES))] * count_y,
+        [extended] * 3 + [pltpu.VMEM((count_y, rows, LANES), f32)],
+        (planes,),
+    )
+    columns = pass_on(columns, "gy")
+    (sent,) = call(
+        functools.partial(send_kernel, count_x),
+        "send",
+        [array((count_x, count_y, 2 * n_f, HALF, n_z))],
+        [],
+        (held,),
+    )
+    sent, columns = lax.optimization_barrier((sent, columns))
+    sent = swap(sent, 2 * n_f).reshape(pairs, 2, 2 * n_f, HALF, n_z)
+    rows = (n_f * count_y + n_f // 2) * SUBLANES
+    blocks = call(
+        functools.partial(expand_kernel, n_f, count_x, count_y),
+        "expand",
+        [array((rows, LANES))] * count_x,
+        [
+            pltpu.VMEM((count_y,) + columns[0].shape, f32),
+            pltpu.VMEM((count_x, rows, LANES), f32),
         ],
-        compiler_params=params,
-        name="sections",
-    )(planes.reshape(count_x, count_y, tiles_in, HALF, n_z))
-    back = lax.all_to_all(
-        results.reshape(devices, tiles_out, HALF, n_z), ("gx", "gy"), 0, 0, tiled=True
-    )
-    flat = jax.ShapeDtypeStruct((n_f, block_x * block_y, n_z), f32)
-    core = jax.ShapeDtypeStruct((n_f, rank // count_x, rank // count_y, n_z), f32)
-    advanced, core_tensor, rebuilt = pl.pallas_call(
-        functools.partial(unpack_kernel, block_x, block_y),
-        out_shape=(flat, core, flat),
-        in_specs=[vmem],
-        out_specs=(vmem, vmem, vmem),
-        compiler_params=params,
-        name="unpack",
-    )(back.reshape(pairs, 2, tiles_out, HALF, n_z))
-    return advanced.reshape(fields.shape), core_tensor, rebuilt.reshape(fields.shape)
+        (spread, *columns),
+    )
+    blocks = pass_on(blocks, "gx")
+    (advanced,) = call(
+        functools.partial(advanced_kernel, block_x, block_y), "advanced", [array(flat)], [], (sent,)
+    )
+    rebuilt, core = call(
+        functools.partial(rebuilt_kernel, block_x, block_y, count_x, count_y),
+        "rebuilt",
+        [array(flat), array((n_f, rank // count_x, rank // count_y, n_z))],
+        [pltpu.VMEM((count_x, rows, LANES), f32)],
+        tuple(blocks),
+    )
+    return advanced.reshape(fields.shape), core, rebuilt.reshape(fields.shape)
 
 
 def extended(block, sides, width):

time: 65.9 us -> 57.4 us (0.87)
  blocking collectives: 55.6 us -> 23.8 us
  starting transfers between devices: 0 us -> 16.3 us
  waiting for transfers between devices: 0 us -> 7.26 us
  Pallas kernels: 6.59 us -> 9.11 us
  local copies, waits for them, and re-layouts: 2.43 us -> 0 us
    all_to_all x2 -> x1, blocking collectives: 55.6 us -> 23.8 us  [swap(): return lax.all_to_all(blocks, ('gx', 'gy'), 0, 0, tiled=True)]
    ppermute x0 -> x10, starting transfers between devices: none -> 10.6 us  [pass_on(): lax.ppermute(block, axis, [(i, (i + k) % count) for i in range(count)])]
    ppermute x0 -> x10, waiting for transfers between devices: none -> 7.25 us  [pass_on(): lax.ppermute(block, axis, [(i, (i + k) % count) for i in range(count)])]
    all_to_all x0 -> x1, starting transfers between devices: none -> 5.69 us  [swap(): return lax.all_to_all(blocks, ('gx', 'gy'), 0, 0, tiled=True)]
    pallas_call x3 -> x6, Pallas kernels: 6.59 us -> 9.11 us  [call(): pl.pallas_call(kernel, out_shape=tuple(outs), in_specs=[space] * len(oper...]
    unnamed x6 -> x0, local copies, waits for them, and re-layouts: 2.43 us -> none
  transfers between devices with their start and end apart: 0 -> 11, of which waited for: 0 -> 6; matrix products, arithmetic and copies ran while one was open for 0% -> 0% of each run, Pallas kernels for 0% -> 3%
where the time goes in v4:
time: 57.4 us; the launch traced here: 57.1 us
  blocking collectives  23.8 us (41%)
  starting transfers between devices  16.3 us (28%)
  Pallas kernels  9.11 us (16%)
  waiting for transfers between devices  7.26 us (13%)
  between operations  0.68 us (1%)
    all_to_all x1, blocking collectives, swap(): return lax.all_to_all(blocks, ('gx', 'gy'), 0, 0, tiled=True)  23.8 us
    ppermute x10, starting transfers between devices, pass_on(): lax.ppermute(block, axis, [(i, (i + k) % count) for i in range(count)])  10.6 us
    pallas_call x6, Pallas kernels, call(): pl.pallas_call(kernel, out_shape=tuple(outs), in_specs=[space] * len(oper...  9.11 us
    ppermute x10, waiting for transfers between devices, pass_on(): lax.ppermute(block, axis, [(i, (i + k) % count) for i in range(count)])  7.25 us
    all_to_all x1, starting transfers between devices, swap(): return lax.all_to_all(blocks, ('gx', 'gy'), 0, 0, tiled=True)  5.69 us
  transfers between devices with their start and end apart: 11, of which 6 were waited for; matrix products, arithmetic and copies ran while one was open for 0% of the time, Pallas kernels for 3%

profile of v4, /device:TPU:1, one launch (start us, length us, event | category | flops | bytes accessed | tf_op | source)
XLA Modules:
  0.0 57.1 jit_solution(17908761514492706687)
XLA Ops:
  0.6 2.3 %pack.1 = f32[16,2,9,4,128]{4,3,2,1,0:T(4,128)} custom-call(f32[4,256,128]{2,1,0:T(8,128)} %bitcast.10, f32[16,32]{1,0:T(8,128)} %factor_x_hbm.1, f32[16,32]{1,0:T(8,128)} %factor_y_hbm.1), custom_call_target="tpu_custom_call" | custom-call | flops 1000000000 | tf_op jit(solution)/shard_map/pack/pallas_call | solution.py:365
  2.9 23.8 %all_to_all.10 = f32[32,9,4,128]{3,2,1,0:T(4,128)S(1)} all-to-all(f32[32,9,4,128]{3,2,1,0:T(4,128)} %bitcast.9), channel_id=1, replica_groups=mesh['gx'=8,'gy'=4] {'gx','gy'}, dimensions={0} | all-to-all | bytes 1179648 | tf_op jit(solution)/shard_map/all_to_all | solution.py:378
  26.7 2.4 %sections.1 = (f32[4,4,8,8,128]{4,3,2,1,0:T(8,128)S(1)}, bf16[2,512,128]{2,1,0:T(8,128)(2,1)S(1)}, f32[96,128]{1,0:T(8,128)S(1)}, f32[96,128]{1,0:T(8,128)S(1)},...) custom-call(f32[8,4,9,4,128]{4,3,2,1,0:T(4,128)S(1)} %bitcast.7), custom_call_target="tpu_custom_call" | custom-call | flops 1000000000 | tf_op jit(solution)/shard_map/sections/pallas_call | solution.py:365
  29.1 0.1 collective-permute-start
  29.2 1.2 %collective-permute-start.1 = (f32[96,128]{1,0:T(8,128)S(1)}, f32[96,128]{1,0:T(8,128)S(1)}, u32[]{:S(2)}, u32[]{:S(2)}) collective-permute-start(f32[96,128]{1,0:T(8,128)S(1)} %get-tuple-element.27), channel_id=1, source_target_pairs={{0,2},{1,3},{2,0},{3,1},{4,6},{5,7},{6,4},{7,5},{8,10},{9,11},{10,... | collective-permute-start | bytes 147464 | tf_op jit(solution)/shard_map/ppermute | solution.py:383
  30.4 2.1 %collective-permute-start.2 = (f32[96,128]{1,0:T(8,128)S(1)}, f32[96,128]{1,0:T(8,128)S(1)}, u32[]{:S(2)}, u32[]{:S(2)}) collective-permute-start(f32[96,128]{1,0:T(8,128)S(1)} %get-tuple-element.28), channel_id=1, source_target_pairs={{0,3},{1,0},{2,1},{3,2},{4,7},{5,4},{6,5},{7,6},{8,11},{9,8},{10,9... | collective-permute-start | bytes 147464 | tf_op jit(solution)/shard_map/ppermute | solution.py:383
  32.4 1.6 %send.1 = f32[8,4,8,4,128]{4,3,2,1,0:T(4,128)} custom-call(f32[4,4,8,8,128]{4,3,2,1,0:T(8,128)S(1)} %get-tuple-element.24.adv), custom_call_target="tpu_custom_call" | custom-call | flops 1000000000 | tf_op jit(solution)/shard_map/send/pallas_call | solution.py:365
  34.0 0.2 collective-permute-done.refs_1_
  34.2 0.0 collective-permute-done.1.refs_2_
  34.2 0.5 collective-permute-done.2.refs_3_
  34.7 5.7 %all-to-all-start.1 = ((f32[32,8,4,128]{3,2,1,0:T(4,128)}), f32[32,8,4,128]{3,2,1,0:T(4,128)S(1)}, u32[]{:S(2)}, u32[]{:S(2)}) async-start(f32[32,8,4,128]{3,2,1,0:T(4,128)} %bitcast.3), calls=%async_computation.1 | async-start | bytes 1048576 | tf_op jit(solution)/shard_map/all_to_all | solution.py:378
  40.4 0.7 %expand.1 = (f32[144,128]{1,0:T(8,128)S(1)}, f32[144,128]{1,0:T(8,128)S(1)}, f32[144,128]{1,0:T(8,128)S(1)}, f32[144,128]{1,0:T(8,128)S(1)}, f32[144,128]{1,0:T(...) custom-call(bf16[2,512,128]{2,1,0:T(8,128)(2,1)S(1)} %get-tuple-element.30.spread_ref, ...), custom_call_target="tpu_custom_call" | custom-call | flops 1000000000 | tf_op jit(solution)/shard_map/expand/pallas_call | solution.py:365
  41.1 1.7 %collective-permute-start.3 = (f32[144,128]{1,0:T(8,128)S(1)}, f32[144,128]{1,0:T(8,128)S(1)}, u32[]{:S(2)}, u32[]{:S(2)}) collective-permute-start(f32[144,128]{1,0:T(8,128)S(1)} %get-tuple-element.36), channel_id=1, source_target_pairs={{0,4},{4,8},{8,12},{12,16},{16,20},{20,24},{24,28},{28,0},{1,5},{5... | collective-permute-start | bytes 221192 | tf_op jit(solution)/shard_map/ppermute | solution.py:383
  42.8 1.2 %collective-permute-start.4 = (f32[144,128]{1,0:T(8,128)S(1)}, f32[144,128]{1,0:T(8,128)S(1)}, u32[]{:S(2)}, u32[]{:S(2)}) collective-permute-start(f32[144,128]{1,0:T(8,128)S(1)} %get-tuple-element.37), channel_id=1, source_target_pairs={{0,8},{4,12},{8,16},{12,20},{16,24},{20,28},{24,0},{28,4},{1,9},{5... | collective-permute-start | bytes 221192 | tf_op jit(solution)/shard_map/ppermute | solution.py:383
  43.9 0.4 collective-permute-start.5
  44.4 0.3 collective-permute-start.6
  44.7 2.3 %collective-permute-start.7 = (f32[144,128]{1,0:T(8,128)S(1)}, f32[144,128]{1,0:T(8,128)S(1)}, u32[]{:S(2)}, u32[]{:S(2)}) collective-permute-start(f32[144,128]{1,0:T(8,128)S(1)} %get-tuple-element.40), channel_id=1, source_target_pairs={{0,20},{4,24},{8,28},{12,0},{16,4},{20,8},{24,12},{28,16},{1,21},{... | collective-permute-start | bytes 221192 | tf_op jit(solution)/shard_map/ppermute | solution.py:383
  46.9 0.0 collective-permute-done.3.refs_1_
  46.9 1.4 %collective-permute-start.8 = (f32[144,128]{1,0:T(8,128)S(1)}, f32[144,128]{1,0:T(8,128)S(1)}, u32[]{:S(2)}, u32[]{:S(2)}) collective-permute-start(f32[144,128]{1,0:T(8,128)S(1)} %get-tuple-element.41), channel_id=1, source_target_pairs={{0,24},{4,28},{8,0},{12,4},{16,8},{20,12},{24,16},{28,20},{1,25},{... | collective-permute-start | bytes 221192 | tf_op jit(solution)/shard_map/ppermute | solution.py:383
  48.4 2.3 %collective-permute-done.4.refs_2_ = f32[144,128]{1,0:T(8,128)S(1)} collective-permute-done((f32[144,128]{1,0:T(8,128)S(1)}, f32[144,128]{1,0:T(8,128)S(1)}, u32[]{:S(2)}, u32[]{:S(2)}) %collective-permute-start.4) | collective-permute-done | bytes 73760 | tf_op jit(solution)/shard_map/ppermute | solution.py:383
  50.6 0.0 collective-permute-start.9
  50.6 1.4 %collective-permute-done.5.refs_3_ = f32[144,128]{1,0:T(8,128)S(1)} collective-permute-done((f32[144,128]{1,0:T(8,128)S(1)}, f32[144,128]{1,0:T(8,128)S(1)}, u32[]{:S(2)}, u32[]{:S(2)}) %collective-permute-start.5) | collective-permute-done | bytes 73760 | tf_op jit(solution)/shard_map/ppermute | solution.py:383
  52.0 2.8 %collective-permute-done.6.refs_4_ = f32[144,128]{1,0:T(8,128)S(1)} collective-permute-done((f32[144,128]{1,0:T(8,128)S(1)}, f32[144,128]{1,0:T(8,128)S(1)}, u32[]{:S(2)}, u32[]{:S(2)}) %collective-permute-start.6) | collective-permute-done | bytes 73760 | tf_op jit(solution)/shard_map/ppermute | solution.py:383
  54.8 0.1 collective-permute-done.7.refs_5_
  55.0 0.0 collective-permute-done.8.refs_6_
  55.0 0.0 collective-permute-done.9.refs_7_
  55.0 1.1 %rebuilt.1 = (f32[4,256,128]{2,1,0:T(8,128)}, f32[4,4,8,128]{3,2,1,0:T(8,128)}) custom-call(f32[144,128]{1,0:T(8,128)S(1)} %get-tuple-element.35.refs_0_, f32[144,128]{1,0:T(8,128)S(1)} %collective-permute-done.3.refs_1_, f32[144,128]{1,0:T(8,128)S(1)} %collective-permute-done.4.refs_2_, f32[144,128]{1,0:T(8,128)S(1)} %collective-permute-done.5.refs_3_, ...), custom_call_target="tpu_custom_call" | custom-call | flops 1000000000 | tf_op jit(solution)/shard_map/rebuilt/pallas_call | solution.py:365
  56.1 0.0 all-to-all-done.1
  56.1 1.0 %advanced.1 = f32[4,256,128]{2,1,0:T(8,128)} custom-call(f32[16,2,8,4,128]{4,3,2,1,0:T(4,128)S(1)} %bitcast.8), custom_call_target="tpu_custom_call" | custom-call | flops 1000000000 | tf_op jit(solution)/shard_map/advanced/pallas_call | solution.py:365
Async XLA Ops:
  29.1 5.1 %collective-permute-start = (f32[96,128]{1,0:T(8,128)S(1)}, f32[96,128]{1,0:T(8,128)S(1)}, u32[]{:S(2)}, u32[]{:S(2)}) collective-permute-start(f32[96,128]{1,0:T(8,128)S(1)} %get-tuple-element.26), channel_id=1, source_target_pairs={{0,1},{1,2},{2,3},{3,0},{4,5},{5,6},{6,7},{7,4},{8,9},{9,10},{10,1... | collective-permute-start | bytes 147464 | tf_op jit(solution)/shard_map/ppermute | solution.py:383
  29.2 5.0 %collective-permute-start.1 = (f32[96,128]{1,0:T(8,128)S(1)}, f32[96,128]{1,0:T(8,128)S(1)}, u32[]{:S(2)}, u32[]{:S(2)}) collective-permute-start(f32[96,128]{1,0:T(8,128)S(1)} %get-tuple-element.27), channel_id=1, source_target_pairs={{0,2},{1,3},{2,0},{3,1},{4,6},{5,7},{6,4},{7,5},{8,10},{9,11},{10,... | collective-permute-start | bytes 147464 | tf_op jit(solution)/shard_map/ppermute | solution.py:383
  30.4 4.3 %collective-permute-start.2 = (f32[96,128]{1,0:T(8,128)S(1)}, f32[96,128]{1,0:T(8,128)S(1)}, u32[]{:S(2)}, u32[]{:S(2)}) collective-permute-start(f32[96,128]{1,0:T(8,128)S(1)} %get-tuple-element.28), channel_id=1, source_target_pairs={{0,3},{1,0},{2,1},{3,2},{4,7},{5,4},{6,5},{7,6},{8,11},{9,8},{10,9... | collective-permute-start | bytes 147464 | tf_op jit(solution)/shard_map/ppermute | solution.py:383
  34.7 21.4 %all-to-all-start.1 = ((f32[32,8,4,128]{3,2,1,0:T(4,128)}), f32[32,8,4,128]{3,2,1,0:T(4,128)S(1)}, u32[]{:S(2)}, u32[]{:S(2)}) async-start(f32[32,8,4,128]{3,2,1,0:T(4,128)} %bitcast.3), calls=%async_computation.1 | async-start | bytes 1048576 | tf_op jit(solution)/shard_map/all_to_all | solution.py:378
  41.1 5.8 %collective-permute-start.3 = (f32[144,128]{1,0:T(8,128)S(1)}, f32[144,128]{1,0:T(8,128)S(1)}, u32[]{:S(2)}, u32[]{:S(2)}) collective-permute-start(f32[144,128]{1,0:T(8,128)S(1)} %get-tuple-element.36), channel_id=1, source_target_pairs={{0,4},{4,8},{8,12},{12,16},{16,20},{20,24},{24,28},{28,0},{1,5},{5... | collective-permute-start | bytes 221192 | tf_op jit(solution)/shard_map/ppermute | solution.py:383
  42.8 7.9 %collective-permute-start.4 = (f32[144,128]{1,0:T(8,128)S(1)}, f32[144,128]{1,0:T(8,128)S(1)}, u32[]{:S(2)}, u32[]{:S(2)}) collective-permute-start(f32[144,128]{1,0:T(8,128)S(1)} %get-tuple-element.37), channel_id=1, source_target_pairs={{0,8},{4,12},{8,16},{12,20},{16,24},{20,28},{24,0},{28,4},{1,9},{5... | collective-permute-start | bytes 221192 | tf_op jit(solution)/shard_map/ppermute | solution.py:383
  43.9 8.1 %collective-permute-start.5 = (f32[144,128]{1,0:T(8,128)S(1)}, f32[144,128]{1,0:T(8,128)S(1)}, u32[]{:S(2)}, u32[]{:S(2)}) collective-permute-start(f32[144,128]{1,0:T(8,128)S(1)} %get-tuple-element.38), channel_id=1, source_target_pairs={{0,12},{4,16},{8,20},{12,24},{16,28},{20,0},{24,4},{28,8},{1,13},{... | collective-permute-start | bytes 221192 | tf_op jit(solution)/shard_map/ppermute | solution.py:383
  44.4 10.4 %collective-permute-start.6 = (f32[144,128]{1,0:T(8,128)S(1)}, f32[144,128]{1,0:T(8,128)S(1)}, u32[]{:S(2)}, u32[]{:S(2)}) collective-permute-start(f32[144,128]{1,0:T(8,128)S(1)} %get-tuple-element.39), channel_id=1, source_target_pairs={{0,16},{4,20},{8,24},{12,28},{16,0},{20,4},{24,8},{28,12},{1,17},{... | collective-permute-start | bytes 221192 | tf_op jit(solution)/shard_map/ppermute | solution.py:383
  44.7 10.3 %collective-permute-start.7 = (f32[144,128]{1,0:T(8,128)S(1)}, f32[144,128]{1,0:T(8,128)S(1)}, u32[]{:S(2)}, u32[]{:S(2)}) collective-permute-start(f32[144,128]{1,0:T(8,128)S(1)} %get-tuple-element.40), channel_id=1, source_target_pairs={{0,20},{4,24},{8,28},{12,0},{16,4},{20,8},{24,12},{28,16},{1,21},{... | collective-permute-start | bytes 221192 | tf_op jit(solution)/shard_map/ppermute | solution.py:383
  46.9 8.0 %collective-permute-start.8 = (f32[144,128]{1,0:T(8,128)S(1)}, f32[144,128]{1,0:T(8,128)S(1)}, u32[]{:S(2)}, u32[]{:S(2)}) collective-permute-start(f32[144,128]{1,0:T(8,128)S(1)} %get-tuple-element.41), channel_id=1, source_target_pairs={{0,24},{4,28},{8,0},{12,4},{16,8},{20,12},{24,16},{28,20},{1,25},{... | collective-permute-start | bytes 221192 | tf_op jit(solution)/shard_map/ppermute | solution.py:383
  50.6 4.3 %collective-permute-start.9 = (f32[144,128]{1,0:T(8,128)S(1)}, f32[144,128]{1,0:T(8,128)S(1)}, u32[]{:S(2)}, u32[]{:S(2)}) collective-permute-start(f32[144,128]{1,0:T(8,128)S(1)} %get-tuple-element.42), channel_id=1, source_target_pairs={{0,28},{4,0},{8,4},{12,8},{16,12},{20,16},{24,20},{28,24},{1,29},{... | collective-permute-start | bytes 221192 | tf_op jit(solution)/shard_map/ppermute | solution.py:383

commit v5 on v4

--- a/solution.py
+++ b/solution.py
@@ -68,7 +68,9 @@
     return blocks
 
 
-def pack_kernel(fields_hbm, factor_x_hbm, factor_y_hbm, out_ref, fields_ref, x_ref, y_ref, sems):
+def pack_kernel(
+    fields_hbm, factor_x_hbm, factor_y_hbm, out_hbm, out_ref, fields_ref, x_ref, y_ref, sems, out_sems
+):
     n_f, rows, _ = fields_ref.shape
     block_x = x_ref.shape[0]
     block_y = rows // block_x
@@ -80,6 +82,12 @@
     copies.append(pltpu.make_async_copy(factor_y_hbm, y_ref, sems.at[n_f + 1]))
     for copy in copies:
         copy.start()
+
+    def leave(f, tiles):
+        at = (slice(None), slice(None), pl.ds(2 * f, tiles))
+        return pltpu.make_async_copy(out_ref.at[at], out_hbm.at[at], out_sems.at[f])
+
+    leaving = [leave(f, 2) for f in range(n_f)] + [leave(n_f, 1)]
     for f in range(n_f):
         copies[f].wait()
         for octet in range(2):
@@ -93,6 +101,7 @@
             turned = matrix.T.reshape(tiles, SUBLANES, LANES)
             out_ref[:, 0, 2 * f + octet] = turned[:, :HALF]
             out_ref[:, 1, 2 * f + octet] = turned[:, HALF:]
+        leaving[f].start()
     copies[n_f].wait()
     copies[n_f + 1].wait()
     part_x = lax.axis_index("gy")
@@ -101,6 +110,9 @@
     own_y = y_ref[pl.ds(part_y * HALF, HALF), :]
     factors = jnp.concatenate([own_x, own_y, own_y, own_y], axis=1)
     out_ref[:, :, 2 * n_f] = jnp.broadcast_to(factors[None, None], (tiles, 2, HALF, LANES))
+    leaving[n_f].start()
+    for copy in leaving:
+        copy.wait()
 
 
 def split(value):
@@ -118,9 +130,10 @@
 
 
 def main_kernel(
-    n_f, count_x, count_y, rank, rescale, in_ref, adv, spread_ref, *refs
+    n_f, count_x, count_y, rank, rescale, in_ref, sent_ref, spread_ref, *refs
 ):
-    column_refs, (ext_a, ext_b, ext_c, staged) = refs[:count_y], refs[count_y:]
+    column_refs = refs[:count_y]
+    ext_a, ext_b, ext_c, adv, staged = refs[count_y:]
     margin = 3
     inner = pl.ds(margin, SUBLANES)
     lower = lax.broadcasted_iota(jnp.int32, (margin, SUBLANES, LANES), 1) < HALF
@@ -205,7 +218,11 @@
         ext_c[s, f, inner] = 0.75 * ext_a[s, f, inner] + (0.25 * center + change)
 
     def third(s, f, center, change):
-        adv[f, s] = (1.0 / 3.0) * ext_a[s, f, inner] + ((2.0 / 3.0) * center + change)
+        done = (1.0 / 3.0) * ext_a[s, f, inner] + ((2.0 / 3.0) * center + change)
+        adv[f, s] = done
+        parts = exchange([done[y] for y in range(SUBLANES)], LANES // SUBLANES)
+        for i, part in enumerate(parts):
+            sent_ref[i, s, 2 * f : 2 * f + 2] = part.reshape(2, HALF, LANES)
 
     each(arrive)
     fill_margins(ext_a)
@@ -254,15 +271,6 @@
     own = lax.axis_index("gy")
     for k, ref in enumerate(column_refs):
         ref[...] = staged[lax.rem(own + k, count_y)]
-
-
-def send_kernel(count_x, adv, out_ref):
-    n_f, count_y = adv.shape[:2]
-    for s in range(count_y):
-        for f in range(n_f):
-            parts = exchange([adv[f, s, y] for y in range(SUBLANES)], LANES // SUBLANES)
-            for i, part in enumerate(parts):
-                out_ref[i, s, 2 * f : 2 * f + 2] = part.reshape(2, HALF, LANES)
 
 
 def expand_kernel(n_f, count_x, count_y, spread_ref, *refs):
@@ -306,27 +314,46 @@
         ref[...] = staged[lax.rem(own + k, count_x)]
 
 
+def leave_fields(ref, hbm, sems):
+    return [
+        pltpu.make_async_copy(ref.at[f], hbm.at[f], sems.at[f]) for f in range(ref.shape[0])
+    ]
+
+
 def scatter_rows(turned, octet, block_x, block_y, target, f):
     for y in range(SUBLANES):
         rows = pl.ds(octet * SUBLANES + y, block_x, stride=block_y)
         target[f, rows, :] = turned[y * block_x : (y + 1) * block_x]
 
 
-def advanced_kernel(block_x, block_y, in_ref, advanced_ref):
+def advanced_kernel(block_x, block_y, in_ref, advanced_hbm, advanced_ref, sems):
+    leaving = leave_fields(advanced_ref, advanced_hbm, sems)
     for f in range(advanced_ref.shape[0]):
         for octet in range(2):
             place = 2 * f + octet
             matrix = jnp.concatenate([in_ref[:, 0, place], in_ref[:, 1, place]], axis=1)
             turned = matrix.reshape(LANES, LANES).T
             scatter_rows(turned, octet, block_x, block_y, advanced_ref, f)
+        leaving[f].start()
+    for copy in leaving:
+        copy.wait()
 
 
 def rebuilt_kernel(block_x, block_y, count_x, count_y, *refs):
-    in_refs, (rebuilt_ref, core_ref, held) = refs[:count_x], refs[count_x:]
+    in_refs, (rebuilt_hbm, core_hbm, held, rebuilt_ref, core_ref, sems) = refs[:count_x], refs[count_x:]
     n_f = rebuilt_ref.shape[0]
+    leaving = leave_fields(rebuilt_ref, rebuilt_hbm, sems)
+    leaving.append(pltpu.make_async_copy(core_ref, core_hbm, sems.at[n_f]))
     own = lax.axis_index("gx")
     for k, ref in enumerate(in_refs):
         held[lax.rem(own + count_x - k, count_x)] = ref[...]
+    a_count = core_ref.shape[1]
+    for pair in range(n_f // 2):
+        at = (n_f * count_y + pair) * SUBLANES
+        tiles = exchange([held[i, at : at + SUBLANES] for i in range(count_x)], LANES // SUBLANES)
+        for place, tile in enumerate(tiles):
+            core_ref[2 * pair + place // a_count, place % a_count] = tile
+    leaving[n_f].start()
     pairs = count_y // 2
     lower = lax.broadcasted_iota(jnp.int32, (count_x, pairs, SUBLANES, LANES), 2) < HALF
     for f in range(n_f):
@@ -338,12 +365,9 @@
         for octet, part in enumerate((first, second)):
             turned = part.reshape(LANES, LANES).T
             scatter_rows(turned, octet, block_x, block_y, rebuilt_ref, f)
-    a_count = core_ref.shape[1]
-    for pair in range(n_f // 2):
-        at = (n_f * count_y + pair) * SUBLANES
-        tiles = exchange([held[i, at : at + SUBLANES] for i in range(count_x)], LANES // SUBLANES)
-        for place, tile in enumerate(tiles):
-            core_ref[2 * pair + place // a_count, place % a_count] = tile
+        leaving[f].start()
+    for copy in leaving:
+        copy.wait()
 
 
 def z_plan(fields, factor_x, factor_y):
@@ -361,15 +385,17 @@
     def array(shape, dtype=f32):
         return jax.ShapeDtypeStruct(shape, dtype)
 
-    def call(kernel, name, outs, scratch, operands, space=vmem, limit=48 * 1024 * 1024):
+    def call(
+        kernel, name, outs, scratch, operands, space=vmem, out_spaces=None, limit=32 * 1024 * 1024, cost=10**9
+    ):
         return pl.pallas_call(
             kernel,
             out_shape=tuple(outs),
             in_specs=[space] * len(operands),
-            out_specs=(vmem,) * len(outs),
+            out_specs=out_spaces or (vmem,) * len(outs),
             scratch_shapes=scratch,
             compiler_params=pltpu.CompilerParams(vmem_limit_bytes=limit),
-            cost_estimate=pl.CostEstimate(flops=10**9, bytes_accessed=0, transcendentals=0),
+            cost_estimate=pl.CostEstimate(flops=cost, bytes_accessed=0, transcendentals=0),
             name=name,
         )(*operands)
 
@@ -392,38 +418,37 @@
         "pack",
         [array((pairs, 2, 2 * n_f + 1, HALF, n_z))],
         [
+            pltpu.VMEM((pairs, 2, 2 * n_f + 1, HALF, n_z), f32),
             pltpu.VMEM(flat, f32),
             pltpu.VMEM(factor_x.shape, f32),
             pltpu.VMEM(factor_y.shape, f32),
             pltpu.SemaphoreType.DMA((n_f + 2,)),
+            pltpu.SemaphoreType.DMA((n_f + 1,)),
         ],
         (fields.reshape(flat), factor_x, factor_y),
-        hbm,
-        None,
+        space=hbm,
+        out_spaces=(hbm,),
+        limit=None,
     )
     planes = swap(packed, 2 * n_f + 1).reshape(count_x, count_y, 2 * n_f + 1, HALF, n_z)
     extended = pltpu.VMEM((count_y, n_f, SUBLANES + 6, SUBLANES, LANES), f32)
     rows = SUBLANES * SUBLANES + HALF * SUBLANES
-    held, spread, *columns = call(
+    sent, spread, *columns = call(
         functools.partial(main_kernel, n_f, count_x, count_y, rank, rescale),
         "sections",
         [
-            array((n_f, count_y, SUBLANES, SUBLANES, LANES)),
+            array((count_x, count_y, 2 * n_f, HALF, n_z)),
             array((2, n_f * LANES, LANES), jnp.bfloat16),
         ]
         + [array((rows, LANES))] * count_y,
-        [extended] * 3 + [pltpu.VMEM((count_y, rows, LANES), f32)],
+        [extended] * 3
+        + [
+            pltpu.VMEM((n_f, count_y, SUBLANES, SUBLANES, LANES), f32),
+            pltpu.VMEM((count_y, rows, LANES), f32),
+        ],
         (planes,),
     )
     columns = pass_on(columns, "gy")
-    (sent,) = call(
-        functools.partial(send_kernel, count_x),
-        "send",
-        [array((count_x, count_y, 2 * n_f, HALF, n_z))],
-        [],
-        (held,),
-    )
-    sent, columns = lax.optimization_barrier((sent, columns))
     sent = swap(sent, 2 * n_f).reshape(pairs, 2, 2 * n_f, HALF, n_z)
     rows = (n_f * count_y + n_f // 2) * SUBLANES
     blocks = call(
@@ -435,17 +460,30 @@
             pltpu.VMEM((count_x, rows, LANES), f32),
         ],
         (spread, *columns),
+        cost=20000000000,
     )
     blocks = pass_on(blocks, "gx")
     (advanced,) = call(
-        functools.partial(advanced_kernel, block_x, block_y), "advanced", [array(flat)], [], (sent,)
+        functools.partial(advanced_kernel, block_x, block_y),
+        "advanced",
+        [array(flat)],
+        [pltpu.VMEM(flat, f32), pltpu.SemaphoreType.DMA((n_f,))],
+        (sent,),
+        out_spaces=(hbm,),
     )
     rebuilt, core = call(
         functools.partial(rebuilt_kernel, block_x, block_y, count_x, count_y),
         "rebuilt",
         [array(flat), array((n_f, rank // count_x, rank // count_y, n_z))],
-        [pltpu.VMEM((count_x, rows, LANES), f32)],
+        [
+            pltpu.VMEM((count_x, rows, LANES), f32),
+            pltpu.VMEM(flat, f32),
+            pltpu.VMEM((n_f, rank // count_x, rank // count_y, n_z), f32),
+            pltpu.SemaphoreType.DMA((n_f + 1,)),
+        ],
         tuple(blocks),
+        out_spaces=(hbm, hbm),
+        cost=1000000000,
     )
     return advanced.reshape(fields.shape), core, rebuilt.reshape(fields.shape)
 

time: 57.4 us -> 54.2 us (0.944)
  starting transfers between devices: 16.3 us -> 14.2 us
  Pallas kernels: 9.11 us -> 8.52 us
    all_to_all x1, starting transfers between devices: 5.69 us -> 3.63 us  [swap(): return lax.all_to_all(blocks, ('gx', 'gy'), 0, 0, tiled=True)]
    pallas_call x6 -> x5, Pallas kernels: 9.11 us -> 8.52 us  [call(): pl.pallas_call(kernel, out_shape=tuple(outs), in_specs=[space] * len(oper...]
  transfers between devices with their start and end apart: 11 -> 11, of which waited for: 6 -> 5; matrix products, arithmetic and copies ran while one was open for 0% -> 0% of each run, Pallas kernels for 3% -> 3%
where the time goes in v5:
time: 54.2 us; the launch traced here: 53.9 us
  blocking collectives  23.8 us (44%)
  starting transfers between devices  14.2 us (26%)
  Pallas kernels  8.52 us (16%)
  waiting for transfers between devices  6.71 us (12%)
  between operations  0.7 us (1%)
    all_to_all x1, blocking collectives, swap(): return lax.all_to_all(blocks, ('gx', 'gy'), 0, 0, tiled=True)  23.8 us
    ppermute x10, starting transfers between devices, pass_on(): lax.ppermute(block, axis, [(i, (i + k) % count) for i in range(count)])  10.5 us
    pallas_call x5, Pallas kernels, call(): pl.pallas_call(kernel, out_shape=tuple(outs), in_specs=[space] * len(oper...  8.52 us
    ppermute x10, waiting for transfers between devices, pass_on(): lax.ppermute(block, axis, [(i, (i + k) % count) for i in range(count)])  6.71 us
    all_to_all x1, starting transfers between devices, swap(): return lax.all_to_all(blocks, ('gx', 'gy'), 0, 0, tiled=True)  3.63 us
  transfers between devices with their start and end apart: 11, of which 5 were waited for; matrix products, arithmetic and copies ran while one was open for 0% of the time, Pallas kernels for 3%

profile of v5, /device:TPU:1, one launch (start us, length us, event | category | flops | bytes accessed | tf_op | source)
XLA Modules:
  0.0 53.9 jit_solution(16607903675349748686)
XLA Ops:
  0.6 2.1 %pack.1 = f32[16,2,9,4,128]{4,3,2,1,0:T(4,128)} custom-call(f32[4,256,128]{2,1,0:T(8,128)} %bitcast.10, f32[16,32]{1,0:T(8,128)} %factor_x_hbm.1, f32[16,32]{1,0:T(8,128)} %factor_y_hbm.1), custom_call_target="tpu_custom_call" | custom-call | flops 1000000000 | tf_op jit(solution)/shard_map/pack/pallas_call | solution.py:391
  2.8 23.8 %all_to_all.10 = f32[32,9,4,128]{3,2,1,0:T(4,128)S(1)} all-to-all(f32[32,9,4,128]{3,2,1,0:T(4,128)} %bitcast.9), channel_id=1, replica_groups=mesh['gx'=8,'gy'=4] {'gx','gy'}, dimensions={0} | all-to-all | bytes 1179648 | tf_op jit(solution)/shard_map/all_to_all | solution.py:404
  26.6 3.6 %sections.1 = (f32[8,4,8,4,128]{4,3,2,1,0:T(4,128)}, bf16[2,512,128]{2,1,0:T(8,128)(2,1)S(1)}, f32[96,128]{1,0:T(8,128)S(1)}, f32[96,128]{1,0:T(8,128)S(1)}, f32...) custom-call(f32[8,4,9,4,128]{4,3,2,1,0:T(4,128)S(1)} %bitcast.7), custom_call_target="tpu_custom_call" | custom-call | flops 1000000000 | tf_op jit(solution)/shard_map/sections/pallas_call | solution.py:391
  30.2 0.0 collective-permute-start
  30.2 1.2 %collective-permute-start.1 = (f32[96,128]{1,0:T(8,128)S(1)}, f32[96,128]{1,0:T(8,128)S(1)}, u32[]{:S(2)}, u32[]{:S(2)}) collective-permute-start(f32[96,128]{1,0:T(8,128)S(1)} %get-tuple-element.23), channel_id=1, source_target_pairs={{0,2},{1,3},{2,0},{3,1},{4,6},{5,7},{6,4},{7,5},{8,10},{9,11},{10,... | collective-permute-start | bytes 147464 | tf_op jit(solution)/shard_map/ppermute | solution.py:409
  31.4 2.1 %collective-permute-start.2 = (f32[96,128]{1,0:T(8,128)S(1)}, f32[96,128]{1,0:T(8,128)S(1)}, u32[]{:S(2)}, u32[]{:S(2)}) collective-permute-start(f32[96,128]{1,0:T(8,128)S(1)} %get-tuple-element.24), channel_id=1, source_target_pairs={{0,3},{1,0},{2,1},{3,2},{4,7},{5,4},{6,5},{7,6},{8,11},{9,8},{10,9... | collective-permute-start | bytes 147464 | tf_op jit(solution)/shard_map/ppermute | solution.py:409
  33.5 3.6 %all-to-all-start.1 = ((f32[32,8,4,128]{3,2,1,0:T(4,128)}), f32[32,8,4,128]{3,2,1,0:T(4,128)S(1)}, u32[]{:S(2)}, u32[]{:S(2)}) async-start(f32[32,8,4,128]{3,2,1,0:T(4,128)} %bitcast.3), calls=%async_computation.1 | async-start | bytes 1048576 | tf_op jit(solution)/shard_map/all_to_all | solution.py:404
  37.1 0.0 collective-permute-done.refs_1_
  37.1 0.0 collective-permute-done.1.refs_2_
  37.1 0.0 collective-permute-done.2.refs_3_
  37.1 0.7 %expand.1 = (f32[144,128]{1,0:T(8,128)S(1)}, f32[144,128]{1,0:T(8,128)S(1)}, f32[144,128]{1,0:T(8,128)S(1)}, f32[144,128]{1,0:T(8,128)S(1)}, f32[144,128]{1,0:T(...) custom-call(bf16[2,512,128]{2,1,0:T(8,128)(2,1)S(1)} %get-tuple-element.20.spread_ref, ...), custom_call_target="tpu_custom_call" | custom-call | flops 20000000000 | tf_op jit(solution)/shard_map/expand/pallas_call | solution.py:391
  37.8 1.8 %collective-permute-start.3 = (f32[144,128]{1,0:T(8,128)S(1)}, f32[144,128]{1,0:T(8,128)S(1)}, u32[]{:S(2)}, u32[]{:S(2)}) collective-permute-start(f32[144,128]{1,0:T(8,128)S(1)} %get-tuple-element.26), channel_id=1, source_target_pairs={{0,4},{4,8},{8,12},{12,16},{16,20},{20,24},{24,28},{28,0},{1,5},{5... | collective-permute-start | bytes 221192 | tf_op jit(solution)/shard_map/ppermute | solution.py:409
  39.7 1.2 %collective-permute-start.4 = (f32[144,128]{1,0:T(8,128)S(1)}, f32[144,128]{1,0:T(8,128)S(1)}, u32[]{:S(2)}, u32[]{:S(2)}) collective-permute-start(f32[144,128]{1,0:T(8,128)S(1)} %get-tuple-element.27), channel_id=1, source_target_pairs={{0,8},{4,12},{8,16},{12,20},{16,24},{20,28},{24,0},{28,4},{1,9},{5... | collective-permute-start | bytes 221192 | tf_op jit(solution)/shard_map/ppermute | solution.py:409
  40.9 0.3 collective-permute-start.5
  41.1 0.4 collective-permute-start.6
  41.5 2.7 %collective-permute-start.7 = (f32[144,128]{1,0:T(8,128)S(1)}, f32[144,128]{1,0:T(8,128)S(1)}, u32[]{:S(2)}, u32[]{:S(2)}) collective-permute-start(f32[144,128]{1,0:T(8,128)S(1)} %get-tuple-element.30), channel_id=1, source_target_pairs={{0,20},{4,24},{8,28},{12,0},{16,4},{20,8},{24,12},{28,16},{1,21},{... | collective-permute-start | bytes 221192 | tf_op jit(solution)/shard_map/ppermute | solution.py:409
  44.2 0.0 collective-permute-done.3.refs_1_
  44.2 0.9 %collective-permute-start.8 = (f32[144,128]{1,0:T(8,128)S(1)}, f32[144,128]{1,0:T(8,128)S(1)}, u32[]{:S(2)}, u32[]{:S(2)}) collective-permute-start(f32[144,128]{1,0:T(8,128)S(1)} %get-tuple-element.31), channel_id=1, source_target_pairs={{0,24},{4,28},{8,0},{12,4},{16,8},{20,12},{24,16},{28,20},{1,25},{... | collective-permute-start | bytes 221192 | tf_op jit(solution)/shard_map/ppermute | solution.py:409
  45.1 2.6 %collective-permute-done.4.refs_2_ = f32[144,128]{1,0:T(8,128)S(1)} collective-permute-done((f32[144,128]{1,0:T(8,128)S(1)}, f32[144,128]{1,0:T(8,128)S(1)}, u32[]{:S(2)}, u32[]{:S(2)}) %collective-permute-start.4) | collective-permute-done | bytes 73760 | tf_op jit(solution)/shard_map/ppermute | solution.py:409
  47.7 0.0 collective-permute-start.9
  47.7 0.4 collective-permute-done.5.refs_3_
  48.1 3.5 %collective-permute-done.6.refs_4_ = f32[144,128]{1,0:T(8,128)S(1)} collective-permute-done((f32[144,128]{1,0:T(8,128)S(1)}, f32[144,128]{1,0:T(8,128)S(1)}, u32[]{:S(2)}, u32[]{:S(2)}) %collective-permute-start.6) | collective-permute-done | bytes 73760 | tf_op jit(solution)/shard_map/ppermute | solution.py:409
  51.6 0.1 collective-permute-done.7.refs_5_
  51.7 0.0 collective-permute-done.8.refs_6_
  51.7 0.1 collective-permute-done.9.refs_7_
  51.8 1.1 %rebuilt.1 = (f32[4,256,128]{2,1,0:T(8,128)}, f32[4,4,8,128]{3,2,1,0:T(8,128)}) custom-call(f32[144,128]{1,0:T(8,128)S(1)} %get-tuple-element.25.refs_0_, f32[144,128]{1,0:T(8,128)S(1)} %collective-permute-done.3.refs_1_, f32[144,128]{1,0:T(8,128)S(1)} %collective-permute-done.4.refs_2_, f32[144,128]{1,0:T(8,128)S(1)} %collective-permute-done.5.refs_3_, ...), custom_call_target="tpu_custom_call" | custom-call | flops 1000000000 | tf_op jit(solution)/shard_map/rebuilt/pallas_call | solution.py:391
  52.9 0.0 all-to-all-done.1
  52.9 0.9 %advanced.1 = f32[4,256,128]{2,1,0:T(8,128)} custom-call(f32[16,2,8,4,128]{4,3,2,1,0:T(4,128)S(1)} %bitcast.8), custom_call_target="tpu_custom_call" | custom-call | flops 1000000000 | tf_op jit(solution)/shard_map/advanced/pallas_call | solution.py:391
Async XLA Ops:
  30.2 6.9 %collective-permute-start = (f32[96,128]{1,0:T(8,128)S(1)}, f32[96,128]{1,0:T(8,128)S(1)}, u32[]{:S(2)}, u32[]{:S(2)}) collective-permute-start(f32[96,128]{1,0:T(8,128)S(1)} %get-tuple-element.22), channel_id=1, source_target_pairs={{0,1},{1,2},{2,3},{3,0},{4,5},{5,6},{6,7},{7,4},{8,9},{9,10},{10,1... | collective-permute-start | bytes 147464 | tf_op jit(solution)/shard_map/ppermute | solution.py:409
  30.2 6.9 %collective-permute-start.1 = (f32[96,128]{1,0:T(8,128)S(1)}, f32[96,128]{1,0:T(8,128)S(1)}, u32[]{:S(2)}, u32[]{:S(2)}) collective-permute-start(f32[96,128]{1,0:T(8,128)S(1)} %get-tuple-element.23), channel_id=1, source_target_pairs={{0,2},{1,3},{2,0},{3,1},{4,6},{5,7},{6,4},{7,5},{8,10},{9,11},{10,... | collective-permute-start | bytes 147464 | tf_op jit(solution)/shard_map/ppermute | solution.py:409
  31.4 5.8 %collective-permute-start.2 = (f32[96,128]{1,0:T(8,128)S(1)}, f32[96,128]{1,0:T(8,128)S(1)}, u32[]{:S(2)}, u32[]{:S(2)}) collective-permute-start(f32[96,128]{1,0:T(8,128)S(1)} %get-tuple-element.24), channel_id=1, source_target_pairs={{0,3},{1,0},{2,1},{3,2},{4,7},{5,4},{6,5},{7,6},{8,11},{9,8},{10,9... | collective-permute-start | bytes 147464 | tf_op jit(solution)/shard_map/ppermute | solution.py:409
  33.5 19.5 %all-to-all-start.1 = ((f32[32,8,4,128]{3,2,1,0:T(4,128)}), f32[32,8,4,128]{3,2,1,0:T(4,128)S(1)}, u32[]{:S(2)}, u32[]{:S(2)}) async-start(f32[32,8,4,128]{3,2,1,0:T(4,128)} %bitcast.3), calls=%async_computation.1 | async-start | bytes 1048576 | tf_op jit(solution)/shard_map/all_to_all | solution.py:404
  37.8 6.4 %collective-permute-start.3 = (f32[144,128]{1,0:T(8,128)S(1)}, f32[144,128]{1,0:T(8,128)S(1)}, u32[]{:S(2)}, u32[]{:S(2)}) collective-permute-start(f32[144,128]{1,0:T(8,128)S(1)} %get-tuple-element.26), channel_id=1, source_target_pairs={{0,4},{4,8},{8,12},{12,16},{16,20},{20,24},{24,28},{28,0},{1,5},{5... | collective-permute-start | bytes 221192 | tf_op jit(solution)/shard_map/ppermute | solution.py:409
  39.7 8.0 %collective-permute-start.4 = (f32[144,128]{1,0:T(8,128)S(1)}, f32[144,128]{1,0:T(8,128)S(1)}, u32[]{:S(2)}, u32[]{:S(2)}) collective-permute-start(f32[144,128]{1,0:T(8,128)S(1)} %get-tuple-element.27), channel_id=1, source_target_pairs={{0,8},{4,12},{8,16},{12,20},{16,24},{20,28},{24,0},{28,4},{1,9},{5... | collective-permute-start | bytes 221192 | tf_op jit(solution)/shard_map/ppermute | solution.py:409
  40.9 7.2 %collective-permute-start.5 = (f32[144,128]{1,0:T(8,128)S(1)}, f32[144,128]{1,0:T(8,128)S(1)}, u32[]{:S(2)}, u32[]{:S(2)}) collective-permute-start(f32[144,128]{1,0:T(8,128)S(1)} %get-tuple-element.28), channel_id=1, source_target_pairs={{0,12},{4,16},{8,20},{12,24},{16,28},{20,0},{24,4},{28,8},{1,13},{... | collective-permute-start | bytes 221192 | tf_op jit(solution)/shard_map/ppermute | solution.py:409
  41.1 10.5 %collective-permute-start.6 = (f32[144,128]{1,0:T(8,128)S(1)}, f32[144,128]{1,0:T(8,128)S(1)}, u32[]{:S(2)}, u32[]{:S(2)}) collective-permute-start(f32[144,128]{1,0:T(8,128)S(1)} %get-tuple-element.29), channel_id=1, source_target_pairs={{0,16},{4,20},{8,24},{12,28},{16,0},{20,4},{24,8},{28,12},{1,17},{... | collective-permute-start | bytes 221192 | tf_op jit(solution)/shard_map/ppermute | solution.py:409
  41.5 10.2 %collective-permute-start.7 = (f32[144,128]{1,0:T(8,128)S(1)}, f32[144,128]{1,0:T(8,128)S(1)}, u32[]{:S(2)}, u32[]{:S(2)}) collective-permute-start(f32[144,128]{1,0:T(8,128)S(1)} %get-tuple-element.30), channel_id=1, source_target_pairs={{0,20},{4,24},{8,28},{12,0},{16,4},{20,8},{24,12},{28,16},{1,21},{... | collective-permute-start | bytes 221192 | tf_op jit(solution)/shard_map/ppermute | solution.py:409
  44.2 7.5 %collective-permute-start.8 = (f32[144,128]{1,0:T(8,128)S(1)}, f32[144,128]{1,0:T(8,128)S(1)}, u32[]{:S(2)}, u32[]{:S(2)}) collective-permute-start(f32[144,128]{1,0:T(8,128)S(1)} %get-tuple-element.31), channel_id=1, source_target_pairs={{0,24},{4,28},{8,0},{12,4},{16,8},{20,12},{24,16},{28,20},{1,25},{... | collective-permute-start | bytes 221192 | tf_op jit(solution)/shard_map/ppermute | solution.py:409
  47.7 4.1 %collective-permute-start.9 = (f32[144,128]{1,0:T(8,128)S(1)}, f32[144,128]{1,0:T(8,128)S(1)}, u32[]{:S(2)}, u32[]{:S(2)}) collective-permute-start(f32[144,128]{1,0:T(8,128)S(1)} %get-tuple-element.32), channel_id=1, source_target_pairs={{0,28},{4,0},{8,4},{12,8},{16,12},{20,16},{24,20},{28,24},{1,29},{... | collective-permute-start | bytes 221192 | tf_op jit(solution)/shard_map/ppermute | solution.py:409

commit v6 on v5

--- a/solution.py
+++ b/solution.py
@@ -68,9 +68,7 @@
     return blocks
 
 
-def pack_kernel(
-    fields_hbm, factor_x_hbm, factor_y_hbm, out_hbm, out_ref, fields_ref, x_ref, y_ref, sems, out_sems
-):
+def pack_kernel(fields_hbm, factor_x_hbm, factor_y_hbm, out_ref, fields_ref, x_ref, y_ref, sems):
     n_f, rows, _ = fields_ref.shape
     block_x = x_ref.shape[0]
     block_y = rows // block_x
@@ -82,12 +80,6 @@
     copies.append(pltpu.make_async_copy(factor_y_hbm, y_ref, sems.at[n_f + 1]))
     for copy in copies:
         copy.start()
-
-    def leave(f, tiles):
-        at = (slice(None), slice(None), pl.ds(2 * f, tiles))
-        return pltpu.make_async_copy(out_ref.at[at], out_hbm.at[at], out_sems.at[f])
-
-    leaving = [leave(f, 2) for f in range(n_f)] + [leave(n_f, 1)]
     for f in range(n_f):
         copies[f].wait()
         for octet in range(2):
@@ -101,7 +93,6 @@
             turned = matrix.T.reshape(tiles, SUBLANES, LANES)
             out_ref[:, 0, 2 * f + octet] = turned[:, :HALF]
             out_ref[:, 1, 2 * f + octet] = turned[:, HALF:]
-        leaving[f].start()
     copies[n_f].wait()
     copies[n_f + 1].wait()
     part_x = lax.axis_index("gy")
@@ -110,9 +101,6 @@
     own_y = y_ref[pl.ds(part_y * HALF, HALF), :]
     factors = jnp.concatenate([own_x, own_y, own_y, own_y], axis=1)
     out_ref[:, :, 2 * n_f] = jnp.broadcast_to(factors[None, None], (tiles, 2, HALF, LANES))
-    leaving[n_f].start()
-    for copy in leaving:
-        copy.wait()
 
 
 def split(value):
@@ -130,10 +118,10 @@
 
 
 def main_kernel(
-    n_f, count_x, count_y, rank, rescale, in_ref, sent_ref, spread_ref, *refs
+    n_f, count_x, count_y, rank, rescale, in_ref, sent_hbm, spread_ref, *refs
 ):
     column_refs = refs[:count_y]
-    ext_a, ext_b, ext_c, adv, staged = refs[count_y:]
+    ext_a, ext_b, ext_c, adv, staged, sent_ref, sent_sem = refs[count_y:]
     margin = 3
     inner = pl.ds(margin, SUBLANES)
     lower = lax.broadcasted_iota(jnp.int32, (margin, SUBLANES, LANES), 1) < HALF
@@ -231,46 +219,52 @@
     section(ext_b, 0.25 * TIME_STEP, second)
     fill_margins(ext_c)
     section(ext_c, 2.0 / 3.0 * TIME_STEP, third)
-
-    plane = count_y * SUBLANES * SUBLANES
-    held = in_ref[:, :, 2 * n_f].reshape(LANES, LANES)
-    held_x = split(held)
-    held_y = split(jnp.where(col < rank, pltpu.roll(held, LANES - rank, 1), held))
-    picks = (row == col // n_f).astype(jnp.bfloat16)
-    spread_x = [mul(part, picks) for part in held_x]
-    weights_x = [
-        jnp.concatenate(
-            [jnp.where(col % n_f == f, part, 0.0).astype(jnp.bfloat16) for f in range(n_f)], axis=0
-        )
-        for part in spread_x
-    ]
-    r = lax.broadcasted_iota(jnp.int32, (plane, LANES), 0)
-    c = lax.broadcasted_iota(jnp.int32, (plane, LANES), 1)
-    from_s, from_y = r // (SUBLANES * SUBLANES), (r // HALF) % 2 * SUBLANES + (r // SUBLANES) % SUBLANES
-    block_x = LANES // count_x
-    held_at = from_y // HALF * block_x + from_s * HALF + from_y % HALF
-    picks = (held_at == c).astype(jnp.bfloat16)
-    same_z = r % HALF == c // rank
-    weights_y = [jnp.where(same_z, mul(picks, part), 0.0).astype(jnp.bfloat16) for part in held_y]
-
-    def by_x(value):
-        return jnp.concatenate([value[f].reshape(plane, LANES) for f in range(n_f)], axis=1)
-
-    partial = mul_split(split(by_x(adv)), weights_x)
-    core = mul_split(weights_y, split(partial), ((0,), (0,)))
-    columns = rescale * mul_split(weights_y, split(core))
-    for part in range(2):
-        spread_ref[part] = weights_x[part]
-
-    block = plane // count_y
-    for s in range(count_y):
-        staged[s, 0:block] = columns[s * block : (s + 1) * block]
-        for z in range(HALF):
-            at = z * rank + s * SUBLANES
-            staged[s, block + z * SUBLANES : block + (z + 1) * SUBLANES] = core[at : at + SUBLANES]
-    own = lax.axis_index("gy")
-    for k, ref in enumerate(column_refs):
-        ref[...] = staged[lax.rem(own + k, count_y)]
+    sent = pltpu.make_async_copy(sent_ref, sent_hbm, sent_sem)
+    sent.start()
+
+    @pl.when(lax.axis_index("gy") >= 0)
+    def tucker():
+        plane = count_y * SUBLANES * SUBLANES
+        held = in_ref[:, :, 2 * n_f].reshape(LANES, LANES)
+        held_x = split(held)
+        held_y = split(jnp.where(col < rank, pltpu.roll(held, LANES - rank, 1), held))
+        picks = (row == col // n_f).astype(jnp.bfloat16)
+        spread_x = [mul(part, picks) for part in held_x]
+        weights_x = [
+            jnp.concatenate(
+                [jnp.where(col % n_f == f, part, 0.0).astype(jnp.bfloat16) for f in range(n_f)], axis=0
+            )
+            for part in spread_x
+        ]
+        r = lax.broadcasted_iota(jnp.int32, (plane, LANES), 0)
+        c = lax.broadcasted_iota(jnp.int32, (plane, LANES), 1)
+        from_s, from_y = r // (SUBLANES * SUBLANES), (r // HALF) % 2 * SUBLANES + (r // SUBLANES) % SUBLANES
+        block_x = LANES // count_x
+        held_at = from_y // HALF * block_x + from_s * HALF + from_y % HALF
+        picks = (held_at == c).astype(jnp.bfloat16)
+        same_z = r % HALF == c // rank
+        weights_y = [jnp.where(same_z, mul(picks, part), 0.0).astype(jnp.bfloat16) for part in held_y]
+
+        def by_x(value):
+            return jnp.concatenate([value[f].reshape(plane, LANES) for f in range(n_f)], axis=1)
+
+        partial = mul_split(split(by_x(adv)), weights_x)
+        core = mul_split(weights_y, split(partial), ((0,), (0,)))
+        columns = rescale * mul_split(weights_y, split(core))
+        for part in range(2):
+            spread_ref[part] = weights_x[part]
+
+        block = plane // count_y
+        for s in range(count_y):
+            staged[s, 0:block] = columns[s * block : (s + 1) * block]
+            for z in range(HALF):
+                at = z * rank + s * SUBLANES
+                staged[s, block + z * SUBLANES : block + (z + 1) * SUBLANES] = core[at : at + SUBLANES]
+        own = lax.axis_index("gy")
+        for k, ref in enumerate(column_refs):
+            ref[...] = staged[lax.rem(own + k, count_y)]
+
+    sent.wait()
 
 
 def expand_kernel(n_f, count_x, count_y, spread_ref, *refs):
@@ -418,17 +412,16 @@
         "pack",
         [array((pairs, 2, 2 * n_f + 1, HALF, n_z))],
         [
-            pltpu.VMEM((pairs, 2, 2 * n_f + 1, HALF, n_z), f32),
             pltpu.VMEM(flat, f32),
             pltpu.VMEM(factor_x.shape, f32),
             pltpu.VMEM(factor_y.shape, f32),
             pltpu.SemaphoreType.DMA((n_f + 2,)),
-            pltpu.SemaphoreType.DMA((n_f + 1,)),
         ],
-        (fields.reshape(flat), factor_x, factor_y),
+        tuple(
+            pltpu.with_memory_space_constraint(v, pltpu.HBM)
+            for v in (fields.reshape(flat), factor_x, factor_y)
+        ),
         space=hbm,
-        out_spaces=(hbm,),
-        limit=None,
     )
     planes = swap(packed, 2 * n_f + 1).reshape(count_x, count_y, 2 * n_f + 1, HALF, n_z)
     extended = pltpu.VMEM((count_y, n_f, SUBLANES + 6, SUBLANES, LANES), f32)
@@ -445,8 +438,11 @@
         + [
             pltpu.VMEM((n_f, count_y, SUBLANES, SUBLANES, LANES), f32),
             pltpu.VMEM((count_y, rows, LANES), f32),
+            pltpu.VMEM((count_x, count_y, 2 * n_f, HALF, n_z), f32),
+            pltpu.SemaphoreType.DMA,
         ],
         (planes,),
+        out_spaces=(hbm,) + (vmem,) * (1 + count_y),
     )
     columns = pass_on(columns, "gy")
     sent = swap(sent, 2 * n_f).reshape(pairs, 2, 2 * n_f, HALF, n_z)

time: 54.2 us -> 52.4 us (0.967)
  Pallas kernels: 8.52 us -> 6.91 us
    pallas_call x5, Pallas kernels: 8.52 us -> 6.91 us  [call(): pl.pallas_call(kernel, out_shape=tuple(outs), in_specs=[space] * len(oper...]
where the time goes in v6:
time: 52.4 us; the launch traced here: 52.1 us
  blocking collectives  23.6 us (45%)
  starting transfers between devices  14.2 us (27%)
  Pallas kernels  6.91 us (13%)
  waiting for transfers between devices  6.72 us (13%)
  between operations  0.72 us (1%)
    all_to_all x1, blocking collectives, swap(): return lax.all_to_all(blocks, ('gx', 'gy'), 0, 0, tiled=True)  23.6 us
    ppermute x10, starting transfers between devices, pass_on(): lax.ppermute(block, axis, [(i, (i + k) % count) for i in range(count)])  10.6 us
    pallas_call x5, Pallas kernels, call(): pl.pallas_call(kernel, out_shape=tuple(outs), in_specs=[space] * len(oper...  6.91 us
    ppermute x10, waiting for transfers between devices, pass_on(): lax.ppermute(block, axis, [(i, (i + k) % count) for i in range(count)])  6.72 us
    all_to_all x1, starting transfers between devices, swap(): return lax.all_to_all(blocks, ('gx', 'gy'), 0, 0, tiled=True)  3.63 us
  transfers between devices with their start and end apart: 11, of which 5 were waited for; matrix products, arithmetic and copies ran while one was open for 0% of the time, Pallas kernels for 3%

profile of v6, /device:TPU:1, one launch (start us, length us, event | category | flops | bytes accessed | tf_op | source)
XLA Modules:
  0.0 52.1 jit_solution(11222095141665152239)
XLA Ops:
  0.6 1.5 %pack.1 = f32[16,2,9,4,128]{4,3,2,1,0:T(4,128)S(1)} custom-call(f32[4,256,128]{2,1,0:T(8,128)} %bitcast.10, f32[16,32]{1,0:T(8,128)} %factor_x_hbm.1, f32[16,32]{1,0:T(8,128)} %factor_y_hbm.1), custom_call_target="tpu_custom_call" | custom-call | flops 1000000000 | tf_op jit(solution)/shard_map/pack/pallas_call | solution.py:385
  2.1 23.6 %all_to_all.10 = f32[32,9,4,128]{3,2,1,0:T(4,128)S(1)} all-to-all(f32[32,9,4,128]{3,2,1,0:T(4,128)S(1)} %bitcast.8), channel_id=1, replica_groups=mesh['gx'=8,'gy'=4] {'gx','gy'}, dimensions={0} | all-to-all | bytes 1179648 | tf_op jit(solution)/shard_map/all_to_all | solution.py:398
  25.7 2.7 %sections.1 = (f32[8,4,8,4,128]{4,3,2,1,0:T(4,128)}, bf16[2,512,128]{2,1,0:T(8,128)(2,1)S(1)}, f32[96,128]{1,0:T(8,128)S(1)}, f32[96,128]{1,0:T(8,128)S(1)}, f32...) custom-call(f32[8,4,9,4,128]{4,3,2,1,0:T(4,128)S(1)} %bitcast.7), custom_call_target="tpu_custom_call" | custom-call | flops 1000000000 | tf_op jit(solution)/shard_map/sections/pallas_call | solution.py:385
  28.4 0.1 collective-permute-start
  28.5 1.2 %collective-permute-start.1 = (f32[96,128]{1,0:T(8,128)S(1)}, f32[96,128]{1,0:T(8,128)S(1)}, u32[]{:S(2)}, u32[]{:S(2)}) collective-permute-start(f32[96,128]{1,0:T(8,128)S(1)} %get-tuple-element.23), channel_id=1, source_target_pairs={{0,2},{1,3},{2,0},{3,1},{4,6},{5,7},{6,4},{7,5},{8,10},{9,11},{10,... | collective-permute-start | bytes 147464 | tf_op jit(solution)/shard_map/ppermute | solution.py:403
  29.6 2.1 %collective-permute-start.2 = (f32[96,128]{1,0:T(8,128)S(1)}, f32[96,128]{1,0:T(8,128)S(1)}, u32[]{:S(2)}, u32[]{:S(2)}) collective-permute-start(f32[96,128]{1,0:T(8,128)S(1)} %get-tuple-element.24), channel_id=1, source_target_pairs={{0,3},{1,0},{2,1},{3,2},{4,7},{5,4},{6,5},{7,6},{8,11},{9,8},{10,9... | collective-permute-start | bytes 147464 | tf_op jit(solution)/shard_map/ppermute | solution.py:403
  31.7 3.6 %all-to-all-start.1 = ((f32[32,8,4,128]{3,2,1,0:T(4,128)}), f32[32,8,4,128]{3,2,1,0:T(4,128)S(1)}, u32[]{:S(2)}, u32[]{:S(2)}) async-start(f32[32,8,4,128]{3,2,1,0:T(4,128)} %bitcast.3), calls=%async_computation.1 | async-start | bytes 1048576 | tf_op jit(solution)/shard_map/all_to_all | solution.py:398
  35.3 0.0 collective-permute-done.refs_1_
  35.4 0.0 collective-permute-done.1.refs_2_
  35.4 0.0 collective-permute-done.2.refs_3_
  35.4 0.7 %expand.1 = (f32[144,128]{1,0:T(8,128)S(1)}, f32[144,128]{1,0:T(8,128)S(1)}, f32[144,128]{1,0:T(8,128)S(1)}, f32[144,128]{1,0:T(8,128)S(1)}, f32[144,128]{1,0:T(...) custom-call(bf16[2,512,128]{2,1,0:T(8,128)(2,1)S(1)} %get-tuple-element.20.spread_ref, ...), custom_call_target="tpu_custom_call" | custom-call | flops 20000000000 | tf_op jit(solution)/shard_map/expand/pallas_call | solution.py:385
  36.1 1.9 %collective-permute-start.3 = (f32[144,128]{1,0:T(8,128)S(1)}, f32[144,128]{1,0:T(8,128)S(1)}, u32[]{:S(2)}, u32[]{:S(2)}) collective-permute-start(f32[144,128]{1,0:T(8,128)S(1)} %get-tuple-element.26), channel_id=1, source_target_pairs={{0,4},{4,8},{8,12},{12,16},{16,20},{20,24},{24,28},{28,0},{1,5},{5... | collective-permute-start | bytes 221192 | tf_op jit(solution)/shard_map/ppermute | solution.py:403
  37.9 1.2 %collective-permute-start.4 = (f32[144,128]{1,0:T(8,128)S(1)}, f32[144,128]{1,0:T(8,128)S(1)}, u32[]{:S(2)}, u32[]{:S(2)}) collective-permute-start(f32[144,128]{1,0:T(8,128)S(1)} %get-tuple-element.27), channel_id=1, source_target_pairs={{0,8},{4,12},{8,16},{12,20},{16,24},{20,28},{24,0},{28,4},{1,9},{5... | collective-permute-start | bytes 221192 | tf_op jit(solution)/shard_map/ppermute | solution.py:403
  39.1 0.2 collective-permute-start.5
  39.4 0.4 collective-permute-start.6
  39.8 2.7 %collective-permute-start.7 = (f32[144,128]{1,0:T(8,128)S(1)}, f32[144,128]{1,0:T(8,128)S(1)}, u32[]{:S(2)}, u32[]{:S(2)}) collective-permute-start(f32[144,128]{1,0:T(8,128)S(1)} %get-tuple-element.30), channel_id=1, source_target_pairs={{0,20},{4,24},{8,28},{12,0},{16,4},{20,8},{24,12},{28,16},{1,21},{... | collective-permute-start | bytes 221192 | tf_op jit(solution)/shard_map/ppermute | solution.py:403
  42.4 0.0 collective-permute-done.3.refs_1_
  42.4 0.9 %collective-permute-start.8 = (f32[144,128]{1,0:T(8,128)S(1)}, f32[144,128]{1,0:T(8,128)S(1)}, u32[]{:S(2)}, u32[]{:S(2)}) collective-permute-start(f32[144,128]{1,0:T(8,128)S(1)} %get-tuple-element.31), channel_id=1, source_target_pairs={{0,24},{4,28},{8,0},{12,4},{16,8},{20,12},{24,16},{28,20},{1,25},{... | collective-permute-start | bytes 221192 | tf_op jit(solution)/shard_map/ppermute | solution.py:403
  43.3 2.6 %collective-permute-done.4.refs_2_ = f32[144,128]{1,0:T(8,128)S(1)} collective-permute-done((f32[144,128]{1,0:T(8,128)S(1)}, f32[144,128]{1,0:T(8,128)S(1)}, u32[]{:S(2)}, u32[]{:S(2)}) %collective-permute-start.4) | collective-permute-done | bytes 73760 | tf_op jit(solution)/shard_map/ppermute | solution.py:403
  45.9 0.0 collective-permute-start.9
  45.9 0.4 collective-permute-done.5.refs_3_
  46.3 3.5 %collective-permute-done.6.refs_4_ = f32[144,128]{1,0:T(8,128)S(1)} collective-permute-done((f32[144,128]{1,0:T(8,128)S(1)}, f32[144,128]{1,0:T(8,128)S(1)}, u32[]{:S(2)}, u32[]{:S(2)}) %collective-permute-start.6) | collective-permute-done | bytes 73760 | tf_op jit(solution)/shard_map/ppermute | solution.py:403
  49.8 0.1 collective-permute-done.7.refs_5_
  50.0 0.0 collective-permute-done.8.refs_6_
  50.0 0.1 collective-permute-done.9.refs_7_
  50.0 1.1 %rebuilt.1 = (f32[4,256,128]{2,1,0:T(8,128)}, f32[4,4,8,128]{3,2,1,0:T(8,128)}) custom-call(f32[144,128]{1,0:T(8,128)S(1)} %get-tuple-element.25.refs_0_, f32[144,128]{1,0:T(8,128)S(1)} %collective-permute-done.3.refs_1_, f32[144,128]{1,0:T(8,128)S(1)} %collective-permute-done.4.refs_2_, f32[144,128]{1,0:T(8,128)S(1)} %collective-permute-done.5.refs_3_, ...), custom_call_target="tpu_custom_call" | custom-call | flops 1000000000 | tf_op jit(solution)/shard_map/rebuilt/pallas_call | solution.py:385
  51.2 0.0 all-to-all-done.1
  51.2 0.9 %advanced.1 = f32[4,256,128]{2,1,0:T(8,128)} custom-call(f32[16,2,8,4,128]{4,3,2,1,0:T(4,128)S(1)} %bitcast.9), custom_call_target="tpu_custom_call" | custom-call | flops 1000000000 | tf_op jit(solution)/shard_map/advanced/pallas_call | solution.py:385
Async XLA Ops:
  28.4 7.0 %collective-permute-start = (f32[96,128]{1,0:T(8,128)S(1)}, f32[96,128]{1,0:T(8,128)S(1)}, u32[]{:S(2)}, u32[]{:S(2)}) collective-permute-start(f32[96,128]{1,0:T(8,128)S(1)} %get-tuple-element.22), channel_id=1, source_target_pairs={{0,1},{1,2},{2,3},{3,0},{4,5},{5,6},{6,7},{7,4},{8,9},{9,10},{10,1... | collective-permute-start | bytes 147464 | tf_op jit(solution)/shard_map/ppermute | solution.py:403
  28.5 6.9 %collective-permute-start.1 = (f32[96,128]{1,0:T(8,128)S(1)}, f32[96,128]{1,0:T(8,128)S(1)}, u32[]{:S(2)}, u32[]{:S(2)}) collective-permute-start(f32[96,128]{1,0:T(8,128)S(1)} %get-tuple-element.23), channel_id=1, source_target_pairs={{0,2},{1,3},{2,0},{3,1},{4,6},{5,7},{6,4},{7,5},{8,10},{9,11},{10,... | collective-permute-start | bytes 147464 | tf_op jit(solution)/shard_map/ppermute | solution.py:403
  29.6 5.8 %collective-permute-start.2 = (f32[96,128]{1,0:T(8,128)S(1)}, f32[96,128]{1,0:T(8,128)S(1)}, u32[]{:S(2)}, u32[]{:S(2)}) collective-permute-start(f32[96,128]{1,0:T(8,128)S(1)} %get-tuple-element.24), channel_id=1, source_target_pairs={{0,3},{1,0},{2,1},{3,2},{4,7},{5,4},{6,5},{7,6},{8,11},{9,8},{10,9... | collective-permute-start | bytes 147464 | tf_op jit(solution)/shard_map/ppermute | solution.py:403
  31.7 19.5 %all-to-all-start.1 = ((f32[32,8,4,128]{3,2,1,0:T(4,128)}), f32[32,8,4,128]{3,2,1,0:T(4,128)S(1)}, u32[]{:S(2)}, u32[]{:S(2)}) async-start(f32[32,8,4,128]{3,2,1,0:T(4,128)} %bitcast.3), calls=%async_computation.1 | async-start | bytes 1048576 | tf_op jit(solution)/shard_map/all_to_all | solution.py:398
  36.1 6.3 %collective-permute-start.3 = (f32[144,128]{1,0:T(8,128)S(1)}, f32[144,128]{1,0:T(8,128)S(1)}, u32[]{:S(2)}, u32[]{:S(2)}) collective-permute-start(f32[144,128]{1,0:T(8,128)S(1)} %get-tuple-element.26), channel_id=1, source_target_pairs={{0,4},{4,8},{8,12},{12,16},{16,20},{20,24},{24,28},{28,0},{1,5},{5... | collective-permute-start | bytes 221192 | tf_op jit(solution)/shard_map/ppermute | solution.py:403
  37.9 8.0 %collective-permute-start.4 = (f32[144,128]{1,0:T(8,128)S(1)}, f32[144,128]{1,0:T(8,128)S(1)}, u32[]{:S(2)}, u32[]{:S(2)}) collective-permute-start(f32[144,128]{1,0:T(8,128)S(1)} %get-tuple-element.27), channel_id=1, source_target_pairs={{0,8},{4,12},{8,16},{12,20},{16,24},{20,28},{24,0},{28,4},{1,9},{5... | collective-permute-start | bytes 221192 | tf_op jit(solution)/shard_map/ppermute | solution.py:403
  39.1 7.2 %collective-permute-start.5 = (f32[144,128]{1,0:T(8,128)S(1)}, f32[144,128]{1,0:T(8,128)S(1)}, u32[]{:S(2)}, u32[]{:S(2)}) collective-permute-start(f32[144,128]{1,0:T(8,128)S(1)} %get-tuple-element.28), channel_id=1, source_target_pairs={{0,12},{4,16},{8,20},{12,24},{16,28},{20,0},{24,4},{28,8},{1,13},{... | collective-permute-start | bytes 221192 | tf_op jit(solution)/shard_map/ppermute | solution.py:403
  39.4 10.5 %collective-permute-start.6 = (f32[144,128]{1,0:T(8,128)S(1)}, f32[144,128]{1,0:T(8,128)S(1)}, u32[]{:S(2)}, u32[]{:S(2)}) collective-permute-start(f32[144,128]{1,0:T(8,128)S(1)} %get-tuple-element.29), channel_id=1, source_target_pairs={{0,16},{4,20},{8,24},{12,28},{16,0},{20,4},{24,8},{28,12},{1,17},{... | collective-permute-start | bytes 221192 | tf_op jit(solution)/shard_map/ppermute | solution.py:403
  39.8 10.2 %collective-permute-start.7 = (f32[144,128]{1,0:T(8,128)S(1)}, f32[144,128]{1,0:T(8,128)S(1)}, u32[]{:S(2)}, u32[]{:S(2)}) collective-permute-start(f32[144,128]{1,0:T(8,128)S(1)} %get-tuple-element.30), channel_id=1, source_target_pairs={{0,20},{4,24},{8,28},{12,0},{16,4},{20,8},{24,12},{28,16},{1,21},{... | collective-permute-start | bytes 221192 | tf_op jit(solution)/shard_map/ppermute | solution.py:403
  42.4 7.6 %collective-permute-start.8 = (f32[144,128]{1,0:T(8,128)S(1)}, f32[144,128]{1,0:T(8,128)S(1)}, u32[]{:S(2)}, u32[]{:S(2)}) collective-permute-start(f32[144,128]{1,0:T(8,128)S(1)} %get-tuple-element.31), channel_id=1, source_target_pairs={{0,24},{4,28},{8,0},{12,4},{16,8},{20,12},{24,16},{28,20},{1,25},{... | collective-permute-start | bytes 221192 | tf_op jit(solution)/shard_map/ppermute | solution.py:403
  45.9 4.1 %collective-permute-start.9 = (f32[144,128]{1,0:T(8,128)S(1)}, f32[144,128]{1,0:T(8,128)S(1)}, u32[]{:S(2)}, u32[]{:S(2)}) collective-permute-start(f32[144,128]{1,0:T(8,128)S(1)} %get-tuple-element.32), channel_id=1, source_target_pairs={{0,28},{4,0},{8,4},{12,8},{16,12},{20,16},{24,20},{28,24},{1,29},{... | collective-permute-start | bytes 221192 | tf_op jit(solution)/shard_map/ppermute | solution.py:403

commit v7 on v6

--- a/solution.py
+++ b/solution.py
@@ -91,16 +91,18 @@
                 axis=0,
             )
             turned = matrix.T.reshape(tiles, SUBLANES, LANES)
-            out_ref[:, 0, 2 * f + octet] = turned[:, :HALF]
-            out_ref[:, 1, 2 * f + octet] = turned[:, HALF:]
+            for part in range(2):
+                at = 2 * (2 * f + octet) + part
+                out_ref[:, 0, at] = turned[:, 2 * part : 2 * part + 2]
+                out_ref[:, 1, at] = turned[:, HALF + 2 * part : HALF + 2 * part + 2]
     copies[n_f].wait()
     copies[n_f + 1].wait()
-    part_x = lax.axis_index("gy")
-    part_y = lax.rem(lax.axis_index("gx"), block_y // HALF)
-    own_x = x_ref[pl.ds(part_x * HALF, HALF), :]
-    own_y = y_ref[pl.ds(part_y * HALF, HALF), :]
-    factors = jnp.concatenate([own_x, own_y, own_y, own_y], axis=1)
-    out_ref[:, :, 2 * n_f] = jnp.broadcast_to(factors[None, None], (tiles, 2, HALF, LANES))
+    own_x = x_ref[pl.ds(lax.axis_index("gy") * HALF, HALF), :]
+    own_y = y_ref[pl.ds(lax.axis_index("gx") * 2, 2), :]
+    row_x = jnp.concatenate([own_x[j : j + 1] for j in range(HALF)], axis=1)
+    row_y = jnp.concatenate([own_y[j % 2 : j % 2 + 1] for j in range(HALF)], axis=1)
+    factors = jnp.concatenate([row_x, row_y], axis=0)
+    out_ref[:, :, 4 * n_f] = jnp.broadcast_to(factors[None, None], (tiles, 2, 2, LANES))
 
 
 def split(value):
@@ -121,7 +123,8 @@
     n_f, count_x, count_y, rank, rescale, in_ref, sent_hbm, spread_ref, *refs
 ):
     column_refs = refs[:count_y]
-    ext_a, ext_b, ext_c, adv, staged, sent_ref, sent_sem = refs[count_y:]
+    ext_a, ext_b, ext_c, adv, staged, sent_ref, sent_sem = refs[count_y : count_y + 7]
+    to_core_ref, project_ref = refs[count_y + 7 :]
     margin = 3
     inner = pl.ds(margin, SUBLANES)
     lower = lax.broadcasted_iota(jnp.int32, (margin, SUBLANES, LANES), 1) < HALF
@@ -194,7 +197,7 @@
     def arrive(s):
         for f in range(n_f):
             got = [
-                in_ref[i, s, 2 * f : 2 * f + 2].reshape(SUBLANES, LANES) for i in range(count_x)
+                in_ref[i, s, 4 * f : 4 * f + 4].reshape(SUBLANES, LANES) for i in range(count_x)
             ]
             for y, block in enumerate(exchange(got, LANES // SUBLANES)):
                 ext_a[s, f, margin + y] = block
@@ -211,6 +214,38 @@
         parts = exchange([done[y] for y in range(SUBLANES)], LANES // SUBLANES)
         for i, part in enumerate(parts):
             sent_ref[i, s, 2 * f : 2 * f + 2] = part.reshape(2, HALF, LANES)
+
+    plane = count_y * SUBLANES * SUBLANES
+    count = count_x * count_y
+    held = in_ref[:, :, 4 * n_f].reshape(2 * count, LANES)
+    held_at = lax.broadcasted_iota(jnp.int32, (LANES, 2 * count), 1)
+    source = lax.broadcasted_iota(jnp.int32, (LANES, 2 * count), 0) // HALF
+    rows_of = (held_at == 2 * source).astype(jnp.bfloat16)
+    spread_x = [jnp.where(row % HALF == col // rank, mul(rows_of, part), 0.0) for part in split(held)]
+    picks = (row % rank == col // n_f).astype(jnp.bfloat16)
+    spread_x = [mul(part.astype(jnp.bfloat16), picks) for part in spread_x]
+    weights_x = [
+        jnp.concatenate(
+            [jnp.where(col % n_f == f, part, 0.0).astype(jnp.bfloat16) for f in range(n_f)], axis=0
+        )
+        for part in spread_x
+    ]
+    r = lax.broadcasted_iota(jnp.int32, (plane, LANES), 0)
+    c = lax.broadcasted_iota(jnp.int32, (plane, LANES), 1)
+    from_s, from_y = r // (SUBLANES * SUBLANES), (r // HALF) % 2 * SUBLANES + (r // SUBLANES) % SUBLANES
+    held_at = lax.broadcasted_iota(jnp.int32, (plane, 2 * count), 1)
+    source = (from_y // 2 * count_y + from_s)[:, : 2 * count]
+    rows_of = (held_at == 2 * source + 1).astype(jnp.bfloat16)
+    spread_y = [jnp.where(from_y % 2 == c // rank % 2, mul(rows_of, part), 0.0) for part in split(held)]
+    spread_y = [part + pltpu.roll(part, rank, 1) for part in spread_y]
+    same_z = r % HALF == c // rank
+    weights_y = [jnp.where(same_z, part, 0.0).astype(jnp.bfloat16) for part in spread_y]
+    for part in range(2):
+        spread_ref[part] = weights_x[part]
+        to_core_ref[part] = weights_y[part].astype(jnp.float32).T.astype(jnp.bfloat16)
+    projector = split(rescale * mul_split(weights_y, weights_y, ((1,), (1,))))
+    for part in range(2):
+        project_ref[part] = projector[part]
 
     each(arrive)
     fill_margins(ext_a)
@@ -224,35 +259,13 @@
 
     @pl.when(lax.axis_index("gy") >= 0)
     def tucker():
-        plane = count_y * SUBLANES * SUBLANES
-        held = in_ref[:, :, 2 * n_f].reshape(LANES, LANES)
-        held_x = split(held)
-        held_y = split(jnp.where(col < rank, pltpu.roll(held, LANES - rank, 1), held))
-        picks = (row == col // n_f).astype(jnp.bfloat16)
-        spread_x = [mul(part, picks) for part in held_x]
-        weights_x = [
-            jnp.concatenate(
-                [jnp.where(col % n_f == f, part, 0.0).astype(jnp.bfloat16) for f in range(n_f)], axis=0
-            )
-            for part in spread_x
-        ]
-        r = lax.broadcasted_iota(jnp.int32, (plane, LANES), 0)
-        c = lax.broadcasted_iota(jnp.int32, (plane, LANES), 1)
-        from_s, from_y = r // (SUBLANES * SUBLANES), (r // HALF) % 2 * SUBLANES + (r // SUBLANES) % SUBLANES
-        block_x = LANES // count_x
-        held_at = from_y // HALF * block_x + from_s * HALF + from_y % HALF
-        picks = (held_at == c).astype(jnp.bfloat16)
-        same_z = r % HALF == c // rank
-        weights_y = [jnp.where(same_z, mul(picks, part), 0.0).astype(jnp.bfloat16) for part in held_y]
-
         def by_x(value):
             return jnp.concatenate([value[f].reshape(plane, LANES) for f in range(n_f)], axis=1)
 
-        partial = mul_split(split(by_x(adv)), weights_x)
-        core = mul_split(weights_y, split(partial), ((0,), (0,)))
-        columns = rescale * mul_split(weights_y, split(core))
-        for part in range(2):
-            spread_ref[part] = weights_x[part]
+        weights_x = [spread_ref[part] for part in range(2)]
+        partial = split(mul_split(split(by_x(adv)), weights_x))
+        core = mul_split([to_core_ref[part] for part in range(2)], partial)
+        columns = mul_split([project_ref[part] for part in range(2)], partial)
 
         block = plane // count_y
         for s in range(count_y):
@@ -393,8 +406,8 @@
             name=name,
         )(*operands)
 
-    def swap(blocks, tiles):
-        blocks = blocks.reshape(devices, tiles, HALF, n_z)
+    def swap(blocks):
+        blocks = blocks.reshape((devices,) + blocks.shape[2:])
         return lax.all_to_all(blocks, ("gx", "gy"), 0, 0, tiled=True)
 
     def pass_on(blocks, axis):
@@ -410,7 +423,7 @@
     (packed,) = call(
         pack_kernel,
         "pack",
-        [array((pairs, 2, 2 * n_f + 1, HALF, n_z))],
+        [array((pairs, 2, 4 * n_f + 1, 2, n_z))],
         [
             pltpu.VMEM(flat, f32),
             pltpu.VMEM(factor_x.shape, f32),
@@ -423,9 +436,10 @@
         ),
         space=hbm,
     )
-    planes = swap(packed, 2 * n_f + 1).reshape(count_x, count_y, 2 * n_f + 1, HALF, n_z)
+    planes = swap(packed).reshape(count_x, count_y, 4 * n_f + 1, 2, n_z)
     extended = pltpu.VMEM((count_y, n_f, SUBLANES + 6, SUBLANES, LANES), f32)
     rows = SUBLANES * SUBLANES + HALF * SUBLANES
+    plane = count_y * SUBLANES * SUBLANES
     sent, spread, *columns = call(
         functools.partial(main_kernel, n_f, count_x, count_y, rank, rescale),
         "sections",
@@ -440,12 +454,14 @@
             pltpu.VMEM((count_y, rows, LANES), f32),
             pltpu.VMEM((count_x, count_y, 2 * n_f, HALF, n_z), f32),
             pltpu.SemaphoreType.DMA,
+            pltpu.VMEM((2, LANES, plane), jnp.bfloat16),
+            pltpu.VMEM((2, plane, plane), jnp.bfloat16),
         ],
         (planes,),
         out_spaces=(hbm,) + (vmem,) * (1 + count_y),
     )
     columns = pass_on(columns, "gy")
-    sent = swap(sent, 2 * n_f).reshape(pairs, 2, 2 * n_f, HALF, n_z)
+    sent = swap(sent).reshape(pairs, 2, 2 * n_f, HALF, n_z)
     rows = (n_f * count_y + n_f // 2) * SUBLANES
     blocks = call(
         functools.partial(expand_kernel, n_f, count_x, count_y),

time: 52.4 us -> 52 us (level)
  blocking collectives: 23.6 us -> 22.9 us
    all_to_all x1, blocking collectives: 23.6 us -> 22.9 us  [swap(): return lax.all_to_all(blocks, ('gx', 'gy'), 0, 0, tiled=True)]
  transfers between devices with their start and end apart: 11 -> 11, of which waited for: 5 -> 5; matrix products, arithmetic and copies ran while one was open for 0% -> 0% of each run, Pallas kernels for 3% -> 4%
where the time goes in v7:
time: 52 us; the launch traced here: 51.7 us
  blocking collectives  22.9 us (44%)
  starting transfers between devices  14.2 us (27%)
  Pallas kernels  7.16 us (14%)
  waiting for transfers between devices  6.72 us (13%)
  between operations  0.72 us (1%)
    all_to_all x1, blocking collectives, swap(): return lax.all_to_all(blocks, ('gx', 'gy'), 0, 0, tiled=True)  22.9 us
    ppermute x10, starting transfers between devices, pass_on(): lax.ppermute(block, axis, [(i, (i + k) % count) for i in range(count)])  10.6 us
    pallas_call x5, Pallas kernels, call(): pl.pallas_call(kernel, out_shape=tuple(outs), in_specs=[space] * len(oper...  7.16 us
    ppermute x10, waiting for transfers between devices, pass_on(): lax.ppermute(block, axis, [(i, (i + k) % count) for i in range(count)])  6.72 us
    all_to_all x1, starting transfers between devices, swap(): return lax.all_to_all(blocks, ('gx', 'gy'), 0, 0, tiled=True)  3.64 us
  transfers between devices with their start and end apart: 11, of which 5 were waited for; matrix products, arithmetic and copies ran while one was open for 0% of the time, Pallas kernels for 4%

profile of v7, /device:TPU:1, one launch (start us, length us, event | category | flops | bytes accessed | tf_op | source)
XLA Modules:
  0.0 51.7 jit_solution(16548435317482376156)
XLA Ops:
  0.6 1.5 %pack.1 = f32[16,2,17,2,128]{4,3,2,1,0:T(2,128)S(1)} custom-call(f32[4,256,128]{2,1,0:T(8,128)} %bitcast.10, f32[16,32]{1,0:T(8,128)} %factor_x_hbm.1, f32[16,32]{1,0:T(8,128)} %factor_y_hbm.1), custom_call_target="tpu_custom_call" | custom-call | flops 1000000000 | tf_op jit(solution)/shard_map/pack/pallas_call | solution.py:398
  2.1 22.9 %all_to_all.10 = f32[32,17,2,128]{3,2,1,0:T(2,128)S(1)} all-to-all(f32[32,17,2,128]{3,2,1,0:T(2,128)S(1)} %bitcast.8), channel_id=1, replica_groups=mesh['gx'=8,'gy'=4] {'gx','gy'}, dimensions={0} | all-to-all | bytes 1114112 | tf_op jit(solution)/shard_map/all_to_all | solution.py:411
  25.0 2.9 %sections.1 = (f32[8,4,8,4,128]{4,3,2,1,0:T(4,128)}, bf16[2,512,128]{2,1,0:T(8,128)(2,1)S(1)}, f32[96,128]{1,0:T(8,128)S(1)}, f32[96,128]{1,0:T(8,128)S(1)}, f32...) custom-call(f32[8,4,17,2,128]{4,3,2,1,0:T(2,128)S(1)} %bitcast.7), custom_call_target="tpu_custom_call" | custom-call | flops 1000000000 | tf_op jit(solution)/shard_map/sections/pallas_call | solution.py:398
  27.9 0.1 collective-permute-start
  28.0 1.2 %collective-permute-start.1 = (f32[96,128]{1,0:T(8,128)S(1)}, f32[96,128]{1,0:T(8,128)S(1)}, u32[]{:S(2)}, u32[]{:S(2)}) collective-permute-start(f32[96,128]{1,0:T(8,128)S(1)} %get-tuple-element.23), channel_id=1, source_target_pairs={{0,2},{1,3},{2,0},{3,1},{4,6},{5,7},{6,4},{7,5},{8,10},{9,11},{10,... | collective-permute-start | bytes 147464 | tf_op jit(solution)/shard_map/ppermute | solution.py:416
  29.2 2.0 %collective-permute-start.2 = (f32[96,128]{1,0:T(8,128)S(1)}, f32[96,128]{1,0:T(8,128)S(1)}, u32[]{:S(2)}, u32[]{:S(2)}) collective-permute-start(f32[96,128]{1,0:T(8,128)S(1)} %get-tuple-element.24), channel_id=1, source_target_pairs={{0,3},{1,0},{2,1},{3,2},{4,7},{5,4},{6,5},{7,6},{8,11},{9,8},{10,9... | collective-permute-start | bytes 147464 | tf_op jit(solution)/shard_map/ppermute | solution.py:416
  31.3 3.6 %all-to-all-start.1 = ((f32[32,8,4,128]{3,2,1,0:T(4,128)}), f32[32,8,4,128]{3,2,1,0:T(4,128)S(1)}, u32[]{:S(2)}, u32[]{:S(2)}) async-start(f32[32,8,4,128]{3,2,1,0:T(4,128)} %bitcast.3), calls=%async_computation.1 | async-start | bytes 1048576 | tf_op jit(solution)/shard_map/all_to_all | solution.py:411
  34.9 0.0 collective-permute-done.refs_1_
  34.9 0.0 collective-permute-done.1.refs_2_
  34.9 0.0 collective-permute-done.2.refs_3_
  34.9 0.7 %expand.1 = (f32[144,128]{1,0:T(8,128)S(1)}, f32[144,128]{1,0:T(8,128)S(1)}, f32[144,128]{1,0:T(8,128)S(1)}, f32[144,128]{1,0:T(8,128)S(1)}, f32[144,128]{1,0:T(...) custom-call(bf16[2,512,128]{2,1,0:T(8,128)(2,1)S(1)} %get-tuple-element.20.spread_ref, ...), custom_call_target="tpu_custom_call" | custom-call | flops 20000000000 | tf_op jit(solution)/shard_map/expand/pallas_call | solution.py:398
  35.6 1.9 %collective-permute-start.3 = (f32[144,128]{1,0:T(8,128)S(1)}, f32[144,128]{1,0:T(8,128)S(1)}, u32[]{:S(2)}, u32[]{:S(2)}) collective-permute-start(f32[144,128]{1,0:T(8,128)S(1)} %get-tuple-element.26), channel_id=1, source_target_pairs={{0,4},{4,8},{8,12},{12,16},{16,20},{20,24},{24,28},{28,0},{1,5},{5... | collective-permute-start | bytes 221192 | tf_op jit(solution)/shard_map/ppermute | solution.py:416
  37.5 1.2 %collective-permute-start.4 = (f32[144,128]{1,0:T(8,128)S(1)}, f32[144,128]{1,0:T(8,128)S(1)}, u32[]{:S(2)}, u32[]{:S(2)}) collective-permute-start(f32[144,128]{1,0:T(8,128)S(1)} %get-tuple-element.27), channel_id=1, source_target_pairs={{0,8},{4,12},{8,16},{12,20},{16,24},{20,28},{24,0},{28,4},{1,9},{5... | collective-permute-start | bytes 221192 | tf_op jit(solution)/shard_map/ppermute | solution.py:416
  38.7 0.2 collective-permute-start.5
  38.9 0.4 collective-permute-start.6
  39.3 2.6 %collective-permute-start.7 = (f32[144,128]{1,0:T(8,128)S(1)}, f32[144,128]{1,0:T(8,128)S(1)}, u32[]{:S(2)}, u32[]{:S(2)}) collective-permute-start(f32[144,128]{1,0:T(8,128)S(1)} %get-tuple-element.30), channel_id=1, source_target_pairs={{0,20},{4,24},{8,28},{12,0},{16,4},{20,8},{24,12},{28,16},{1,21},{... | collective-permute-start | bytes 221192 | tf_op jit(solution)/shard_map/ppermute | solution.py:416
  42.0 0.0 collective-permute-done.3.refs_1_
  42.0 0.9 %collective-permute-start.8 = (f32[144,128]{1,0:T(8,128)S(1)}, f32[144,128]{1,0:T(8,128)S(1)}, u32[]{:S(2)}, u32[]{:S(2)}) collective-permute-start(f32[144,128]{1,0:T(8,128)S(1)} %get-tuple-element.31), channel_id=1, source_target_pairs={{0,24},{4,28},{8,0},{12,4},{16,8},{20,12},{24,16},{28,20},{1,25},{... | collective-permute-start | bytes 221192 | tf_op jit(solution)/shard_map/ppermute | solution.py:416
  42.9 2.6 %collective-permute-done.4.refs_2_ = f32[144,128]{1,0:T(8,128)S(1)} collective-permute-done((f32[144,128]{1,0:T(8,128)S(1)}, f32[144,128]{1,0:T(8,128)S(1)}, u32[]{:S(2)}, u32[]{:S(2)}) %collective-permute-start.4) | collective-permute-done | bytes 73760 | tf_op jit(solution)/shard_map/ppermute | solution.py:416
  45.5 0.0 collective-permute-start.9
  45.5 0.4 collective-permute-done.5.refs_3_
  45.9 3.5 %collective-permute-done.6.refs_4_ = f32[144,128]{1,0:T(8,128)S(1)} collective-permute-done((f32[144,128]{1,0:T(8,128)S(1)}, f32[144,128]{1,0:T(8,128)S(1)}, u32[]{:S(2)}, u32[]{:S(2)}) %collective-permute-start.6) | collective-permute-done | bytes 73760 | tf_op jit(solution)/shard_map/ppermute | solution.py:416
  49.4 0.1 collective-permute-done.7.refs_5_
  49.5 0.0 collective-permute-done.8.refs_6_
  49.5 0.1 collective-permute-done.9.refs_7_
  49.6 1.1 %rebuilt.1 = (f32[4,256,128]{2,1,0:T(8,128)}, f32[4,4,8,128]{3,2,1,0:T(8,128)}) custom-call(f32[144,128]{1,0:T(8,128)S(1)} %get-tuple-element.25.refs_0_, f32[144,128]{1,0:T(8,128)S(1)} %collective-permute-done.3.refs_1_, f32[144,128]{1,0:T(8,128)S(1)} %collective-permute-done.4.refs_2_, f32[144,128]{1,0:T(8,128)S(1)} %collective-permute-done.5.refs_3_, ...), custom_call_target="tpu_custom_call" | custom-call | flops 1000000000 | tf_op jit(solution)/shard_map/rebuilt/pallas_call | solution.py:398
  50.7 0.0 all-to-all-done.1
  50.8 0.9 %advanced.1 = f32[4,256,128]{2,1,0:T(8,128)} custom-call(f32[16,2,8,4,128]{4,3,2,1,0:T(4,128)S(1)} %bitcast.9), custom_call_target="tpu_custom_call" | custom-call | flops 1000000000 | tf_op jit(solution)/shard_map/advanced/pallas_call | solution.py:398
Async XLA Ops:
  27.9 7.0 %collective-permute-start = (f32[96,128]{1,0:T(8,128)S(1)}, f32[96,128]{1,0:T(8,128)S(1)}, u32[]{:S(2)}, u32[]{:S(2)}) collective-permute-start(f32[96,128]{1,0:T(8,128)S(1)} %get-tuple-element.22), channel_id=1, source_target_pairs={{0,1},{1,2},{2,3},{3,0},{4,5},{5,6},{6,7},{7,4},{8,9},{9,10},{10,1... | collective-permute-start | bytes 147464 | tf_op jit(solution)/shard_map/ppermute | solution.py:416
  28.0 6.9 %collective-permute-start.1 = (f32[96,128]{1,0:T(8,128)S(1)}, f32[96,128]{1,0:T(8,128)S(1)}, u32[]{:S(2)}, u32[]{:S(2)}) collective-permute-start(f32[96,128]{1,0:T(8,128)S(1)} %get-tuple-element.23), channel_id=1, source_target_pairs={{0,2},{1,3},{2,0},{3,1},{4,6},{5,7},{6,4},{7,5},{8,10},{9,11},{10,... | collective-permute-start | bytes 147464 | tf_op jit(solution)/shard_map/ppermute | solution.py:416
  29.2 5.7 %collective-permute-start.2 = (f32[96,128]{1,0:T(8,128)S(1)}, f32[96,128]{1,0:T(8,128)S(1)}, u32[]{:S(2)}, u32[]{:S(2)}) collective-permute-start(f32[96,128]{1,0:T(8,128)S(1)} %get-tuple-element.24), channel_id=1, source_target_pairs={{0,3},{1,0},{2,1},{3,2},{4,7},{5,4},{6,5},{7,6},{8,11},{9,8},{10,9... | collective-permute-start | bytes 147464 | tf_op jit(solution)/shard_map/ppermute | solution.py:416
  31.3 19.5 %all-to-all-start.1 = ((f32[32,8,4,128]{3,2,1,0:T(4,128)}), f32[32,8,4,128]{3,2,1,0:T(4,128)S(1)}, u32[]{:S(2)}, u32[]{:S(2)}) async-start(f32[32,8,4,128]{3,2,1,0:T(4,128)} %bitcast.3), calls=%async_computation.1 | async-start | bytes 1048576 | tf_op jit(solution)/shard_map/all_to_all | solution.py:411
  35.6 6.4 %collective-permute-start.3 = (f32[144,128]{1,0:T(8,128)S(1)}, f32[144,128]{1,0:T(8,128)S(1)}, u32[]{:S(2)}, u32[]{:S(2)}) collective-permute-start(f32[144,128]{1,0:T(8,128)S(1)} %get-tuple-element.26), channel_id=1, source_target_pairs={{0,4},{4,8},{8,12},{12,16},{16,20},{20,24},{24,28},{28,0},{1,5},{5... | collective-permute-start | bytes 221192 | tf_op jit(solution)/shard_map/ppermute | solution.py:416
  37.5 7.9 %collective-permute-start.4 = (f32[144,128]{1,0:T(8,128)S(1)}, f32[144,128]{1,0:T(8,128)S(1)}, u32[]{:S(2)}, u32[]{:S(2)}) collective-permute-start(f32[144,128]{1,0:T(8,128)S(1)} %get-tuple-element.27), channel_id=1, source_target_pairs={{0,8},{4,12},{8,16},{12,20},{16,24},{20,28},{24,0},{28,4},{1,9},{5... | collective-permute-start | bytes 221192 | tf_op jit(solution)/shard_map/ppermute | solution.py:416
  38.7 7.2 %collective-permute-start.5 = (f32[144,128]{1,0:T(8,128)S(1)}, f32[144,128]{1,0:T(8,128)S(1)}, u32[]{:S(2)}, u32[]{:S(2)}) collective-permute-start(f32[144,128]{1,0:T(8,128)S(1)} %get-tuple-element.28), channel_id=1, source_target_pairs={{0,12},{4,16},{8,20},{12,24},{16,28},{20,0},{24,4},{28,8},{1,13},{... | collective-permute-start | bytes 221192 | tf_op jit(solution)/shard_map/ppermute | solution.py:416
  38.9 10.5 %collective-permute-start.6 = (f32[144,128]{1,0:T(8,128)S(1)}, f32[144,128]{1,0:T(8,128)S(1)}, u32[]{:S(2)}, u32[]{:S(2)}) collective-permute-start(f32[144,128]{1,0:T(8,128)S(1)} %get-tuple-element.29), channel_id=1, source_target_pairs={{0,16},{4,20},{8,24},{12,28},{16,0},{20,4},{24,8},{28,12},{1,17},{... | collective-permute-start | bytes 221192 | tf_op jit(solution)/shard_map/ppermute | solution.py:416
  39.3 10.2 %collective-permute-start.7 = (f32[144,128]{1,0:T(8,128)S(1)}, f32[144,128]{1,0:T(8,128)S(1)}, u32[]{:S(2)}, u32[]{:S(2)}) collective-permute-start(f32[144,128]{1,0:T(8,128)S(1)} %get-tuple-element.30), channel_id=1, source_target_pairs={{0,20},{4,24},{8,28},{12,0},{16,4},{20,8},{24,12},{28,16},{1,21},{... | collective-permute-start | bytes 221192 | tf_op jit(solution)/shard_map/ppermute | solution.py:416
  42.0 7.5 %collective-permute-start.8 = (f32[144,128]{1,0:T(8,128)S(1)}, f32[144,128]{1,0:T(8,128)S(1)}, u32[]{:S(2)}, u32[]{:S(2)}) collective-permute-start(f32[144,128]{1,0:T(8,128)S(1)} %get-tuple-element.31), channel_id=1, source_target_pairs={{0,24},{4,28},{8,0},{12,4},{16,8},{20,12},{24,16},{28,20},{1,25},{... | collective-permute-start | bytes 221192 | tf_op jit(solution)/shard_map/ppermute | solution.py:416
  45.5 4.1 %collective-permute-start.9 = (f32[144,128]{1,0:T(8,128)S(1)}, f32[144,128]{1,0:T(8,128)S(1)}, u32[]{:S(2)}, u32[]{:S(2)}) collective-permute-start(f32[144,128]{1,0:T(8,128)S(1)} %get-tuple-element.32), channel_id=1, source_target_pairs={{0,28},{4,0},{8,4},{12,8},{16,12},{20,16},{24,20},{28,24},{1,29},{... | collective-permute-start | bytes 221192 | tf_op jit(solution)/shard_map/ppermute | solution.py:416

commit v8 on v7

--- a/solution.py
+++ b/solution.py
@@ -321,21 +321,24 @@
         ref[...] = staged[lax.rem(own + k, count_x)]
 
 
-def leave_fields(ref, hbm, sems):
-    return [
-        pltpu.make_async_copy(ref.at[f], hbm.at[f], sems.at[f]) for f in range(ref.shape[0])
-    ]
-
-
 def scatter_rows(turned, octet, block_x, block_y, target, f):
     for y in range(SUBLANES):
         rows = pl.ds(octet * SUBLANES + y, block_x, stride=block_y)
         target[f, rows, :] = turned[y * block_x : (y + 1) * block_x]
 
 
-def advanced_kernel(block_x, block_y, in_ref, advanced_hbm, advanced_ref, sems):
-    leaving = leave_fields(advanced_ref, advanced_hbm, sems)
-    for f in range(advanced_ref.shape[0]):
+def results_kernel(
+    block_x, block_y, in_ref, rebuilt_ref, core_ref, advanced_hbm, rebuilt_hbm, core_hbm, advanced_ref, sems
+):
+    n_f = advanced_ref.shape[0]
+    leaving = [
+        pltpu.make_async_copy(advanced_ref.at[f], advanced_hbm.at[f], sems.at[f]) for f in range(n_f)
+    ]
+    leaving.append(pltpu.make_async_copy(rebuilt_ref, rebuilt_hbm, sems.at[n_f]))
+    leaving.append(pltpu.make_async_copy(core_ref, core_hbm, sems.at[n_f + 1]))
+    leaving[n_f].start()
+    leaving[n_f + 1].start()
+    for f in range(n_f):
         for octet in range(2):
             place = 2 * f + octet
             matrix = jnp.concatenate([in_ref[:, 0, place], in_ref[:, 1, place]], axis=1)
@@ -347,10 +350,8 @@
 
 
 def rebuilt_kernel(block_x, block_y, count_x, count_y, *refs):
-    in_refs, (rebuilt_hbm, core_hbm, held, rebuilt_ref, core_ref, sems) = refs[:count_x], refs[count_x:]
+    in_refs, (rebuilt_ref, core_ref, held) = refs[:count_x], refs[count_x:]
     n_f = rebuilt_ref.shape[0]
-    leaving = leave_fields(rebuilt_ref, rebuilt_hbm, sems)
-    leaving.append(pltpu.make_async_copy(core_ref, core_hbm, sems.at[n_f]))
     own = lax.axis_index("gx")
     for k, ref in enumerate(in_refs):
         held[lax.rem(own + count_x - k, count_x)] = ref[...]
@@ -360,7 +361,6 @@
         tiles = exchange([held[i, at : at + SUBLANES] for i in range(count_x)], LANES // SUBLANES)
         for place, tile in enumerate(tiles):
             core_ref[2 * pair + place // a_count, place % a_count] = tile
-    leaving[n_f].start()
     pairs = count_y // 2
     lower = lax.broadcasted_iota(jnp.int32, (count_x, pairs, SUBLANES, LANES), 2) < HALF
     for f in range(n_f):
@@ -372,9 +372,6 @@
         for octet, part in enumerate((first, second)):
             turned = part.reshape(LANES, LANES).T
             scatter_rows(turned, octet, block_x, block_y, rebuilt_ref, f)
-        leaving[f].start()
-    for copy in leaving:
-        copy.wait()
 
 
 def z_plan(fields, factor_x, factor_y):
@@ -475,27 +472,21 @@
         cost=20000000000,
     )
     blocks = pass_on(blocks, "gx")
-    (advanced,) = call(
-        functools.partial(advanced_kernel, block_x, block_y),
-        "advanced",
-        [array(flat)],
-        [pltpu.VMEM(flat, f32), pltpu.SemaphoreType.DMA((n_f,))],
-        (sent,),
-        out_spaces=(hbm,),
-    )
+    core_shape = (n_f, rank // count_x, rank // count_y, n_z)
     rebuilt, core = call(
         functools.partial(rebuilt_kernel, block_x, block_y, count_x, count_y),
         "rebuilt",
-        [array(flat), array((n_f, rank // count_x, rank // count_y, n_z))],
-        [
-            pltpu.VMEM((count_x, rows, LANES), f32),
-            pltpu.VMEM(flat, f32),
-            pltpu.VMEM((n_f, rank // count_x, rank // count_y, n_z), f32),
-            pltpu.SemaphoreType.DMA((n_f + 1,)),
-        ],
+        [array(flat), array(core_shape)],
+        [pltpu.VMEM((count_x, rows, LANES), f32)],
         tuple(blocks),
-        out_spaces=(hbm, hbm),
-        cost=1000000000,
+    )
+    advanced, rebuilt, core = call(
+        functools.partial(results_kernel, block_x, block_y),
+        "results",
+        [array(flat), array(flat), array(core_shape)],
+        [pltpu.VMEM(flat, f32), pltpu.SemaphoreType.DMA((n_f + 2,))],
+        (sent, rebuilt, core),
+        out_spaces=(hbm,) * 3,
     )
     return advanced.reshape(fields.shape), core, rebuilt.reshape(fields.shape)
 

time: 52 us -> 51.5 us (level)
  Pallas kernels: 7.16 us -> 6.54 us
    pallas_call x5, Pallas kernels: 7.16 us -> 6.54 us  [call(): pl.pallas_call(kernel, out_shape=tuple(outs), in_specs=[space] * len(oper...]
  transfers between devices with their start and end apart: 11 -> 11, of which waited for: 5 -> 6; matrix products, arithmetic and copies ran while one was open for 0% -> 0% of each run, Pallas kernels for 4% -> 2%
where the time goes in v8:
time: 51.5 us; the launch traced here: 51.2 us
  blocking collectives  22.9 us (44%)
  starting transfers between devices  14.2 us (28%)
  waiting for transfers between devices  6.89 us (13%)
  Pallas kernels  6.54 us (13%)
  between operations  0.71 us (1%)
    all_to_all x1, blocking collectives, swap(): return lax.all_to_all(blocks, ('gx', 'gy'), 0, 0, tiled=True)  22.9 us
    ppermute x10, starting transfers between devices, pass_on(): lax.ppermute(block, axis, [(i, (i + k) % count) for i in range(count)])  10.6 us
    ppermute x10, waiting for transfers between devices, pass_on(): lax.ppermute(block, axis, [(i, (i + k) % count) for i in range(count)])  6.72 us
    pallas_call x5, Pallas kernels, call(): pl.pallas_call(kernel, out_shape=tuple(outs), in_specs=[space] * len(oper...  6.54 us
    all_to_all x1, starting transfers between devices, swap(): return lax.all_to_all(blocks, ('gx', 'gy'), 0, 0, tiled=True)  3.64 us
  transfers between devices with their start and end apart: 11, of which 6 were waited for; matrix products, arithmetic and copies ran while one was open for 0% of the time, Pallas kernels for 2%

profile of v8, /device:TPU:1, one launch (start us, length us, event | category | flops | bytes accessed | tf_op | source)
XLA Modules:
  0.0 51.2 jit_solution(6924126373047774301)
XLA Ops:
  0.6 1.5 %pack.1 = f32[16,2,17,2,128]{4,3,2,1,0:T(2,128)S(1)} custom-call(f32[4,256,128]{2,1,0:T(8,128)} %bitcast.10, f32[16,32]{1,0:T(8,128)} %factor_x_hbm.1, f32[16,32]{1,0:T(8,128)} %factor_y_hbm.1), custom_call_target="tpu_custom_call" | custom-call | flops 1000000000 | tf_op jit(solution)/shard_map/pack/pallas_call | solution.py:395
  2.1 22.9 %all_to_all.10 = f32[32,17,2,128]{3,2,1,0:T(2,128)S(1)} all-to-all(f32[32,17,2,128]{3,2,1,0:T(2,128)S(1)} %bitcast.8), channel_id=1, replica_groups=mesh['gx'=8,'gy'=4] {'gx','gy'}, dimensions={0} | all-to-all | bytes 1114112 | tf_op jit(solution)/shard_map/all_to_all | solution.py:408
  25.0 2.9 %sections.1 = (f32[8,4,8,4,128]{4,3,2,1,0:T(4,128)}, bf16[2,512,128]{2,1,0:T(8,128)(2,1)S(1)}, f32[96,128]{1,0:T(8,128)S(1)}, f32[96,128]{1,0:T(8,128)S(1)}, f32...) custom-call(f32[8,4,17,2,128]{4,3,2,1,0:T(2,128)S(1)} %bitcast.7), custom_call_target="tpu_custom_call" | custom-call | flops 1000000000 | tf_op jit(solution)/shard_map/sections/pallas_call | solution.py:395
  27.9 0.1 collective-permute-start
  28.0 1.2 %collective-permute-start.1 = (f32[96,128]{1,0:T(8,128)S(1)}, f32[96,128]{1,0:T(8,128)S(1)}, u32[]{:S(2)}, u32[]{:S(2)}) collective-permute-start(f32[96,128]{1,0:T(8,128)S(1)} %get-tuple-element.26), channel_id=1, source_target_pairs={{0,2},{1,3},{2,0},{3,1},{4,6},{5,7},{6,4},{7,5},{8,10},{9,11},{10,... | collective-permute-start | bytes 147464 | tf_op jit(solution)/shard_map/ppermute | solution.py:413
  29.2 2.0 %collective-permute-start.2 = (f32[96,128]{1,0:T(8,128)S(1)}, f32[96,128]{1,0:T(8,128)S(1)}, u32[]{:S(2)}, u32[]{:S(2)}) collective-permute-start(f32[96,128]{1,0:T(8,128)S(1)} %get-tuple-element.27), channel_id=1, source_target_pairs={{0,3},{1,0},{2,1},{3,2},{4,7},{5,4},{6,5},{7,6},{8,11},{9,8},{10,9... | collective-permute-start | bytes 147464 | tf_op jit(solution)/shard_map/ppermute | solution.py:413
  31.3 3.6 %all-to-all-start.1 = ((f32[32,8,4,128]{3,2,1,0:T(4,128)}), f32[32,8,4,128]{3,2,1,0:T(4,128)S(1)}, u32[]{:S(2)}, u32[]{:S(2)}) async-start(f32[32,8,4,128]{3,2,1,0:T(4,128)} %bitcast.3), calls=%async_computation.1 | async-start | bytes 1048576 | tf_op jit(solution)/shard_map/all_to_all | solution.py:408
  34.9 0.0 collective-permute-done.refs_1_
  34.9 0.0 collective-permute-done.1.refs_2_
  34.9 0.0 collective-permute-done.2.refs_3_
  34.9 0.7 %expand.1 = (f32[144,128]{1,0:T(8,128)S(1)}, f32[144,128]{1,0:T(8,128)S(1)}, f32[144,128]{1,0:T(8,128)S(1)}, f32[144,128]{1,0:T(8,128)S(1)}, f32[144,128]{1,0:T(...) custom-call(bf16[2,512,128]{2,1,0:T(8,128)(2,1)S(1)} %get-tuple-element.23.spread_ref, ...), custom_call_target="tpu_custom_call" | custom-call | flops 20000000000 | tf_op jit(solution)/shard_map/expand/pallas_call | solution.py:395
  35.6 1.9 %collective-permute-start.3 = (f32[144,128]{1,0:T(8,128)S(1)}, f32[144,128]{1,0:T(8,128)S(1)}, u32[]{:S(2)}, u32[]{:S(2)}) collective-permute-start(f32[144,128]{1,0:T(8,128)S(1)} %get-tuple-element.29), channel_id=1, source_target_pairs={{0,4},{4,8},{8,12},{12,16},{16,20},{20,24},{24,28},{28,0},{1,5},{5... | collective-permute-start | bytes 221192 | tf_op jit(solution)/shard_map/ppermute | solution.py:413
  37.5 1.2 %collective-permute-start.4 = (f32[144,128]{1,0:T(8,128)S(1)}, f32[144,128]{1,0:T(8,128)S(1)}, u32[]{:S(2)}, u32[]{:S(2)}) collective-permute-start(f32[144,128]{1,0:T(8,128)S(1)} %get-tuple-element.30), channel_id=1, source_target_pairs={{0,8},{4,12},{8,16},{12,20},{16,24},{20,28},{24,0},{28,4},{1,9},{5... | collective-permute-start | bytes 221192 | tf_op jit(solution)/shard_map/ppermute | solution.py:413
  38.7 0.2 collective-permute-start.5
  38.9 0.4 collective-permute-start.6
  39.3 2.6 %collective-permute-start.7 = (f32[144,128]{1,0:T(8,128)S(1)}, f32[144,128]{1,0:T(8,128)S(1)}, u32[]{:S(2)}, u32[]{:S(2)}) collective-permute-start(f32[144,128]{1,0:T(8,128)S(1)} %get-tuple-element.33), channel_id=1, source_target_pairs={{0,20},{4,24},{8,28},{12,0},{16,4},{20,8},{24,12},{28,16},{1,21},{... | collective-permute-start | bytes 221192 | tf_op jit(solution)/shard_map/ppermute | solution.py:413
  42.0 0.0 collective-permute-done.3.refs_1_
  42.0 0.9 %collective-permute-start.8 = (f32[144,128]{1,0:T(8,128)S(1)}, f32[144,128]{1,0:T(8,128)S(1)}, u32[]{:S(2)}, u32[]{:S(2)}) collective-permute-start(f32[144,128]{1,0:T(8,128)S(1)} %get-tuple-element.34), channel_id=1, source_target_pairs={{0,24},{4,28},{8,0},{12,4},{16,8},{20,12},{24,16},{28,20},{1,25},{... | collective-permute-start | bytes 221192 | tf_op jit(solution)/shard_map/ppermute | solution.py:413
  42.9 2.6 %collective-permute-done.4.refs_2_ = f32[144,128]{1,0:T(8,128)S(1)} collective-permute-done((f32[144,128]{1,0:T(8,128)S(1)}, f32[144,128]{1,0:T(8,128)S(1)}, u32[]{:S(2)}, u32[]{:S(2)}) %collective-permute-start.4) | collective-permute-done | bytes 73760 | tf_op jit(solution)/shard_map/ppermute | solution.py:413
  45.5 0.0 collective-permute-start.9
  45.5 0.4 collective-permute-done.5.refs_3_
  45.9 3.5 %collective-permute-done.6.refs_4_ = f32[144,128]{1,0:T(8,128)S(1)} collective-permute-done((f32[144,128]{1,0:T(8,128)S(1)}, f32[144,128]{1,0:T(8,128)S(1)}, u32[]{:S(2)}, u32[]{:S(2)}) %collective-permute-start.6) | collective-permute-done | bytes 73760 | tf_op jit(solution)/shard_map/ppermute | solution.py:413
  49.4 0.1 collective-permute-done.7.refs_5_
  49.5 0.0 collective-permute-done.8.refs_6_
  49.5 0.1 collective-permute-done.9.refs_7_
  49.6 0.4 rebuilt.1
  50.0 0.2 all-to-all-done.1
  50.2 1.0 %results.1 = (f32[4,256,128]{2,1,0:T(8,128)}, f32[4,256,128]{2,1,0:T(8,128)}, f32[4,4,8,128]{3,2,1,0:T(8,128)}) custom-call(f32[16,2,8,4,128]{4,3,2,1,0:T(4,128)S(1)} %bitcast.9, f32[4,256,128]{2,1,0:T(8,128)S(1)} %get-tuple-element.36.rebuilt_ref, f32[4,4,8,128]{3,2,1,0:T(8,128)S(1)} %get-tuple-element.37.core_ref), custom_call_target="tpu_custom_call" | custom-call | flops 1000000000 | tf_op jit(solution)/shard_map/results/pallas_call | solution.py:395
Async XLA Ops:
  27.9 7.0 %collective-permute-start = (f32[96,128]{1,0:T(8,128)S(1)}, f32[96,128]{1,0:T(8,128)S(1)}, u32[]{:S(2)}, u32[]{:S(2)}) collective-permute-start(f32[96,128]{1,0:T(8,128)S(1)} %get-tuple-element.25), channel_id=1, source_target_pairs={{0,1},{1,2},{2,3},{3,0},{4,5},{5,6},{6,7},{7,4},{8,9},{9,10},{10,1... | collective-permute-start | bytes 147464 | tf_op jit(solution)/shard_map/ppermute | solution.py:413
  28.0 6.9 %collective-permute-start.1 = (f32[96,128]{1,0:T(8,128)S(1)}, f32[96,128]{1,0:T(8,128)S(1)}, u32[]{:S(2)}, u32[]{:S(2)}) collective-permute-start(f32[96,128]{1,0:T(8,128)S(1)} %get-tuple-element.26), channel_id=1, source_target_pairs={{0,2},{1,3},{2,0},{3,1},{4,6},{5,7},{6,4},{7,5},{8,10},{9,11},{10,... | collective-permute-start | bytes 147464 | tf_op jit(solution)/shard_map/ppermute | solution.py:413
  29.2 5.7 %collective-permute-start.2 = (f32[96,128]{1,0:T(8,128)S(1)}, f32[96,128]{1,0:T(8,128)S(1)}, u32[]{:S(2)}, u32[]{:S(2)}) collective-permute-start(f32[96,128]{1,0:T(8,128)S(1)} %get-tuple-element.27), channel_id=1, source_target_pairs={{0,3},{1,0},{2,1},{3,2},{4,7},{5,4},{6,5},{7,6},{8,11},{9,8},{10,9... | collective-permute-start | bytes 147464 | tf_op jit(solution)/shard_map/ppermute | solution.py:413
  31.3 18.9 %all-to-all-start.1 = ((f32[32,8,4,128]{3,2,1,0:T(4,128)}), f32[32,8,4,128]{3,2,1,0:T(4,128)S(1)}, u32[]{:S(2)}, u32[]{:S(2)}) async-start(f32[32,8,4,128]{3,2,1,0:T(4,128)} %bitcast.3), calls=%async_computation.1 | async-start | bytes 1048576 | tf_op jit(solution)/shard_map/all_to_all | solution.py:408
  35.6 6.4 %collective-permute-start.3 = (f32[144,128]{1,0:T(8,128)S(1)}, f32[144,128]{1,0:T(8,128)S(1)}, u32[]{:S(2)}, u32[]{:S(2)}) collective-permute-start(f32[144,128]{1,0:T(8,128)S(1)} %get-tuple-element.29), channel_id=1, source_target_pairs={{0,4},{4,8},{8,12},{12,16},{16,20},{20,24},{24,28},{28,0},{1,5},{5... | collective-permute-start | bytes 221192 | tf_op jit(solution)/shard_map/ppermute | solution.py:413
  37.5 7.9 %collective-permute-start.4 = (f32[144,128]{1,0:T(8,128)S(1)}, f32[144,128]{1,0:T(8,128)S(1)}, u32[]{:S(2)}, u32[]{:S(2)}) collective-permute-start(f32[144,128]{1,0:T(8,128)S(1)} %get-tuple-element.30), channel_id=1, source_target_pairs={{0,8},{4,12},{8,16},{12,20},{16,24},{20,28},{24,0},{28,4},{1,9},{5... | collective-permute-start | bytes 221192 | tf_op jit(solution)/shard_map/ppermute | solution.py:413
  38.7 7.2 %collective-permute-start.5 = (f32[144,128]{1,0:T(8,128)S(1)}, f32[144,128]{1,0:T(8,128)S(1)}, u32[]{:S(2)}, u32[]{:S(2)}) collective-permute-start(f32[144,128]{1,0:T(8,128)S(1)} %get-tuple-element.31), channel_id=1, source_target_pairs={{0,12},{4,16},{8,20},{12,24},{16,28},{20,0},{24,4},{28,8},{1,13},{... | collective-permute-start | bytes 221192 | tf_op jit(solution)/shard_map/ppermute | solution.py:413
  38.9 10.5 %collective-permute-start.6 = (f32[144,128]{1,0:T(8,128)S(1)}, f32[144,128]{1,0:T(8,128)S(1)}, u32[]{:S(2)}, u32[]{:S(2)}) collective-permute-start(f32[144,128]{1,0:T(8,128)S(1)} %get-tuple-element.32), channel_id=1, source_target_pairs={{0,16},{4,20},{8,24},{12,28},{16,0},{20,4},{24,8},{28,12},{1,17},{... | collective-permute-start | bytes 221192 | tf_op jit(solution)/shard_map/ppermute | solution.py:413
  39.3 10.2 %collective-permute-start.7 = (f32[144,128]{1,0:T(8,128)S(1)}, f32[144,128]{1,0:T(8,128)S(1)}, u32[]{:S(2)}, u32[]{:S(2)}) collective-permute-start(f32[144,128]{1,0:T(8,128)S(1)} %get-tuple-element.33), channel_id=1, source_target_pairs={{0,20},{4,24},{8,28},{12,0},{16,4},{20,8},{24,12},{28,16},{1,21},{... | collective-permute-start | bytes 221192 | tf_op jit(solution)/shard_map/ppermute | solution.py:413
  42.0 7.5 %collective-permute-start.8 = (f32[144,128]{1,0:T(8,128)S(1)}, f32[144,128]{1,0:T(8,128)S(1)}, u32[]{:S(2)}, u32[]{:S(2)}) collective-permute-start(f32[144,128]{1,0:T(8,128)S(1)} %get-tuple-element.34), channel_id=1, source_target_pairs={{0,24},{4,28},{8,0},{12,4},{16,8},{20,12},{24,16},{28,20},{1,25},{... | collective-permute-start | bytes 221192 | tf_op jit(solution)/shard_map/ppermute | solution.py:413
  45.5 4.1 %collective-permute-start.9 = (f32[144,128]{1,0:T(8,128)S(1)}, f32[144,128]{1,0:T(8,128)S(1)}, u32[]{:S(2)}, u32[]{:S(2)}) collective-permute-start(f32[144,128]{1,0:T(8,128)S(1)} %get-tuple-element.35), channel_id=1, source_target_pairs={{0,28},{4,0},{8,4},{12,8},{16,12},{20,16},{24,20},{28,24},{1,29},{... | collective-permute-start | bytes 221192 | tf_op jit(solution)/shard_map/ppermute | solution.py:413

commit v9 on v8

--- a/solution.py
+++ b/solution.py
@@ -39,10 +39,14 @@
     )
 
 
+def digit(index, size, count):
+    return lax.shift_right_logical(index, size.bit_length() - 1) & (count - 1)
+
+
 def exchange(blocks, stride):
     count = len(blocks)
     period = stride * count
-    group = lax.broadcasted_iota(jnp.int32, (SUBLANES, LANES), 1) // stride % count
+    group = digit(lax.broadcasted_iota(jnp.int32, (SUBLANES, LANES), 1), stride, count)
     if period == LANES:
         blocks = [pltpu.roll(b, i * stride, 1) if i else b for i, b in enumerate(blocks)]
         step = 1
@@ -81,7 +85,9 @@
     for copy in copies:
         copy.start()
     for f in range(n_f):
-        copies[f].wait()
+        if f % 2 == 0:
+            copies[f].wait()
+            copies[f + 1].wait()
         for octet in range(2):
             matrix = jnp.concatenate(
                 [
@@ -124,22 +130,18 @@
 ):
     column_refs = refs[:count_y]
     ext_a, ext_b, ext_c, adv, staged, sent_ref, sent_sem = refs[count_y : count_y + 7]
-    to_core_ref, project_ref = refs[count_y + 7 :]
+    to_core_ref, from_core_ref = refs[count_y + 7 :]
     margin = 3
     inner = pl.ds(margin, SUBLANES)
     lower = lax.broadcasted_iota(jnp.int32, (margin, SUBLANES, LANES), 1) < HALF
 
     def each(body):
-        def step(s, carry):
+        for s in range(count_y):
             body(s)
-            return carry
-
-        lax.fori_loop(0, count_y, step, 0, unroll=True)
 
     def fill_margins(ext):
         def one(s):
-            before = lax.rem(s + count_y - 1, count_y)
-            after = lax.rem(s + 1, count_y)
+            before, after = (s - 1) % count_y, (s + 1) % count_y
             for f in range(n_f):
                 old = ext[before, f, pl.ds(SUBLANES, margin)]
                 own = ext[s, f, pl.ds(SUBLANES, margin)]
@@ -219,33 +221,33 @@
     count = count_x * count_y
     held = in_ref[:, :, 4 * n_f].reshape(2 * count, LANES)
     held_at = lax.broadcasted_iota(jnp.int32, (LANES, 2 * count), 1)
-    source = lax.broadcasted_iota(jnp.int32, (LANES, 2 * count), 0) // HALF
+    source = digit(lax.broadcasted_iota(jnp.int32, (LANES, 2 * count), 0), HALF, count)
     rows_of = (held_at == 2 * source).astype(jnp.bfloat16)
-    spread_x = [jnp.where(row % HALF == col // rank, mul(rows_of, part), 0.0) for part in split(held)]
-    picks = (row % rank == col // n_f).astype(jnp.bfloat16)
+    spread_x = [jnp.where(digit(row, 1, HALF) == digit(col, rank, HALF), mul(rows_of, part), 0.0) for part in split(held)]
+    picks = (digit(row, 1, rank) == digit(col, n_f, rank)).astype(jnp.bfloat16)
     spread_x = [mul(part.astype(jnp.bfloat16), picks) for part in spread_x]
     weights_x = [
         jnp.concatenate(
-            [jnp.where(col % n_f == f, part, 0.0).astype(jnp.bfloat16) for f in range(n_f)], axis=0
+            [jnp.where(digit(col, 1, n_f) == f, part, 0.0).astype(jnp.bfloat16) for f in range(n_f)], axis=0
         )
         for part in spread_x
     ]
     r = lax.broadcasted_iota(jnp.int32, (plane, LANES), 0)
     c = lax.broadcasted_iota(jnp.int32, (plane, LANES), 1)
-    from_s, from_y = r // (SUBLANES * SUBLANES), (r // HALF) % 2 * SUBLANES + (r // SUBLANES) % SUBLANES
+    from_s = digit(r, SUBLANES * SUBLANES, count_y)
+    octet, from_y = digit(r, HALF, 2), digit(r, SUBLANES, SUBLANES)
     held_at = lax.broadcasted_iota(jnp.int32, (plane, 2 * count), 1)
-    source = (from_y // 2 * count_y + from_s)[:, : 2 * count]
+    source = ((octet * HALF + digit(from_y, 2, HALF)) * count_y + from_s)[:, : 2 * count]
     rows_of = (held_at == 2 * source + 1).astype(jnp.bfloat16)
-    spread_y = [jnp.where(from_y % 2 == c // rank % 2, mul(rows_of, part), 0.0) for part in split(held)]
+    spread_y = [jnp.where(digit(from_y, 1, 2) == digit(c, rank, 2), mul(rows_of, part), 0.0) for part in split(held)]
     spread_y = [part + pltpu.roll(part, rank, 1) for part in spread_y]
-    same_z = r % HALF == c // rank
+    same_z = digit(r, 1, HALF) == digit(c, rank, HALF)
     weights_y = [jnp.where(same_z, part, 0.0).astype(jnp.bfloat16) for part in spread_y]
     for part in range(2):
         spread_ref[part] = weights_x[part]
         to_core_ref[part] = weights_y[part].astype(jnp.float32).T.astype(jnp.bfloat16)
-    projector = split(rescale * mul_split(weights_y, weights_y, ((1,), (1,))))
     for part in range(2):
-        project_ref[part] = projector[part]
+        from_core_ref[part] = weights_y[part]
 
     each(arrive)
     fill_margins(ext_a)
@@ -265,7 +267,7 @@
         weights_x = [spread_ref[part] for part in range(2)]
         partial = split(mul_split(split(by_x(adv)), weights_x))
         core = mul_split([to_core_ref[part] for part in range(2)], partial)
-        columns = mul_split([project_ref[part] for part in range(2)], partial)
+        columns = rescale * mul_split([from_core_ref[part] for part in range(2)], split(core))
 
         block = plane // count_y
         for s in range(count_y):
@@ -452,7 +454,7 @@
             pltpu.VMEM((count_x, count_y, 2 * n_f, HALF, n_z), f32),
             pltpu.SemaphoreType.DMA,
             pltpu.VMEM((2, LANES, plane), jnp.bfloat16),
-            pltpu.VMEM((2, plane, plane), jnp.bfloat16),
+            pltpu.VMEM((2, plane, LANES), jnp.bfloat16),
         ],
         (planes,),
         out_spaces=(hbm,) + (vmem,) * (1 + count_y),

time: 51.5 us -> 51.2 us (level)
  no operation moved by 1% of the time
where the time goes in v9:
time: 51.2 us; the launch traced here: 50.9 us
  blocking collectives  22.9 us (45%)
  starting transfers between devices  14.2 us (28%)
  waiting for transfers between devices  6.9 us (13%)
  Pallas kernels  6.23 us (12%)
  between operations  0.71 us (1%)
    all_to_all x1, blocking collectives, swap(): return lax.all_to_all(blocks, ('gx', 'gy'), 0, 0, tiled=True)  22.9 us
    ppermute x10, starting transfers between devices, pass_on(): lax.ppermute(block, axis, [(i, (i + k) % count) for i in range(count)])  10.6 us
    ppermute x10, waiting for transfers between devices, pass_on(): lax.ppermute(block, axis, [(i, (i + k) % count) for i in range(count)])  6.72 us
    pallas_call x5, Pallas kernels, call(): pl.pallas_call(kernel, out_shape=tuple(outs), in_specs=[space] * len(oper...  6.23 us
    all_to_all x1, starting transfers between devices, swap(): return lax.all_to_all(blocks, ('gx', 'gy'), 0, 0, tiled=True)  3.64 us
  transfers between devices with their start and end apart: 11, of which 6 were waited for; matrix products, arithmetic and copies ran while one was open for 0% of the time, Pallas kernels for 2%

profile of v9, /device:TPU:1, one launch (start us, length us, event | category | flops | bytes accessed | tf_op | source)
XLA Modules:
  0.0 50.9 jit_solution(11328994117458253163)
XLA Ops:
  0.6 1.4 %pack.1 = f32[16,2,17,2,128]{4,3,2,1,0:T(2,128)S(1)} custom-call(f32[4,256,128]{2,1,0:T(8,128)} %bitcast.10, f32[16,32]{1,0:T(8,128)} %factor_x_hbm.1, f32[16,32]{1,0:T(8,128)} %factor_y_hbm.1), custom_call_target="tpu_custom_call" | custom-call | flops 1000000000 | tf_op jit(solution)/shard_map/pack/pallas_call | solution.py:397
  2.0 22.9 %all_to_all.10 = f32[32,17,2,128]{3,2,1,0:T(2,128)S(1)} all-to-all(f32[32,17,2,128]{3,2,1,0:T(2,128)S(1)} %bitcast.8), channel_id=1, replica_groups=mesh['gx'=8,'gy'=4] {'gx','gy'}, dimensions={0} | all-to-all | bytes 1114112 | tf_op jit(solution)/shard_map/all_to_all | solution.py:410
  24.9 2.7 %sections.1 = (f32[8,4,8,4,128]{4,3,2,1,0:T(4,128)}, bf16[2,512,128]{2,1,0:T(8,128)(2,1)S(1)}, f32[96,128]{1,0:T(8,128)S(1)}, f32[96,128]{1,0:T(8,128)S(1)}, f32...) custom-call(f32[8,4,17,2,128]{4,3,2,1,0:T(2,128)S(1)} %bitcast.7), custom_call_target="tpu_custom_call" | custom-call | flops 1000000000 | tf_op jit(solution)/shard_map/sections/pallas_call | solution.py:397
  27.6 0.1 collective-permute-start
  27.7 1.2 %collective-permute-start.1 = (f32[96,128]{1,0:T(8,128)S(1)}, f32[96,128]{1,0:T(8,128)S(1)}, u32[]{:S(2)}, u32[]{:S(2)}) collective-permute-start(f32[96,128]{1,0:T(8,128)S(1)} %get-tuple-element.26), channel_id=1, source_target_pairs={{0,2},{1,3},{2,0},{3,1},{4,6},{5,7},{6,4},{7,5},{8,10},{9,11},{10,... | collective-permute-start | bytes 147464 | tf_op jit(solution)/shard_map/ppermute | solution.py:415
  29.0 2.0 %collective-permute-start.2 = (f32[96,128]{1,0:T(8,128)S(1)}, f32[96,128]{1,0:T(8,128)S(1)}, u32[]{:S(2)}, u32[]{:S(2)}) collective-permute-start(f32[96,128]{1,0:T(8,128)S(1)} %get-tuple-element.27), channel_id=1, source_target_pairs={{0,3},{1,0},{2,1},{3,2},{4,7},{5,4},{6,5},{7,6},{8,11},{9,8},{10,9... | collective-permute-start | bytes 147464 | tf_op jit(solution)/shard_map/ppermute | solution.py:415
  31.0 3.6 %all-to-all-start.1 = ((f32[32,8,4,128]{3,2,1,0:T(4,128)}), f32[32,8,4,128]{3,2,1,0:T(4,128)S(1)}, u32[]{:S(2)}, u32[]{:S(2)}) async-start(f32[32,8,4,128]{3,2,1,0:T(4,128)} %bitcast.3), calls=%async_computation.1 | async-start | bytes 1048576 | tf_op jit(solution)/shard_map/all_to_all | solution.py:410
  34.6 0.0 collective-permute-done.refs_1_
  34.6 0.0 collective-permute-done.1.refs_2_
  34.6 0.0 collective-permute-done.2.refs_3_
  34.6 0.7 %expand.1 = (f32[144,128]{1,0:T(8,128)S(1)}, f32[144,128]{1,0:T(8,128)S(1)}, f32[144,128]{1,0:T(8,128)S(1)}, f32[144,128]{1,0:T(8,128)S(1)}, f32[144,128]{1,0:T(...) custom-call(bf16[2,512,128]{2,1,0:T(8,128)(2,1)S(1)} %get-tuple-element.23.spread_ref, ...), custom_call_target="tpu_custom_call" | custom-call | flops 20000000000 | tf_op jit(solution)/shard_map/expand/pallas_call | solution.py:397
  35.3 1.9 %collective-permute-start.3 = (f32[144,128]{1,0:T(8,128)S(1)}, f32[144,128]{1,0:T(8,128)S(1)}, u32[]{:S(2)}, u32[]{:S(2)}) collective-permute-start(f32[144,128]{1,0:T(8,128)S(1)} %get-tuple-element.29), channel_id=1, source_target_pairs={{0,4},{4,8},{8,12},{12,16},{16,20},{20,24},{24,28},{28,0},{1,5},{5... | collective-permute-start | bytes 221192 | tf_op jit(solution)/shard_map/ppermute | solution.py:415
  37.2 1.2 %collective-permute-start.4 = (f32[144,128]{1,0:T(8,128)S(1)}, f32[144,128]{1,0:T(8,128)S(1)}, u32[]{:S(2)}, u32[]{:S(2)}) collective-permute-start(f32[144,128]{1,0:T(8,128)S(1)} %get-tuple-element.30), channel_id=1, source_target_pairs={{0,8},{4,12},{8,16},{12,20},{16,24},{20,28},{24,0},{28,4},{1,9},{5... | collective-permute-start | bytes 221192 | tf_op jit(solution)/shard_map/ppermute | solution.py:415
  38.4 0.2 collective-permute-start.5
  38.6 0.4 collective-permute-start.6
  39.0 2.7 %collective-permute-start.7 = (f32[144,128]{1,0:T(8,128)S(1)}, f32[144,128]{1,0:T(8,128)S(1)}, u32[]{:S(2)}, u32[]{:S(2)}) collective-permute-start(f32[144,128]{1,0:T(8,128)S(1)} %get-tuple-element.33), channel_id=1, source_target_pairs={{0,20},{4,24},{8,28},{12,0},{16,4},{20,8},{24,12},{28,16},{1,21},{... | collective-permute-start | bytes 221192 | tf_op jit(solution)/shard_map/ppermute | solution.py:415
  41.7 0.0 collective-permute-done.3.refs_1_
  41.7 0.9 %collective-permute-start.8 = (f32[144,128]{1,0:T(8,128)S(1)}, f32[144,128]{1,0:T(8,128)S(1)}, u32[]{:S(2)}, u32[]{:S(2)}) collective-permute-start(f32[144,128]{1,0:T(8,128)S(1)} %get-tuple-element.34), channel_id=1, source_target_pairs={{0,24},{4,28},{8,0},{12,4},{16,8},{20,12},{24,16},{28,20},{1,25},{... | collective-permute-start | bytes 221192 | tf_op jit(solution)/shard_map/ppermute | solution.py:415
  42.6 2.6 %collective-permute-done.4.refs_2_ = f32[144,128]{1,0:T(8,128)S(1)} collective-permute-done((f32[144,128]{1,0:T(8,128)S(1)}, f32[144,128]{1,0:T(8,128)S(1)}, u32[]{:S(2)}, u32[]{:S(2)}) %collective-permute-start.4) | collective-permute-done | bytes 73760 | tf_op jit(solution)/shard_map/ppermute | solution.py:415
  45.2 0.0 collective-permute-start.9
  45.2 0.4 collective-permute-done.5.refs_3_
  45.6 3.5 %collective-permute-done.6.refs_4_ = f32[144,128]{1,0:T(8,128)S(1)} collective-permute-done((f32[144,128]{1,0:T(8,128)S(1)}, f32[144,128]{1,0:T(8,128)S(1)}, u32[]{:S(2)}, u32[]{:S(2)}) %collective-permute-start.6) | collective-permute-done | bytes 73760 | tf_op jit(solution)/shard_map/ppermute | solution.py:415
  49.1 0.1 collective-permute-done.7.refs_5_
  49.2 0.0 collective-permute-done.8.refs_6_
  49.2 0.1 collective-permute-done.9.refs_7_
  49.3 0.4 rebuilt.1
  49.7 0.2 all-to-all-done.1
  49.9 1.0 %results.1 = (f32[4,256,128]{2,1,0:T(8,128)}, f32[4,256,128]{2,1,0:T(8,128)}, f32[4,4,8,128]{3,2,1,0:T(8,128)}) custom-call(f32[16,2,8,4,128]{4,3,2,1,0:T(4,128)S(1)} %bitcast.9, f32[4,256,128]{2,1,0:T(8,128)S(1)} %get-tuple-element.36.rebuilt_ref, f32[4,4,8,128]{3,2,1,0:T(8,128)S(1)} %get-tuple-element.37.core_ref), custom_call_target="tpu_custom_call" | custom-call | flops 1000000000 | tf_op jit(solution)/shard_map/results/pallas_call | solution.py:397
Async XLA Ops:
  27.6 7.0 %collective-permute-start = (f32[96,128]{1,0:T(8,128)S(1)}, f32[96,128]{1,0:T(8,128)S(1)}, u32[]{:S(2)}, u32[]{:S(2)}) collective-permute-start(f32[96,128]{1,0:T(8,128)S(1)} %get-tuple-element.25), channel_id=1, source_target_pairs={{0,1},{1,2},{2,3},{3,0},{4,5},{5,6},{6,7},{7,4},{8,9},{9,10},{10,1... | collective-permute-start | bytes 147464 | tf_op jit(solution)/shard_map/ppermute | solution.py:415
  27.7 6.9 %collective-permute-start.1 = (f32[96,128]{1,0:T(8,128)S(1)}, f32[96,128]{1,0:T(8,128)S(1)}, u32[]{:S(2)}, u32[]{:S(2)}) collective-permute-start(f32[96,128]{1,0:T(8,128)S(1)} %get-tuple-element.26), channel_id=1, source_target_pairs={{0,2},{1,3},{2,0},{3,1},{4,6},{5,7},{6,4},{7,5},{8,10},{9,11},{10,... | collective-permute-start | bytes 147464 | tf_op jit(solution)/shard_map/ppermute | solution.py:415
  29.0 5.7 %collective-permute-start.2 = (f32[96,128]{1,0:T(8,128)S(1)}, f32[96,128]{1,0:T(8,128)S(1)}, u32[]{:S(2)}, u32[]{:S(2)}) collective-permute-start(f32[96,128]{1,0:T(8,128)S(1)} %get-tuple-element.27), channel_id=1, source_target_pairs={{0,3},{1,0},{2,1},{3,2},{4,7},{5,4},{6,5},{7,6},{8,11},{9,8},{10,9... | collective-permute-start | bytes 147464 | tf_op jit(solution)/shard_map/ppermute | solution.py:415
  31.0 18.9 %all-to-all-start.1 = ((f32[32,8,4,128]{3,2,1,0:T(4,128)}), f32[32,8,4,128]{3,2,1,0:T(4,128)S(1)}, u32[]{:S(2)}, u32[]{:S(2)}) async-start(f32[32,8,4,128]{3,2,1,0:T(4,128)} %bitcast.3), calls=%async_computation.1 | async-start | bytes 1048576 | tf_op jit(solution)/shard_map/all_to_all | solution.py:410
  35.3 6.4 %collective-permute-start.3 = (f32[144,128]{1,0:T(8,128)S(1)}, f32[144,128]{1,0:T(8,128)S(1)}, u32[]{:S(2)}, u32[]{:S(2)}) collective-permute-start(f32[144,128]{1,0:T(8,128)S(1)} %get-tuple-element.29), channel_id=1, source_target_pairs={{0,4},{4,8},{8,12},{12,16},{16,20},{20,24},{24,28},{28,0},{1,5},{5... | collective-permute-start | bytes 221192 | tf_op jit(solution)/shard_map/ppermute | solution.py:415
  37.2 8.0 %collective-permute-start.4 = (f32[144,128]{1,0:T(8,128)S(1)}, f32[144,128]{1,0:T(8,128)S(1)}, u32[]{:S(2)}, u32[]{:S(2)}) collective-permute-start(f32[144,128]{1,0:T(8,128)S(1)} %get-tuple-element.30), channel_id=1, source_target_pairs={{0,8},{4,12},{8,16},{12,20},{16,24},{20,28},{24,0},{28,4},{1,9},{5... | collective-permute-start | bytes 221192 | tf_op jit(solution)/shard_map/ppermute | solution.py:415
  38.4 7.2 %collective-permute-start.5 = (f32[144,128]{1,0:T(8,128)S(1)}, f32[144,128]{1,0:T(8,128)S(1)}, u32[]{:S(2)}, u32[]{:S(2)}) collective-permute-start(f32[144,128]{1,0:T(8,128)S(1)} %get-tuple-element.31), channel_id=1, source_target_pairs={{0,12},{4,16},{8,20},{12,24},{16,28},{20,0},{24,4},{28,8},{1,13},{... | collective-permute-start | bytes 221192 | tf_op jit(solution)/shard_map/ppermute | solution.py:415
  38.6 10.5 %collective-permute-start.6 = (f32[144,128]{1,0:T(8,128)S(1)}, f32[144,128]{1,0:T(8,128)S(1)}, u32[]{:S(2)}, u32[]{:S(2)}) collective-permute-start(f32[144,128]{1,0:T(8,128)S(1)} %get-tuple-element.32), channel_id=1, source_target_pairs={{0,16},{4,20},{8,24},{12,28},{16,0},{20,4},{24,8},{28,12},{1,17},{... | collective-permute-start | bytes 221192 | tf_op jit(solution)/shard_map/ppermute | solution.py:415
  39.0 10.2 %collective-permute-start.7 = (f32[144,128]{1,0:T(8,128)S(1)}, f32[144,128]{1,0:T(8,128)S(1)}, u32[]{:S(2)}, u32[]{:S(2)}) collective-permute-start(f32[144,128]{1,0:T(8,128)S(1)} %get-tuple-element.33), channel_id=1, source_target_pairs={{0,20},{4,24},{8,28},{12,0},{16,4},{20,8},{24,12},{28,16},{1,21},{... | collective-permute-start | bytes 221192 | tf_op jit(solution)/shard_map/ppermute | solution.py:415
  41.7 7.5 %collective-permute-start.8 = (f32[144,128]{1,0:T(8,128)S(1)}, f32[144,128]{1,0:T(8,128)S(1)}, u32[]{:S(2)}, u32[]{:S(2)}) collective-permute-start(f32[144,128]{1,0:T(8,128)S(1)} %get-tuple-element.34), channel_id=1, source_target_pairs={{0,24},{4,28},{8,0},{12,4},{16,8},{20,12},{24,16},{28,20},{1,25},{... | collective-permute-start | bytes 221192 | tf_op jit(solution)/shard_map/ppermute | solution.py:415
  45.2 4.1 %collective-permute-start.9 = (f32[144,128]{1,0:T(8,128)S(1)}, f32[144,128]{1,0:T(8,128)S(1)}, u32[]{:S(2)}, u32[]{:S(2)}) collective-permute-start(f32[144,128]{1,0:T(8,128)S(1)} %get-tuple-element.35), channel_id=1, source_target_pairs={{0,28},{4,0},{8,4},{12,8},{16,12},{20,16},{24,20},{28,24},{1,29},{... | collective-permute-start | bytes 221192 | tf_op jit(solution)/shard_map/ppermute | solution.py:415

commit v10 on v9

--- a/solution.py
+++ b/solution.py
@@ -72,7 +72,8 @@
     return blocks
 
 
-def pack_kernel(fields_hbm, factor_x_hbm, factor_y_hbm, out_ref, fields_ref, x_ref, y_ref, sems):
+def pack_kernel(constants, fields_hbm, factor_x_hbm, factor_y_hbm, out_ref, *refs):
+    *constant_refs, fields_ref, x_ref, y_ref, sems = refs
     n_f, rows, _ = fields_ref.shape
     block_x = x_ref.shape[0]
     block_y = rows // block_x
@@ -84,6 +85,7 @@
     copies.append(pltpu.make_async_copy(factor_y_hbm, y_ref, sems.at[n_f + 1]))
     for copy in copies:
         copy.start()
+    constants(*constant_refs)
     for f in range(n_f):
         if f % 2 == 0:
             copies[f].wait()
@@ -125,8 +127,40 @@
     return mul(a[0], b[0], dims) + (mul(a[0], b[1], dims) + mul(a[1], b[0], dims))
 
 
+def constants_kernel(
+    n_f, count_x, count_y, rank, taps_ref, rows_x_ref, lanes_x_ref, picks_ref, rows_y_ref, lanes_y_ref
+):
+    row = lax.broadcasted_iota(jnp.int32, (LANES, LANES), 0)
+    col = lax.broadcasted_iota(jnp.int32, (LANES, LANES), 1)
+    ahead = (row - col) & (LANES - 1)
+    taps = jnp.zeros((LANES, LANES), jnp.float32)
+    for shift, weight in ((1, 45.0), (2, -9.0), (3, 1.0)):
+        taps = jnp.where(ahead == shift, weight, taps)
+        taps = jnp.where(ahead == LANES - shift, -weight, taps)
+    taps = taps.astype(jnp.bfloat16)
+    taps = jnp.concatenate([taps, taps], axis=0)
+    taps_ref[...] = taps
+    count = count_x * count_y
+    plane = count_y * SUBLANES * SUBLANES
+    held_at = lax.broadcasted_iota(jnp.int32, (LANES, 2 * count), 1)
+    source = digit(lax.broadcasted_iota(jnp.int32, (LANES, 2 * count), 0), HALF, count)
+    rows_x_ref[...] = (held_at == 2 * source).astype(jnp.bfloat16)
+    lanes_x_ref[...] = (digit(row, 1, HALF) == digit(col, rank, HALF)).astype(jnp.float32)
+    picks_ref[...] = (digit(row, 1, rank) == digit(col, n_f, rank)).astype(jnp.bfloat16)
+    r = lax.broadcasted_iota(jnp.int32, (plane, LANES), 0)
+    c = lax.broadcasted_iota(jnp.int32, (plane, LANES), 1)
+    from_s = digit(r, SUBLANES * SUBLANES, count_y)
+    octet, from_y = digit(r, HALF, 2), digit(r, SUBLANES, SUBLANES)
+    held_at = lax.broadcasted_iota(jnp.int32, (plane, 2 * count), 1)
+    source = ((octet * HALF + digit(from_y, 2, HALF)) * count_y + from_s)[:, : 2 * count]
+    rows_y_ref[...] = (held_at == 2 * source + 1).astype(jnp.bfloat16)
+    lanes_y_ref[0] = (digit(from_y, 1, 2) == digit(c, rank, 2)).astype(jnp.float32)
+    lanes_y_ref[1] = (digit(r, 1, HALF) == digit(c, rank, HALF)).astype(jnp.float32)
+
+
 def main_kernel(
-    n_f, count_x, count_y, rank, rescale, in_ref, sent_hbm, spread_ref, *refs
+    n_f, count_x, count_y, rank, rescale, in_ref,
+    taps_ref, rows_x_ref, lanes_x_ref, picks_ref, rows_y_ref, lanes_y_ref, sent_hbm, spread_ref, *refs
 ):
     column_refs = refs[:count_y]
     ext_a, ext_b, ext_c, adv, staged, sent_ref, sent_sem = refs[count_y : count_y + 7]
@@ -154,15 +188,7 @@
 
         each(one)
 
-    row = lax.broadcasted_iota(jnp.int32, (LANES, LANES), 0)
-    col = lax.broadcasted_iota(jnp.int32, (LANES, LANES), 1)
-    ahead = (row - col) & (LANES - 1)
-    taps = jnp.zeros((LANES, LANES), jnp.float32)
-    for shift, weight in ((1, 45.0), (2, -9.0), (3, 1.0)):
-        taps = jnp.where(ahead == shift, weight, taps)
-        taps = jnp.where(ahead == LANES - shift, -weight, taps)
-    taps = taps.astype(jnp.bfloat16)
-    taps = jnp.concatenate([taps, taps], axis=0)
+    taps = taps_ref[...]
 
     def section(ext, step, store):
         def one(s):
@@ -218,31 +244,20 @@
             sent_ref[i, s, 2 * f : 2 * f + 2] = part.reshape(2, HALF, LANES)
 
     plane = count_y * SUBLANES * SUBLANES
-    count = count_x * count_y
-    held = in_ref[:, :, 4 * n_f].reshape(2 * count, LANES)
-    held_at = lax.broadcasted_iota(jnp.int32, (LANES, 2 * count), 1)
-    source = digit(lax.broadcasted_iota(jnp.int32, (LANES, 2 * count), 0), HALF, count)
-    rows_of = (held_at == 2 * source).astype(jnp.bfloat16)
-    spread_x = [jnp.where(digit(row, 1, HALF) == digit(col, rank, HALF), mul(rows_of, part), 0.0) for part in split(held)]
-    picks = (digit(row, 1, rank) == digit(col, n_f, rank)).astype(jnp.bfloat16)
-    spread_x = [mul(part.astype(jnp.bfloat16), picks) for part in spread_x]
+    held = in_ref[:, :, 4 * n_f].reshape(2 * count_x * count_y, LANES)
+    held = split(held)
+    spread_x = [mul(rows_x_ref[...], part) * lanes_x_ref[...] for part in held]
+    spread_x = [mul(part.astype(jnp.bfloat16), picks_ref[...]) for part in spread_x]
+    col = lax.broadcasted_iota(jnp.int32, (LANES, LANES), 1)
     weights_x = [
         jnp.concatenate(
             [jnp.where(digit(col, 1, n_f) == f, part, 0.0).astype(jnp.bfloat16) for f in range(n_f)], axis=0
         )
         for part in spread_x
     ]
-    r = lax.broadcasted_iota(jnp.int32, (plane, LANES), 0)
-    c = lax.broadcasted_iota(jnp.int32, (plane, LANES), 1)
-    from_s = digit(r, SUBLANES * SUBLANES, count_y)
-    octet, from_y = digit(r, HALF, 2), digit(r, SUBLANES, SUBLANES)
-    held_at = lax.broadcasted_iota(jnp.int32, (plane, 2 * count), 1)
-    source = ((octet * HALF + digit(from_y, 2, HALF)) * count_y + from_s)[:, : 2 * count]
-    rows_of = (held_at == 2 * source + 1).astype(jnp.bfloat16)
-    spread_y = [jnp.where(digit(from_y, 1, 2) == digit(c, rank, 2), mul(rows_of, part), 0.0) for part in split(held)]
+    spread_y = [mul(rows_y_ref[...], part) * lanes_y_ref[0] for part in held]
     spread_y = [part + pltpu.roll(part, rank, 1) for part in spread_y]
-    same_z = digit(r, 1, HALF) == digit(c, rank, HALF)
-    weights_y = [jnp.where(same_z, part, 0.0).astype(jnp.bfloat16) for part in spread_y]
+    weights_y = [(part * lanes_y_ref[1]).astype(jnp.bfloat16) for part in spread_y]
     for part in range(2):
         spread_ref[part] = weights_x[part]
         to_core_ref[part] = weights_y[part].astype(jnp.float32).T.astype(jnp.bfloat16)
@@ -419,10 +434,21 @@
         return [blocks[0]] + moved
 
     flat = (n_f, block_x * block_y, n_z)
-    (packed,) = call(
-        pack_kernel,
+    plane = count_y * SUBLANES * SUBLANES
+    packed, *constants = call(
+        functools.partial(
+            pack_kernel, functools.partial(constants_kernel, n_f, count_x, count_y, rank)
+        ),
         "pack",
-        [array((pairs, 2, 4 * n_f + 1, 2, n_z))],
+        [
+            array((pairs, 2, 4 * n_f + 1, 2, n_z)),
+            array((2 * LANES, LANES), jnp.bfloat16),
+            array((LANES, 2 * devices), jnp.bfloat16),
+            array((LANES, LANES)),
+            array((LANES, LANES), jnp.bfloat16),
+            array((plane, 2 * devices), jnp.bfloat16),
+            array((2, plane, LANES)),
+        ],
         [
             pltpu.VMEM(flat, f32),
             pltpu.VMEM(factor_x.shape, f32),
@@ -456,7 +482,7 @@
             pltpu.VMEM((2, LANES, plane), jnp.bfloat16),
             pltpu.VMEM((2, plane, LANES), jnp.bfloat16),
         ],
-        (planes,),
+        (planes, *constants),
         out_spaces=(hbm,) + (vmem,) * (1 + count_y),
     )
     columns = pass_on(columns, "gy")

time: 51.2 us -> 51.1 us (level)
  no operation moved by 1% of the time
where the time goes in v10:
time: 51.1 us; the launch traced here: 50.9 us
  blocking collectives  22.9 us (45%)
  starting transfers between devices  14.2 us (28%)
  waiting for transfers between devices  6.9 us (14%)
  Pallas kernels  6.15 us (12%)
  between operations  0.71 us (1%)
    all_to_all x1, blocking collectives, swap(): return lax.all_to_all(blocks, ('gx', 'gy'), 0, 0, tiled=True)  22.9 us
    ppermute x10, starting transfers between devices, pass_on(): lax.ppermute(block, axis, [(i, (i + k) % count) for i in range(count)])  10.6 us
    ppermute x10, waiting for transfers between devices, pass_on(): lax.ppermute(block, axis, [(i, (i + k) % count) for i in range(count)])  6.72 us
    pallas_call x5, Pallas kernels, call(): pl.pallas_call(kernel, out_shape=tuple(outs), in_specs=[space] * len(oper...  6.15 us
    all_to_all x1, starting transfers between devices, swap(): return lax.all_to_all(blocks, ('gx', 'gy'), 0, 0, tiled=True)  3.64 us
  transfers between devices with their start and end apart: 11, of which 6 were waited for; matrix products, arithmetic and copies ran while one was open for 0% of the time, Pallas kernels for 2%

profile of v10, /device:TPU:1, one launch (start us, length us, event | category | flops | bytes accessed | tf_op | source)
XLA Modules:
  0.0 50.9 jit_solution(823346259005006160)
XLA Ops:
  0.6 1.4 %pack.1 = (f32[16,2,17,2,128]{4,3,2,1,0:T(2,128)S(1)}, bf16[256,128]{1,0:T(8,128)(2,1)S(1)}, bf16[128,64]{1,0:T(8,128)(2,1)S(1)}, f32[128,128]{1,0:T(8,128)S(1)}...) custom-call(f32[4,256,128]{2,1,0:T(8,128)} %bitcast.10, ...), custom_call_target="tpu_custom_call" | custom-call | flops 1000000000 | tf_op jit(solution)/shard_map/pack/pallas_call | solution.py:412
  2.0 22.9 %all_to_all.10 = f32[32,17,2,128]{3,2,1,0:T(2,128)S(1)} all-to-all(f32[32,17,2,128]{3,2,1,0:T(2,128)S(1)} %bitcast.8), channel_id=1, replica_groups=mesh['gx'=8,'gy'=4] {'gx','gy'}, dimensions={0} | all-to-all | bytes 1114112 | tf_op jit(solution)/shard_map/all_to_all | solution.py:425
  24.9 2.6 %sections.1 = (f32[8,4,8,4,128]{4,3,2,1,0:T(4,128)}, bf16[2,512,128]{2,1,0:T(8,128)(2,1)S(1)}, f32[96,128]{1,0:T(8,128)S(1)}, f32[96,128]{1,0:T(8,128)S(1)}, f32...) custom-call(f32[8,4,17,2,128]{4,3,2,1,0:T(2,128)S(1)} %bitcast.7, bf16[256,128]{1,0:T(8,128)(2,1)S(1)} %get-tuple-element.30.taps_ref, ...), custom_call_target="tpu_custom_call" | custom-call | flops 1000000000 | tf_op jit(solution)/shard_map/sections/pallas_call | solution.py:412
  27.6 0.1 collective-permute-start
  27.6 1.2 %collective-permute-start.1 = (f32[96,128]{1,0:T(8,128)S(1)}, f32[96,128]{1,0:T(8,128)S(1)}, u32[]{:S(2)}, u32[]{:S(2)}) collective-permute-start(f32[96,128]{1,0:T(8,128)S(1)} %get-tuple-element.40), channel_id=1, source_target_pairs={{0,2},{1,3},{2,0},{3,1},{4,6},{5,7},{6,4},{7,5},{8,10},{9,11},{10,... | collective-permute-start | bytes 147464 | tf_op jit(solution)/shard_map/ppermute | solution.py:430
  28.9 2.0 %collective-permute-start.2 = (f32[96,128]{1,0:T(8,128)S(1)}, f32[96,128]{1,0:T(8,128)S(1)}, u32[]{:S(2)}, u32[]{:S(2)}) collective-permute-start(f32[96,128]{1,0:T(8,128)S(1)} %get-tuple-element.41), channel_id=1, source_target_pairs={{0,3},{1,0},{2,1},{3,2},{4,7},{5,4},{6,5},{7,6},{8,11},{9,8},{10,9... | collective-permute-start | bytes 147464 | tf_op jit(solution)/shard_map/ppermute | solution.py:430
  30.9 3.6 %all-to-all-start.1 = ((f32[32,8,4,128]{3,2,1,0:T(4,128)}), f32[32,8,4,128]{3,2,1,0:T(4,128)S(1)}, u32[]{:S(2)}, u32[]{:S(2)}) async-start(f32[32,8,4,128]{3,2,1,0:T(4,128)} %bitcast.3), calls=%async_computation.1 | async-start | bytes 1048576 | tf_op jit(solution)/shard_map/all_to_all | solution.py:425
  34.5 0.0 collective-permute-done.refs_1_
  34.5 0.0 collective-permute-done.1.refs_2_
  34.6 0.0 collective-permute-done.2.refs_3_
  34.6 0.7 %expand.1 = (f32[144,128]{1,0:T(8,128)S(1)}, f32[144,128]{1,0:T(8,128)S(1)}, f32[144,128]{1,0:T(8,128)S(1)}, f32[144,128]{1,0:T(8,128)S(1)}, f32[144,128]{1,0:T(...) custom-call(bf16[2,512,128]{2,1,0:T(8,128)(2,1)S(1)} %get-tuple-element.37.spread_ref, ...), custom_call_target="tpu_custom_call" | custom-call | flops 20000000000 | tf_op jit(solution)/shard_map/expand/pallas_call | solution.py:412
  35.3 1.9 %collective-permute-start.3 = (f32[144,128]{1,0:T(8,128)S(1)}, f32[144,128]{1,0:T(8,128)S(1)}, u32[]{:S(2)}, u32[]{:S(2)}) collective-permute-start(f32[144,128]{1,0:T(8,128)S(1)} %get-tuple-element.43), channel_id=1, source_target_pairs={{0,4},{4,8},{8,12},{12,16},{16,20},{20,24},{24,28},{28,0},{1,5},{5... | collective-permute-start | bytes 221192 | tf_op jit(solution)/shard_map/ppermute | solution.py:430
  37.1 1.2 %collective-permute-start.4 = (f32[144,128]{1,0:T(8,128)S(1)}, f32[144,128]{1,0:T(8,128)S(1)}, u32[]{:S(2)}, u32[]{:S(2)}) collective-permute-start(f32[144,128]{1,0:T(8,128)S(1)} %get-tuple-element.44), channel_id=1, source_target_pairs={{0,8},{4,12},{8,16},{12,20},{16,24},{20,28},{24,0},{28,4},{1,9},{5... | collective-permute-start | bytes 221192 | tf_op jit(solution)/shard_map/ppermute | solution.py:430
  38.3 0.2 collective-permute-start.5
  38.6 0.4 collective-permute-start.6
  39.0 2.6 %collective-permute-start.7 = (f32[144,128]{1,0:T(8,128)S(1)}, f32[144,128]{1,0:T(8,128)S(1)}, u32[]{:S(2)}, u32[]{:S(2)}) collective-permute-start(f32[144,128]{1,0:T(8,128)S(1)} %get-tuple-element.47), channel_id=1, source_target_pairs={{0,20},{4,24},{8,28},{12,0},{16,4},{20,8},{24,12},{28,16},{1,21},{... | collective-permute-start | bytes 221192 | tf_op jit(solution)/shard_map/ppermute | solution.py:430
  41.6 0.0 collective-permute-done.3.refs_1_
  41.6 0.9 %collective-permute-start.8 = (f32[144,128]{1,0:T(8,128)S(1)}, f32[144,128]{1,0:T(8,128)S(1)}, u32[]{:S(2)}, u32[]{:S(2)}) collective-permute-start(f32[144,128]{1,0:T(8,128)S(1)} %get-tuple-element.48), channel_id=1, source_target_pairs={{0,24},{4,28},{8,0},{12,4},{16,8},{20,12},{24,16},{28,20},{1,25},{... | collective-permute-start | bytes 221192 | tf_op jit(solution)/shard_map/ppermute | solution.py:430
  42.5 2.6 %collective-permute-done.4.refs_2_ = f32[144,128]{1,0:T(8,128)S(1)} collective-permute-done((f32[144,128]{1,0:T(8,128)S(1)}, f32[144,128]{1,0:T(8,128)S(1)}, u32[]{:S(2)}, u32[]{:S(2)}) %collective-permute-start.4) | collective-permute-done | bytes 73760 | tf_op jit(solution)/shard_map/ppermute | solution.py:430
  45.1 0.0 collective-permute-start.9
  45.1 0.4 collective-permute-done.5.refs_3_
  45.5 3.5 %collective-permute-done.6.refs_4_ = f32[144,128]{1,0:T(8,128)S(1)} collective-permute-done((f32[144,128]{1,0:T(8,128)S(1)}, f32[144,128]{1,0:T(8,128)S(1)}, u32[]{:S(2)}, u32[]{:S(2)}) %collective-permute-start.6) | collective-permute-done | bytes 73760 | tf_op jit(solution)/shard_map/ppermute | solution.py:430
  49.0 0.1 collective-permute-done.7.refs_5_
  49.2 0.0 collective-permute-done.8.refs_6_
  49.2 0.1 collective-permute-done.9.refs_7_
  49.2 0.4 rebuilt.1
  49.6 0.2 all-to-all-done.1
  49.8 1.0 %results.1 = (f32[4,256,128]{2,1,0:T(8,128)}, f32[4,256,128]{2,1,0:T(8,128)}, f32[4,4,8,128]{3,2,1,0:T(8,128)}) custom-call(f32[16,2,8,4,128]{4,3,2,1,0:T(4,128)S(1)} %bitcast.9, f32[4,256,128]{2,1,0:T(8,128)S(1)} %get-tuple-element.50.rebuilt_ref, f32[4,4,8,128]{3,2,1,0:T(8,128)S(1)} %get-tuple-element.51.core_ref), custom_call_target="tpu_custom_call" | custom-call | flops 1000000000 | tf_op jit(solution)/shard_map/results/pallas_call | solution.py:412
Async XLA Ops:
  27.6 7.0 %collective-permute-start = (f32[96,128]{1,0:T(8,128)S(1)}, f32[96,128]{1,0:T(8,128)S(1)}, u32[]{:S(2)}, u32[]{:S(2)}) collective-permute-start(f32[96,128]{1,0:T(8,128)S(1)} %get-tuple-element.39), channel_id=1, source_target_pairs={{0,1},{1,2},{2,3},{3,0},{4,5},{5,6},{6,7},{7,4},{8,9},{9,10},{10,1... | collective-permute-start | bytes 147464 | tf_op jit(solution)/shard_map/ppermute | solution.py:430
  27.6 6.9 %collective-permute-start.1 = (f32[96,128]{1,0:T(8,128)S(1)}, f32[96,128]{1,0:T(8,128)S(1)}, u32[]{:S(2)}, u32[]{:S(2)}) collective-permute-start(f32[96,128]{1,0:T(8,128)S(1)} %get-tuple-element.40), channel_id=1, source_target_pairs={{0,2},{1,3},{2,0},{3,1},{4,6},{5,7},{6,4},{7,5},{8,10},{9,11},{10,... | collective-permute-start | bytes 147464 | tf_op jit(solution)/shard_map/ppermute | solution.py:430
  28.9 5.7 %collective-permute-start.2 = (f32[96,128]{1,0:T(8,128)S(1)}, f32[96,128]{1,0:T(8,128)S(1)}, u32[]{:S(2)}, u32[]{:S(2)}) collective-permute-start(f32[96,128]{1,0:T(8,128)S(1)} %get-tuple-element.41), channel_id=1, source_target_pairs={{0,3},{1,0},{2,1},{3,2},{4,7},{5,4},{6,5},{7,6},{8,11},{9,8},{10,9... | collective-permute-start | bytes 147464 | tf_op jit(solution)/shard_map/ppermute | solution.py:430
  30.9 18.9 %all-to-all-start.1 = ((f32[32,8,4,128]{3,2,1,0:T(4,128)}), f32[32,8,4,128]{3,2,1,0:T(4,128)S(1)}, u32[]{:S(2)}, u32[]{:S(2)}) async-start(f32[32,8,4,128]{3,2,1,0:T(4,128)} %bitcast.3), calls=%async_computation.1 | async-start | bytes 1048576 | tf_op jit(solution)/shard_map/all_to_all | solution.py:425
  35.3 6.4 %collective-permute-start.3 = (f32[144,128]{1,0:T(8,128)S(1)}, f32[144,128]{1,0:T(8,128)S(1)}, u32[]{:S(2)}, u32[]{:S(2)}) collective-permute-start(f32[144,128]{1,0:T(8,128)S(1)} %get-tuple-element.43), channel_id=1, source_target_pairs={{0,4},{4,8},{8,12},{12,16},{16,20},{20,24},{24,28},{28,0},{1,5},{5... | collective-permute-start | bytes 221192 | tf_op jit(solution)/shard_map/ppermute | solution.py:430
  37.1 8.0 %collective-permute-start.4 = (f32[144,128]{1,0:T(8,128)S(1)}, f32[144,128]{1,0:T(8,128)S(1)}, u32[]{:S(2)}, u32[]{:S(2)}) collective-permute-start(f32[144,128]{1,0:T(8,128)S(1)} %get-tuple-element.44), channel_id=1, source_target_pairs={{0,8},{4,12},{8,16},{12,20},{16,24},{20,28},{24,0},{28,4},{1,9},{5... | collective-permute-start | bytes 221192 | tf_op jit(solution)/shard_map/ppermute | solution.py:430
  38.3 7.2 %collective-permute-start.5 = (f32[144,128]{1,0:T(8,128)S(1)}, f32[144,128]{1,0:T(8,128)S(1)}, u32[]{:S(2)}, u32[]{:S(2)}) collective-permute-start(f32[144,128]{1,0:T(8,128)S(1)} %get-tuple-element.45), channel_id=1, source_target_pairs={{0,12},{4,16},{8,20},{12,24},{16,28},{20,0},{24,4},{28,8},{1,13},{... | collective-permute-start | bytes 221192 | tf_op jit(solution)/shard_map/ppermute | solution.py:430
  38.6 10.5 %collective-permute-start.6 = (f32[144,128]{1,0:T(8,128)S(1)}, f32[144,128]{1,0:T(8,128)S(1)}, u32[]{:S(2)}, u32[]{:S(2)}) collective-permute-start(f32[144,128]{1,0:T(8,128)S(1)} %get-tuple-element.46), channel_id=1, source_target_pairs={{0,16},{4,20},{8,24},{12,28},{16,0},{20,4},{24,8},{28,12},{1,17},{... | collective-permute-start | bytes 221192 | tf_op jit(solution)/shard_map/ppermute | solution.py:430
  39.0 10.2 %collective-permute-start.7 = (f32[144,128]{1,0:T(8,128)S(1)}, f32[144,128]{1,0:T(8,128)S(1)}, u32[]{:S(2)}, u32[]{:S(2)}) collective-permute-start(f32[144,128]{1,0:T(8,128)S(1)} %get-tuple-element.47), channel_id=1, source_target_pairs={{0,20},{4,24},{8,28},{12,0},{16,4},{20,8},{24,12},{28,16},{1,21},{... | collective-permute-start | bytes 221192 | tf_op jit(solution)/shard_map/ppermute | solution.py:430
  41.6 7.6 %collective-permute-start.8 = (f32[144,128]{1,0:T(8,128)S(1)}, f32[144,128]{1,0:T(8,128)S(1)}, u32[]{:S(2)}, u32[]{:S(2)}) collective-permute-start(f32[144,128]{1,0:T(8,128)S(1)} %get-tuple-element.48), channel_id=1, source_target_pairs={{0,24},{4,28},{8,0},{12,4},{16,8},{20,12},{24,16},{28,20},{1,25},{... | collective-permute-start | bytes 221192 | tf_op jit(solution)/shard_map/ppermute | solution.py:430
  45.1 4.1 %collective-permute-start.9 = (f32[144,128]{1,0:T(8,128)S(1)}, f32[144,128]{1,0:T(8,128)S(1)}, u32[]{:S(2)}, u32[]{:S(2)}) collective-permute-start(f32[144,128]{1,0:T(8,128)S(1)} %get-tuple-element.49), channel_id=1, source_target_pairs={{0,28},{4,0},{8,4},{12,8},{16,12},{20,16},{24,20},{28,24},{1,29},{... | collective-permute-start | bytes 221192 | tf_op jit(solution)/shard_map/ppermute | solution.py:430

commit v11 on v10

--- a/solution.py
+++ b/solution.py
@@ -241,7 +241,7 @@
         adv[f, s] = done
         parts = exchange([done[y] for y in range(SUBLANES)], LANES // SUBLANES)
         for i, part in enumerate(parts):
-            sent_ref[i, s, 2 * f : 2 * f + 2] = part.reshape(2, HALF, LANES)
+            sent_ref[i, s, f * SUBLANES : (f + 1) * SUBLANES] = part
 
     plane = count_y * SUBLANES * SUBLANES
     held = in_ref[:, :, 4 * n_f].reshape(2 * count_x * count_y, LANES)
@@ -356,10 +356,13 @@
     leaving[n_f].start()
     leaving[n_f + 1].start()
     for f in range(n_f):
-        for octet in range(2):
-            place = 2 * f + octet
-            matrix = jnp.concatenate([in_ref[:, 0, place], in_ref[:, 1, place]], axis=1)
-            turned = matrix.reshape(LANES, LANES).T
+        at = pl.ds(f * SUBLANES, SUBLANES)
+        even, odd = in_ref[:, 0, at, :], in_ref[:, 1, at, :]
+        lower = lax.broadcasted_iota(jnp.int32, even.shape, 1) < HALF
+        first = jnp.where(lower, even, pltpu.roll(odd, HALF, 1))
+        second = jnp.where(lower, pltpu.roll(even, HALF, 1), odd)
+        for octet, part in enumerate((first, second)):
+            turned = part.reshape(LANES, LANES).T
             scatter_rows(turned, octet, block_x, block_y, advanced_ref, f)
         leaving[f].start()
     for copy in leaving:
@@ -469,7 +472,7 @@
         functools.partial(main_kernel, n_f, count_x, count_y, rank, rescale),
         "sections",
         [
-            array((count_x, count_y, 2 * n_f, HALF, n_z)),
+            array((count_x, count_y, n_f * SUBLANES, n_z)),
             array((2, n_f * LANES, LANES), jnp.bfloat16),
         ]
         + [array((rows, LANES))] * count_y,
@@ -477,7 +480,7 @@
         + [
             pltpu.VMEM((n_f, count_y, SUBLANES, SUBLANES, LANES), f32),
             pltpu.VMEM((count_y, rows, LANES), f32),
-            pltpu.VMEM((count_x, count_y, 2 * n_f, HALF, n_z), f32),
+            pltpu.VMEM((count_x, count_y, n_f * SUBLANES, n_z), f32),
             pltpu.SemaphoreType.DMA,
             pltpu.VMEM((2, LANES, plane), jnp.bfloat16),
             pltpu.VMEM((2, plane, LANES), jnp.bfloat16),
@@ -486,7 +489,7 @@
         out_spaces=(hbm,) + (vmem,) * (1 + count_y),
     )
     columns = pass_on(columns, "gy")
-    sent = swap(sent).reshape(pairs, 2, 2 * n_f, HALF, n_z)
+    sent = swap(sent).reshape(pairs, 2, n_f * SUBLANES, n_z)
     rows = (n_f * count_y + n_f // 2) * SUBLANES
     blocks = call(
         functools.partial(expand_kernel, n_f, count_x, count_y),

time: 51.1 us -> 51.1 us (level)
  no operation moved by 1% of the time
where the time goes in v11:
time: 51.1 us; the launch traced here: 50.9 us
  blocking collectives  22.9 us (45%)
  starting transfers between devices  14.2 us (28%)
  waiting for transfers between devices  6.9 us (14%)
  Pallas kernels  6.14 us (12%)
  between operations  0.71 us (1%)
    all_to_all x1, blocking collectives, swap(): return lax.all_to_all(blocks, ('gx', 'gy'), 0, 0, tiled=True)  22.9 us
    ppermute x10, starting transfers between devices, pass_on(): lax.ppermute(block, axis, [(i, (i + k) % count) for i in range(count)])  10.6 us
    ppermute x10, waiting for transfers between devices, pass_on(): lax.ppermute(block, axis, [(i, (i + k) % count) for i in range(count)])  6.72 us
    pallas_call x5, Pallas kernels, call(): pl.pallas_call(kernel, out_shape=tuple(outs), in_specs=[space] * len(oper...  6.14 us
    all_to_all x1, starting transfers between devices, swap(): return lax.all_to_all(blocks, ('gx', 'gy'), 0, 0, tiled=True)  3.64 us
  transfers between devices with their start and end apart: 11, of which 6 were waited for; matrix products, arithmetic and copies ran while one was open for 0% of the time, Pallas kernels for 2%

profile of v11, /device:TPU:1, one launch (start us, length us, event | category | flops | bytes accessed | tf_op | source)
XLA Modules:
  0.0 50.9 jit_solution(3487047326744085186)
XLA Ops:
  0.6 1.4 %pack.1 = (f32[16,2,17,2,128]{4,3,2,1,0:T(2,128)S(1)}, bf16[256,128]{1,0:T(8,128)(2,1)S(1)}, bf16[128,64]{1,0:T(8,128)(2,1)S(1)}, f32[128,128]{1,0:T(8,128)S(1)}...) custom-call(f32[4,256,128]{2,1,0:T(8,128)} %bitcast.10, ...), custom_call_target="tpu_custom_call" | custom-call | flops 1000000000 | tf_op jit(solution)/shard_map/pack/pallas_call | solution.py:415
  2.0 22.9 %all_to_all.10 = f32[32,17,2,128]{3,2,1,0:T(2,128)S(1)} all-to-all(f32[32,17,2,128]{3,2,1,0:T(2,128)S(1)} %bitcast.8), channel_id=1, replica_groups=mesh['gx'=8,'gy'=4] {'gx','gy'}, dimensions={0} | all-to-all | bytes 1114112 | tf_op jit(solution)/shard_map/all_to_all | solution.py:428
  24.9 2.6 %sections.1 = (f32[8,4,32,128]{3,2,1,0:T(8,128)}, bf16[2,512,128]{2,1,0:T(8,128)(2,1)S(1)}, f32[96,128]{1,0:T(8,128)S(1)}, f32[96,128]{1,0:T(8,128)S(1)}, f32[96,128]{1,0:T(8,128)S(1)}, /*index=5*/f32[96,128]{1,0:T(8,128)S(1)}) custom-call(f32[8,4,17,2,128]{4,3,2,1,0:T(2,128)S(1)} %bitcast.7, bf16[256,128]{1,0:T(8,128)(2,1)S(1)} %get-tuple-element.30.taps_ref, ...), custom_call_target="tpu_custom_call" | custom-call | flops 1000000000 | tf_op jit(solution)/shard_map/sections/pallas_call | solution.py:415
  27.6 0.1 collective-permute-start
  27.6 1.2 %collective-permute-start.1 = (f32[96,128]{1,0:T(8,128)S(1)}, f32[96,128]{1,0:T(8,128)S(1)}, u32[]{:S(2)}, u32[]{:S(2)}) collective-permute-start(f32[96,128]{1,0:T(8,128)S(1)} %get-tuple-element.40), channel_id=1, source_target_pairs={{0,2},{1,3},{2,0},{3,1},{4,6},{5,7},{6,4},{7,5},{8,10},{9,11},{10,... | collective-permute-start | bytes 147464 | tf_op jit(solution)/shard_map/ppermute | solution.py:433
  28.9 2.0 %collective-permute-start.2 = (f32[96,128]{1,0:T(8,128)S(1)}, f32[96,128]{1,0:T(8,128)S(1)}, u32[]{:S(2)}, u32[]{:S(2)}) collective-permute-start(f32[96,128]{1,0:T(8,128)S(1)} %get-tuple-element.41), channel_id=1, source_target_pairs={{0,3},{1,0},{2,1},{3,2},{4,7},{5,4},{6,5},{7,6},{8,11},{9,8},{10,9... | collective-permute-start | bytes 147464 | tf_op jit(solution)/shard_map/ppermute | solution.py:433
  30.9 3.6 %all-to-all-start.1 = ((f32[32,32,128]{2,1,0:T(8,128)}), f32[32,32,128]{2,1,0:T(8,128)S(1)}, u32[]{:S(2)}, u32[]{:S(2)}) async-start(f32[32,32,128]{2,1,0:T(8,128)} %bitcast.3), calls=%async_computation.1 | async-start | bytes 1048576 | tf_op jit(solution)/shard_map/all_to_all | solution.py:428
  34.5 0.0 collective-permute-done.refs_1_
  34.5 0.0 collective-permute-done.1.refs_2_
  34.5 0.0 collective-permute-done.2.refs_3_
  34.6 0.7 %expand.1 = (f32[144,128]{1,0:T(8,128)S(1)}, f32[144,128]{1,0:T(8,128)S(1)}, f32[144,128]{1,0:T(8,128)S(1)}, f32[144,128]{1,0:T(8,128)S(1)}, f32[144,128]{1,0:T(...) custom-call(bf16[2,512,128]{2,1,0:T(8,128)(2,1)S(1)} %get-tuple-element.37.spread_ref, ...), custom_call_target="tpu_custom_call" | custom-call | flops 20000000000 | tf_op jit(solution)/shard_map/expand/pallas_call | solution.py:415
  35.2 1.9 %collective-permute-start.3 = (f32[144,128]{1,0:T(8,128)S(1)}, f32[144,128]{1,0:T(8,128)S(1)}, u32[]{:S(2)}, u32[]{:S(2)}) collective-permute-start(f32[144,128]{1,0:T(8,128)S(1)} %get-tuple-element.43), channel_id=1, source_target_pairs={{0,4},{4,8},{8,12},{12,16},{16,20},{20,24},{24,28},{28,0},{1,5},{5... | collective-permute-start | bytes 221192 | tf_op jit(solution)/shard_map/ppermute | solution.py:433
  37.1 1.2 %collective-permute-start.4 = (f32[144,128]{1,0:T(8,128)S(1)}, f32[144,128]{1,0:T(8,128)S(1)}, u32[]{:S(2)}, u32[]{:S(2)}) collective-permute-start(f32[144,128]{1,0:T(8,128)S(1)} %get-tuple-element.44), channel_id=1, source_target_pairs={{0,8},{4,12},{8,16},{12,20},{16,24},{20,28},{24,0},{28,4},{1,9},{5... | collective-permute-start | bytes 221192 | tf_op jit(solution)/shard_map/ppermute | solution.py:433
  38.3 0.2 collective-permute-start.5
  38.5 0.4 collective-permute-start.6
  38.9 2.7 %collective-permute-start.7 = (f32[144,128]{1,0:T(8,128)S(1)}, f32[144,128]{1,0:T(8,128)S(1)}, u32[]{:S(2)}, u32[]{:S(2)}) collective-permute-start(f32[144,128]{1,0:T(8,128)S(1)} %get-tuple-element.47), channel_id=1, source_target_pairs={{0,20},{4,24},{8,28},{12,0},{16,4},{20,8},{24,12},{28,16},{1,21},{... | collective-permute-start | bytes 221192 | tf_op jit(solution)/shard_map/ppermute | solution.py:433
  41.6 0.0 collective-permute-done.3.refs_1_
  41.6 0.9 %collective-permute-start.8 = (f32[144,128]{1,0:T(8,128)S(1)}, f32[144,128]{1,0:T(8,128)S(1)}, u32[]{:S(2)}, u32[]{:S(2)}) collective-permute-start(f32[144,128]{1,0:T(8,128)S(1)} %get-tuple-element.48), channel_id=1, source_target_pairs={{0,24},{4,28},{8,0},{12,4},{16,8},{20,12},{24,16},{28,20},{1,25},{... | collective-permute-start | bytes 221192 | tf_op jit(solution)/shard_map/ppermute | solution.py:433
  42.5 2.6 %collective-permute-done.4.refs_2_ = f32[144,128]{1,0:T(8,128)S(1)} collective-permute-done((f32[144,128]{1,0:T(8,128)S(1)}, f32[144,128]{1,0:T(8,128)S(1)}, u32[]{:S(2)}, u32[]{:S(2)}) %collective-permute-start.4) | collective-permute-done | bytes 73760 | tf_op jit(solution)/shard_map/ppermute | solution.py:433
  45.1 0.0 collective-permute-start.9
  45.1 0.4 collective-permute-done.5.refs_3_
  45.5 3.5 %collective-permute-done.6.refs_4_ = f32[144,128]{1,0:T(8,128)S(1)} collective-permute-done((f32[144,128]{1,0:T(8,128)S(1)}, f32[144,128]{1,0:T(8,128)S(1)}, u32[]{:S(2)}, u32[]{:S(2)}) %collective-permute-start.6) | collective-permute-done | bytes 73760 | tf_op jit(solution)/shard_map/ppermute | solution.py:433
  49.0 0.1 collective-permute-done.7.refs_5_
  49.2 0.0 collective-permute-done.8.refs_6_
  49.2 0.1 collective-permute-done.9.refs_7_
  49.2 0.4 rebuilt.1
  49.6 0.2 all-to-all-done.1
  49.8 1.0 %results.1 = (f32[4,256,128]{2,1,0:T(8,128)}, f32[4,256,128]{2,1,0:T(8,128)}, f32[4,4,8,128]{3,2,1,0:T(8,128)}) custom-call(f32[16,2,32,128]{3,2,1,0:T(8,128)S(1)} %bitcast.9, f32[4,256,128]{2,1,0:T(8,128)S(1)} %get-tuple-element.50.rebuilt_ref, f32[4,4,8,128]{3,2,1,0:T(8,128)S(1)} %get-tuple-element.51.core_ref), custom_call_target="tpu_custom_call" | custom-call | flops 1000000000 | tf_op jit(solution)/shard_map/results/pallas_call | solution.py:415
Async XLA Ops:
  27.6 7.0 %collective-permute-start = (f32[96,128]{1,0:T(8,128)S(1)}, f32[96,128]{1,0:T(8,128)S(1)}, u32[]{:S(2)}, u32[]{:S(2)}) collective-permute-start(f32[96,128]{1,0:T(8,128)S(1)} %get-tuple-element.39), channel_id=1, source_target_pairs={{0,1},{1,2},{2,3},{3,0},{4,5},{5,6},{6,7},{7,4},{8,9},{9,10},{10,1... | collective-permute-start | bytes 147464 | tf_op jit(solution)/shard_map/ppermute | solution.py:433
  27.6 6.9 %collective-permute-start.1 = (f32[96,128]{1,0:T(8,128)S(1)}, f32[96,128]{1,0:T(8,128)S(1)}, u32[]{:S(2)}, u32[]{:S(2)}) collective-permute-start(f32[96,128]{1,0:T(8,128)S(1)} %get-tuple-element.40), channel_id=1, source_target_pairs={{0,2},{1,3},{2,0},{3,1},{4,6},{5,7},{6,4},{7,5},{8,10},{9,11},{10,... | collective-permute-start | bytes 147464 | tf_op jit(solution)/shard_map/ppermute | solution.py:433
  28.9 5.7 %collective-permute-start.2 = (f32[96,128]{1,0:T(8,128)S(1)}, f32[96,128]{1,0:T(8,128)S(1)}, u32[]{:S(2)}, u32[]{:S(2)}) collective-permute-start(f32[96,128]{1,0:T(8,128)S(1)} %get-tuple-element.41), channel_id=1, source_target_pairs={{0,3},{1,0},{2,1},{3,2},{4,7},{5,4},{6,5},{7,6},{8,11},{9,8},{10,9... | collective-permute-start | bytes 147464 | tf_op jit(solution)/shard_map/ppermute | solution.py:433
  30.9 18.9 %all-to-all-start.1 = ((f32[32,32,128]{2,1,0:T(8,128)}), f32[32,32,128]{2,1,0:T(8,128)S(1)}, u32[]{:S(2)}, u32[]{:S(2)}) async-start(f32[32,32,128]{2,1,0:T(8,128)} %bitcast.3), calls=%async_computation.1 | async-start | bytes 1048576 | tf_op jit(solution)/shard_map/all_to_all | solution.py:428
  35.2 6.4 %collective-permute-start.3 = (f32[144,128]{1,0:T(8,128)S(1)}, f32[144,128]{1,0:T(8,128)S(1)}, u32[]{:S(2)}, u32[]{:S(2)}) collective-permute-start(f32[144,128]{1,0:T(8,128)S(1)} %get-tuple-element.43), channel_id=1, source_target_pairs={{0,4},{4,8},{8,12},{12,16},{16,20},{20,24},{24,28},{28,0},{1,5},{5... | collective-permute-start | bytes 221192 | tf_op jit(solution)/shard_map/ppermute | solution.py:433
  37.1 8.0 %collective-permute-start.4 = (f32[144,128]{1,0:T(8,128)S(1)}, f32[144,128]{1,0:T(8,128)S(1)}, u32[]{:S(2)}, u32[]{:S(2)}) collective-permute-start(f32[144,128]{1,0:T(8,128)S(1)} %get-tuple-element.44), channel_id=1, source_target_pairs={{0,8},{4,12},{8,16},{12,20},{16,24},{20,28},{24,0},{28,4},{1,9},{5... | collective-permute-start | bytes 221192 | tf_op jit(solution)/shard_map/ppermute | solution.py:433
  38.3 7.2 %collective-permute-start.5 = (f32[144,128]{1,0:T(8,128)S(1)}, f32[144,128]{1,0:T(8,128)S(1)}, u32[]{:S(2)}, u32[]{:S(2)}) collective-permute-start(f32[144,128]{1,0:T(8,128)S(1)} %get-tuple-element.45), channel_id=1, source_target_pairs={{0,12},{4,16},{8,20},{12,24},{16,28},{20,0},{24,4},{28,8},{1,13},{... | collective-permute-start | bytes 221192 | tf_op jit(solution)/shard_map/ppermute | solution.py:433
  38.5 10.5 %collective-permute-start.6 = (f32[144,128]{1,0:T(8,128)S(1)}, f32[144,128]{1,0:T(8,128)S(1)}, u32[]{:S(2)}, u32[]{:S(2)}) collective-permute-start(f32[144,128]{1,0:T(8,128)S(1)} %get-tuple-element.46), channel_id=1, source_target_pairs={{0,16},{4,20},{8,24},{12,28},{16,0},{20,4},{24,8},{28,12},{1,17},{... | collective-permute-start | bytes 221192 | tf_op jit(solution)/shard_map/ppermute | solution.py:433
  38.9 10.2 %collective-permute-start.7 = (f32[144,128]{1,0:T(8,128)S(1)}, f32[144,128]{1,0:T(8,128)S(1)}, u32[]{:S(2)}, u32[]{:S(2)}) collective-permute-start(f32[144,128]{1,0:T(8,128)S(1)} %get-tuple-element.47), channel_id=1, source_target_pairs={{0,20},{4,24},{8,28},{12,0},{16,4},{20,8},{24,12},{28,16},{1,21},{... | collective-permute-start | bytes 221192 | tf_op jit(solution)/shard_map/ppermute | solution.py:433
  41.6 7.5 %collective-permute-start.8 = (f32[144,128]{1,0:T(8,128)S(1)}, f32[144,128]{1,0:T(8,128)S(1)}, u32[]{:S(2)}, u32[]{:S(2)}) collective-permute-start(f32[144,128]{1,0:T(8,128)S(1)} %get-tuple-element.48), channel_id=1, source_target_pairs={{0,24},{4,28},{8,0},{12,4},{16,8},{20,12},{24,16},{28,20},{1,25},{... | collective-permute-start | bytes 221192 | tf_op jit(solution)/shard_map/ppermute | solution.py:433
  45.1 4.1 %collective-permute-start.9 = (f32[144,128]{1,0:T(8,128)S(1)}, f32[144,128]{1,0:T(8,128)S(1)}, u32[]{:S(2)}, u32[]{:S(2)}) collective-permute-start(f32[144,128]{1,0:T(8,128)S(1)} %get-tuple-element.49), channel_id=1, source_target_pairs={{0,28},{4,0},{8,4},{12,8},{16,12},{20,16},{24,20},{28,24},{1,29},{... | collective-permute-start | bytes 221192 | tf_op jit(solution)/shard_map/ppermute | solution.py:433

commit v12 on v10

--- a/solution.py
+++ b/solution.py
@@ -355,13 +355,16 @@
     leaving.append(pltpu.make_async_copy(core_ref, core_hbm, sems.at[n_f + 1]))
     leaving[n_f].start()
     leaving[n_f + 1].start()
-    for f in range(n_f):
+    def turn(f):
         for octet in range(2):
             place = 2 * f + octet
             matrix = jnp.concatenate([in_ref[:, 0, place], in_ref[:, 1, place]], axis=1)
             turned = matrix.reshape(LANES, LANES).T
             scatter_rows(turned, octet, block_x, block_y, advanced_ref, f)
         leaving[f].start()
+
+    for f in range(n_f):
+        pl.when(lax.axis_index("gy") >= 0)(functools.partial(turn, f))
     for copy in leaving:
         copy.wait()
 

time: 51.1 us -> 51.1 us (level)
  no operation moved by 1% of the time
where the time goes in v12:
time: 51.1 us; the launch traced here: 50.9 us
  blocking collectives  22.9 us (45%)
  starting transfers between devices  14.2 us (28%)
  waiting for transfers between devices  6.9 us (14%)
  Pallas kernels  6.15 us (12%)
  between operations  0.71 us (1%)
    all_to_all x1, blocking collectives, swap(): return lax.all_to_all(blocks, ('gx', 'gy'), 0, 0, tiled=True)  22.9 us
    ppermute x10, starting transfers between devices, pass_on(): lax.ppermute(block, axis, [(i, (i + k) % count) for i in range(count)])  10.6 us
    ppermute x10, waiting for transfers between devices, pass_on(): lax.ppermute(block, axis, [(i, (i + k) % count) for i in range(count)])  6.72 us
    pallas_call x5, Pallas kernels, call(): pl.pallas_call(kernel, out_shape=tuple(outs), in_specs=[space] * len(oper...  6.15 us
    all_to_all x1, starting transfers between devices, swap(): return lax.all_to_all(blocks, ('gx', 'gy'), 0, 0, tiled=True)  3.64 us
  transfers between devices with their start and end apart: 11, of which 6 were waited for; matrix products, arithmetic and copies ran while one was open for 0% of the time, Pallas kernels for 2%

profile of v12, /device:TPU:1, one launch (start us, length us, event | category | flops | bytes accessed | tf_op | source)
XLA Modules:
  0.0 50.9 jit_solution(1061102928030434099)
XLA Ops:
  0.6 1.4 %pack.1 = (f32[16,2,17,2,128]{4,3,2,1,0:T(2,128)S(1)}, bf16[256,128]{1,0:T(8,128)(2,1)S(1)}, bf16[128,64]{1,0:T(8,128)(2,1)S(1)}, f32[128,128]{1,0:T(8,128)S(1)}...) custom-call(f32[4,256,128]{2,1,0:T(8,128)} %bitcast.10, ...), custom_call_target="tpu_custom_call" | custom-call | flops 1000000000 | tf_op jit(solution)/shard_map/pack/pallas_call | solution.py:415
  2.0 22.9 %all_to_all.10 = f32[32,17,2,128]{3,2,1,0:T(2,128)S(1)} all-to-all(f32[32,17,2,128]{3,2,1,0:T(2,128)S(1)} %bitcast.8), channel_id=1, replica_groups=mesh['gx'=8,'gy'=4] {'gx','gy'}, dimensions={0} | all-to-all | bytes 1114112 | tf_op jit(solution)/shard_map/all_to_all | solution.py:428
  24.9 2.6 %sections.1 = (f32[8,4,8,4,128]{4,3,2,1,0:T(4,128)}, bf16[2,512,128]{2,1,0:T(8,128)(2,1)S(1)}, f32[96,128]{1,0:T(8,128)S(1)}, f32[96,128]{1,0:T(8,128)S(1)}, f32...) custom-call(f32[8,4,17,2,128]{4,3,2,1,0:T(2,128)S(1)} %bitcast.7, bf16[256,128]{1,0:T(8,128)(2,1)S(1)} %get-tuple-element.30.taps_ref, ...), custom_call_target="tpu_custom_call" | custom-call | flops 1000000000 | tf_op jit(solution)/shard_map/sections/pallas_call | solution.py:415
  27.6 0.1 collective-permute-start
  27.6 1.2 %collective-permute-start.1 = (f32[96,128]{1,0:T(8,128)S(1)}, f32[96,128]{1,0:T(8,128)S(1)}, u32[]{:S(2)}, u32[]{:S(2)}) collective-permute-start(f32[96,128]{1,0:T(8,128)S(1)} %get-tuple-element.40), channel_id=1, source_target_pairs={{0,2},{1,3},{2,0},{3,1},{4,6},{5,7},{6,4},{7,5},{8,10},{9,11},{10,... | collective-permute-start | bytes 147464 | tf_op jit(solution)/shard_map/ppermute | solution.py:433
  28.9 2.0 %collective-permute-start.2 = (f32[96,128]{1,0:T(8,128)S(1)}, f32[96,128]{1,0:T(8,128)S(1)}, u32[]{:S(2)}, u32[]{:S(2)}) collective-permute-start(f32[96,128]{1,0:T(8,128)S(1)} %get-tuple-element.41), channel_id=1, source_target_pairs={{0,3},{1,0},{2,1},{3,2},{4,7},{5,4},{6,5},{7,6},{8,11},{9,8},{10,9... | collective-permute-start | bytes 147464 | tf_op jit(solution)/shard_map/ppermute | solution.py:433
  30.9 3.6 %all-to-all-start.1 = ((f32[32,8,4,128]{3,2,1,0:T(4,128)}), f32[32,8,4,128]{3,2,1,0:T(4,128)S(1)}, u32[]{:S(2)}, u32[]{:S(2)}) async-start(f32[32,8,4,128]{3,2,1,0:T(4,128)} %bitcast.3), calls=%async_computation.1 | async-start | bytes 1048576 | tf_op jit(solution)/shard_map/all_to_all | solution.py:428
  34.5 0.0 collective-permute-done.refs_1_
  34.5 0.0 collective-permute-done.1.refs_2_
  34.6 0.0 collective-permute-done.2.refs_3_
  34.6 0.7 %expand.1 = (f32[144,128]{1,0:T(8,128)S(1)}, f32[144,128]{1,0:T(8,128)S(1)}, f32[144,128]{1,0:T(8,128)S(1)}, f32[144,128]{1,0:T(8,128)S(1)}, f32[144,128]{1,0:T(...) custom-call(bf16[2,512,128]{2,1,0:T(8,128)(2,1)S(1)} %get-tuple-element.37.spread_ref, ...), custom_call_target="tpu_custom_call" | custom-call | flops 20000000000 | tf_op jit(solution)/shard_map/expand/pallas_call | solution.py:415
  35.3 1.9 %collective-permute-start.3 = (f32[144,128]{1,0:T(8,128)S(1)}, f32[144,128]{1,0:T(8,128)S(1)}, u32[]{:S(2)}, u32[]{:S(2)}) collective-permute-start(f32[144,128]{1,0:T(8,128)S(1)} %get-tuple-element.43), channel_id=1, source_target_pairs={{0,4},{4,8},{8,12},{12,16},{16,20},{20,24},{24,28},{28,0},{1,5},{5... | collective-permute-start | bytes 221192 | tf_op jit(solution)/shard_map/ppermute | solution.py:433
  37.1 1.2 %collective-permute-start.4 = (f32[144,128]{1,0:T(8,128)S(1)}, f32[144,128]{1,0:T(8,128)S(1)}, u32[]{:S(2)}, u32[]{:S(2)}) collective-permute-start(f32[144,128]{1,0:T(8,128)S(1)} %get-tuple-element.44), channel_id=1, source_target_pairs={{0,8},{4,12},{8,16},{12,20},{16,24},{20,28},{24,0},{28,4},{1,9},{5... | collective-permute-start | bytes 221192 | tf_op jit(solution)/shard_map/ppermute | solution.py:433
  38.3 0.2 collective-permute-start.5
  38.6 0.4 collective-permute-start.6
  39.0 2.6 %collective-permute-start.7 = (f32[144,128]{1,0:T(8,128)S(1)}, f32[144,128]{1,0:T(8,128)S(1)}, u32[]{:S(2)}, u32[]{:S(2)}) collective-permute-start(f32[144,128]{1,0:T(8,128)S(1)} %get-tuple-element.47), channel_id=1, source_target_pairs={{0,20},{4,24},{8,28},{12,0},{16,4},{20,8},{24,12},{28,16},{1,21},{... | collective-permute-start | bytes 221192 | tf_op jit(solution)/shard_map/ppermute | solution.py:433
  41.6 0.0 collective-permute-done.3.refs_1_
  41.6 0.9 %collective-permute-start.8 = (f32[144,128]{1,0:T(8,128)S(1)}, f32[144,128]{1,0:T(8,128)S(1)}, u32[]{:S(2)}, u32[]{:S(2)}) collective-permute-start(f32[144,128]{1,0:T(8,128)S(1)} %get-tuple-element.48), channel_id=1, source_target_pairs={{0,24},{4,28},{8,0},{12,4},{16,8},{20,12},{24,16},{28,20},{1,25},{... | collective-permute-start | bytes 221192 | tf_op jit(solution)/shard_map/ppermute | solution.py:433
  42.5 2.6 %collective-permute-done.4.refs_2_ = f32[144,128]{1,0:T(8,128)S(1)} collective-permute-done((f32[144,128]{1,0:T(8,128)S(1)}, f32[144,128]{1,0:T(8,128)S(1)}, u32[]{:S(2)}, u32[]{:S(2)}) %collective-permute-start.4) | collective-permute-done | bytes 73760 | tf_op jit(solution)/shard_map/ppermute | solution.py:433
  45.1 0.0 collective-permute-start.9
  45.1 0.4 collective-permute-done.5.refs_3_
  45.5 3.5 %collective-permute-done.6.refs_4_ = f32[144,128]{1,0:T(8,128)S(1)} collective-permute-done((f32[144,128]{1,0:T(8,128)S(1)}, f32[144,128]{1,0:T(8,128)S(1)}, u32[]{:S(2)}, u32[]{:S(2)}) %collective-permute-start.6) | collective-permute-done | bytes 73760 | tf_op jit(solution)/shard_map/ppermute | solution.py:433
  49.0 0.1 collective-permute-done.7.refs_5_
  49.2 0.0 collective-permute-done.8.refs_6_
  49.2 0.1 collective-permute-done.9.refs_7_
  49.2 0.4 rebuilt.1
  49.6 0.2 all-to-all-done.1
  49.8 1.0 %results.1 = (f32[4,256,128]{2,1,0:T(8,128)}, f32[4,256,128]{2,1,0:T(8,128)}, f32[4,4,8,128]{3,2,1,0:T(8,128)}) custom-call(f32[16,2,8,4,128]{4,3,2,1,0:T(4,128)S(1)} %bitcast.9, f32[4,256,128]{2,1,0:T(8,128)S(1)} %get-tuple-element.50.rebuilt_ref, f32[4,4,8,128]{3,2,1,0:T(8,128)S(1)} %get-tuple-element.51.core_ref), custom_call_target="tpu_custom_call" | custom-call | flops 1000000000 | tf_op jit(solution)/shard_map/results/pallas_call | solution.py:415
Async XLA Ops:
  27.6 7.0 %collective-permute-start = (f32[96,128]{1,0:T(8,128)S(1)}, f32[96,128]{1,0:T(8,128)S(1)}, u32[]{:S(2)}, u32[]{:S(2)}) collective-permute-start(f32[96,128]{1,0:T(8,128)S(1)} %get-tuple-element.39), channel_id=1, source_target_pairs={{0,1},{1,2},{2,3},{3,0},{4,5},{5,6},{6,7},{7,4},{8,9},{9,10},{10,1... | collective-permute-start | bytes 147464 | tf_op jit(solution)/shard_map/ppermute | solution.py:433
  27.6 6.9 %collective-permute-start.1 = (f32[96,128]{1,0:T(8,128)S(1)}, f32[96,128]{1,0:T(8,128)S(1)}, u32[]{:S(2)}, u32[]{:S(2)}) collective-permute-start(f32[96,128]{1,0:T(8,128)S(1)} %get-tuple-element.40), channel_id=1, source_target_pairs={{0,2},{1,3},{2,0},{3,1},{4,6},{5,7},{6,4},{7,5},{8,10},{9,11},{10,... | collective-permute-start | bytes 147464 | tf_op jit(solution)/shard_map/ppermute | solution.py:433
  28.9 5.7 %collective-permute-start.2 = (f32[96,128]{1,0:T(8,128)S(1)}, f32[96,128]{1,0:T(8,128)S(1)}, u32[]{:S(2)}, u32[]{:S(2)}) collective-permute-start(f32[96,128]{1,0:T(8,128)S(1)} %get-tuple-element.41), channel_id=1, source_target_pairs={{0,3},{1,0},{2,1},{3,2},{4,7},{5,4},{6,5},{7,6},{8,11},{9,8},{10,9... | collective-permute-start | bytes 147464 | tf_op jit(solution)/shard_map/ppermute | solution.py:433
  30.9 18.9 %all-to-all-start.1 = ((f32[32,8,4,128]{3,2,1,0:T(4,128)}), f32[32,8,4,128]{3,2,1,0:T(4,128)S(1)}, u32[]{:S(2)}, u32[]{:S(2)}) async-start(f32[32,8,4,128]{3,2,1,0:T(4,128)} %bitcast.3), calls=%async_computation.1 | async-start | bytes 1048576 | tf_op jit(solution)/shard_map/all_to_all | solution.py:428
  35.3 6.4 %collective-permute-start.3 = (f32[144,128]{1,0:T(8,128)S(1)}, f32[144,128]{1,0:T(8,128)S(1)}, u32[]{:S(2)}, u32[]{:S(2)}) collective-permute-start(f32[144,128]{1,0:T(8,128)S(1)} %get-tuple-element.43), channel_id=1, source_target_pairs={{0,4},{4,8},{8,12},{12,16},{16,20},{20,24},{24,28},{28,0},{1,5},{5... | collective-permute-start | bytes 221192 | tf_op jit(solution)/shard_map/ppermute | solution.py:433
  37.1 8.0 %collective-permute-start.4 = (f32[144,128]{1,0:T(8,128)S(1)}, f32[144,128]{1,0:T(8,128)S(1)}, u32[]{:S(2)}, u32[]{:S(2)}) collective-permute-start(f32[144,128]{1,0:T(8,128)S(1)} %get-tuple-element.44), channel_id=1, source_target_pairs={{0,8},{4,12},{8,16},{12,20},{16,24},{20,28},{24,0},{28,4},{1,9},{5... | collective-permute-start | bytes 221192 | tf_op jit(solution)/shard_map/ppermute | solution.py:433
  38.3 7.2 %collective-permute-start.5 = (f32[144,128]{1,0:T(8,128)S(1)}, f32[144,128]{1,0:T(8,128)S(1)}, u32[]{:S(2)}, u32[]{:S(2)}) collective-permute-start(f32[144,128]{1,0:T(8,128)S(1)} %get-tuple-element.45), channel_id=1, source_target_pairs={{0,12},{4,16},{8,20},{12,24},{16,28},{20,0},{24,4},{28,8},{1,13},{... | collective-permute-start | bytes 221192 | tf_op jit(solution)/shard_map/ppermute | solution.py:433
  38.6 10.5 %collective-permute-start.6 = (f32[144,128]{1,0:T(8,128)S(1)}, f32[144,128]{1,0:T(8,128)S(1)}, u32[]{:S(2)}, u32[]{:S(2)}) collective-permute-start(f32[144,128]{1,0:T(8,128)S(1)} %get-tuple-element.46), channel_id=1, source_target_pairs={{0,16},{4,20},{8,24},{12,28},{16,0},{20,4},{24,8},{28,12},{1,17},{... | collective-permute-start | bytes 221192 | tf_op jit(solution)/shard_map/ppermute | solution.py:433
  39.0 10.2 %collective-permute-start.7 = (f32[144,128]{1,0:T(8,128)S(1)}, f32[144,128]{1,0:T(8,128)S(1)}, u32[]{:S(2)}, u32[]{:S(2)}) collective-permute-start(f32[144,128]{1,0:T(8,128)S(1)} %get-tuple-element.47), channel_id=1, source_target_pairs={{0,20},{4,24},{8,28},{12,0},{16,4},{20,8},{24,12},{28,16},{1,21},{... | collective-permute-start | bytes 221192 | tf_op jit(solution)/shard_map/ppermute | solution.py:433
  41.6 7.6 %collective-permute-start.8 = (f32[144,128]{1,0:T(8,128)S(1)}, f32[144,128]{1,0:T(8,128)S(1)}, u32[]{:S(2)}, u32[]{:S(2)}) collective-permute-start(f32[144,128]{1,0:T(8,128)S(1)} %get-tuple-element.48), channel_id=1, source_target_pairs={{0,24},{4,28},{8,0},{12,4},{16,8},{20,12},{24,16},{28,20},{1,25},{... | collective-permute-start | bytes 221192 | tf_op jit(solution)/shard_map/ppermute | solution.py:433
  45.1 4.1 %collective-permute-start.9 = (f32[144,128]{1,0:T(8,128)S(1)}, f32[144,128]{1,0:T(8,128)S(1)}, u32[]{:S(2)}, u32[]{:S(2)}) collective-permute-start(f32[144,128]{1,0:T(8,128)S(1)} %get-tuple-element.49), channel_id=1, source_target_pairs={{0,28},{4,0},{8,4},{12,8},{16,12},{20,16},{24,20},{28,24},{1,29},{... | collective-permute-start | bytes 221192 | tf_op jit(solution)/shard_map/ppermute | solution.py:433
